TPU v7x, 512 devices: a whole 4x8x8 slice. The times are simulated.
512 devices in a mesh: smp: 8 (over x, y_hi), proto: 64 (over y_lo, z, core).
Axes of the slice: x: 4, y: 8 (y_hi: 2, y_lo: 4; y = y_hi * 4 + y_lo), z: 8, core: 2. Of those that a mesh axis runs over, the one named last changes fastest.
Arguments:
- teacher_features: bfloat16 [1024, 512], P('smp', 'proto'), may hold values from -6 to 6
- student_features: bfloat16 [1024, 512], P('smp', 'proto'), may hold values from -6 to 6
- teacher_weight: bfloat16 [131072, 512], P('proto'), may hold values from -0.45 to 0.45
- student_weight: bfloat16 [131072, 512], P('proto'), may hold values from -0.19921875 to 0.19921875
Outputs:
- sample_loss: float32 [1024], P('smp')
- grad_features: float32 [1024, 512], P('smp', 'proto')
- grad_weight: float32 [131072, 512], P('proto', 'smp')
All inputs are finite; a program needn't handle non-finite values.
Results may differ from a plain program's by a relative error of at most 0.0085.
Values may be sent and summed in bfloat16 or wider, within the bound.
No kernel may reach another device: no remote copies, remote signals or barrier semaphores. Data moves between devices by JAX's collectives and lax.ppermute only.
A program may use at most 64 MiB of HBM per device.

v0:
```python
import jax
import jax.numpy as jnp
from jax import lax
from jax.sharding import PartitionSpec as P

ITERS = 3


TEACHER_TEMP = 0.07
STUDENT_TEMP = 0.1


def sent_to_all(x, axis):
    count = lax.axis_size(axis)
    return lax.all_to_all(jnp.broadcast_to(x[None], (count, *x.shape)), axis, 0, 0, tiled=True)


def taken_together(x, axis):
    return sent_to_all(x, axis).sum(axis=0)


def packed_total(arrays, axis):
    flat, at, done = (jnp.concatenate([a.reshape(-1) for a in arrays]), 0, [])
    total = taken_together(flat, axis)
    for a in arrays:
        done.append(total[at : at + a.size].reshape(a.shape))
        at += a.size
    return tuple(done)


def turned_gather(arrays, axis, dims):
    turned = [jnp.moveaxis(a, dim, 0) for a, dim in zip(arrays, dims)]
    widths = [t[0].size for t in turned]
    both = jnp.concatenate([t.reshape(-1, w) for t, w in zip(turned, widths)], axis=1)
    whole = lax.all_gather(both, axis, axis=0, tiled=True)
    pieces = jnp.split(whole, [sum(widths[:k]) for k in range(1, len(widths))], axis=1)
    return tuple(
        (
            jnp.moveaxis(b.reshape(-1, *t.shape[1:]), 0, dim)
            for b, t, dim in zip(pieces, turned, dims)
        )
    )


def cut_along(x, dim, count):
    before, after = (x.shape[:dim], x.shape[dim + 1 :])
    return jnp.moveaxis(x.reshape(*before, count, -1, *after), dim, 0)


def sent_and_summed(x, axis, dim):
    count = lax.axis_size(axis)
    pieces = lax.all_to_all(cut_along(x, dim, count), axis, 0, 0, tiled=True)
    return jnp.sum(pieces.astype(jnp.float32), axis=0)


def sum_at_owner(x, axis, dim):
    pieces = cut_along(x, dim, lax.axis_size(axis))
    arrived = lax.all_to_all(pieces, axis, split_axis=0, concat_axis=0, tiled=True)
    return arrived.sum(axis=0)


def unit_rows(features):
    values = features.astype(jnp.float32)
    scale = lax.rsqrt(jnp.sum(values * values, axis=1) + 1e-06)
    return ((values * scale[:, None]).astype(jnp.bfloat16), scale)


def project(rows, weight):
    return lax.dot_general(
        rows, weight, (((1,), (1,)), ((), ())), preferred_element_type=jnp.float32
    )


def sample_totals(values):
    return (taken_together(values[0], "proto"),)


def student_totals(values):
    return packed_total((values[0], values[1]), "proto")


def on_device(teacher_features, student_features, teacher_weight, student_weight):
    teacher_all, student_all = turned_gather((teacher_features, student_features), "proto", (1, 1))
    sample_rows = teacher_features.shape[0]
    proto_rows = teacher_weight.shape[0]
    samples = sample_rows * lax.axis_size("smp")
    protos = proto_rows * lax.axis_size("proto")
    teacher_unit, unused = unit_rows(teacher_all)
    student_unit, student_scale = unit_rows(student_all)
    kernel = jnp.exp(project(teacher_unit, teacher_weight) / TEACHER_TEMP)
    col_scale = jnp.ones((sample_rows,), jnp.float32)
    row_scale = jnp.ones((proto_rows,), jnp.float32)
    exp_total = None
    for step in range(ITERS):
        proto_mass = jnp.dot(col_scale, kernel, precision=lax.Precision.HIGHEST)
        row_scale = 1.0 / (protos * taken_together(proto_mass, "smp"))
        sample_part = jnp.dot(kernel, row_scale, precision=lax.Precision.HIGHEST)
        sample_mass = sample_totals((sample_part,))[0]
        col_scale = 1.0 / (samples * sample_mass)
    targets = samples * kernel * row_scale[None, :] * col_scale[:, None]
    logits = project(student_unit, student_weight) / STUDENT_TEMP
    expo = jnp.exp(logits)
    logits, expo, local_total = (logits, expo, jnp.sum(expo, axis=1))
    weighted = jnp.sum(targets * logits, axis=1)
    exp_total, weighted_total = student_totals((local_total, weighted))
    probs = expo / exp_total[:, None]
    sample_loss = jnp.log(exp_total) - weighted_total
    logit_grad = ((probs - targets) / (samples * STUDENT_TEMP)).astype(jnp.bfloat16)
    weight_part = lax.dot_general(
        logit_grad, student_unit, (((0,), (0,)), ((), ())), preferred_element_type=jnp.float32
    )
    grad_weight = sent_and_summed(weight_part.astype(jnp.bfloat16), "smp", 1)
    unit_part = jnp.dot(logit_grad, student_weight, preferred_element_type=jnp.float32)
    unit_grad = sum_at_owner(unit_part, "proto", 1)
    feats = student_features.astype(jnp.float32)
    inner_prod = taken_together(jnp.sum(feats * unit_grad, axis=1), "proto")
    grad_features = (
        student_scale[:, None] * unit_grad - (student_scale**3 * inner_prod)[:, None] * feats
    )
    return (sample_loss, grad_features, grad_weight)


def solution(mesh):
    placed = (P("smp", "proto"), P("smp", "proto"), P("proto", None), P("proto", None))
    return jax.shard_map(
        on_device,
        mesh=mesh,
        in_specs=placed,
        out_specs=(P("smp"), P("smp", "proto"), P("proto", "smp")),
        check_vma=False,
    )
```

profile of v0, /device:TPU:8, one launch (start us, length us, event | category | flops | bytes accessed | tf_op | source)
XLA Modules:
  0.0 290.4 jit_solution(18363776780646376817)
XLA Ops:
  0.6 0.0 copy-start
  0.6 0.9 pad_maximum_fusion
  1.5 71.8 %all_gather.3 = bf16[512,256]{1,0:T(8,128)(2,1)S(1)} all-gather(bf16[8,256]{1,0:T(8,128)(2,1)S(1)} %pad_maximum_fusion), channel_id=1, replica_groups=mesh['smp'=8,'proto'=64] {'proto'}, dimensions={0}, use_global_device_ids=true | all-gather | bytes 266240 | tf_op jit(solution)/shard_map/all_gather | solution.py:35
  73.3 0.1 fusion.3
  73.4 2.4 fusion
  75.8 0.6 fusion.21
  76.5 17.3 %all_to_all.58 = f32[8,1,2048]{2,1,0:T(1,128)S(1)} all-to-all(f32[8,1,2048]{2,1,0:T(1,128)S(1)} %broadcast_in_dim.16), channel_id=1, replica_groups=mesh['smp'=8,'proto'=64] {'smp'}, dimensions={0} | all-to-all | bytes 131072 | tf_op jit(solution)/shard_map/all_to_all | solution.py:15
  93.7 0.1 reduce_sum.138
  93.8 0.9 convolution_bitcast_fusion.3
  94.8 27.2 %all_to_all.59 = f32[64,1,128]{2,1,0:T(1,128)S(1)} all-to-all(f32[64,1,128]{2,1,0:T(1,128)S(1)} %broadcast_in_dim.17), channel_id=1, replica_groups=mesh['smp'=8,'proto'=64] {'proto'}, dimensions={0} | all-to-all | bytes 65536 | tf_op jit(solution)/shard_map/all_to_all | solution.py:15
  122.0 0.6 fusion.15
  122.6 12.9 %all_to_all.60 = f32[8,1,2048]{2,1,0:T(1,128)S(1)} all-to-all(f32[8,1,2048]{2,1,0:T(1,128)S(1)} %broadcast_in_dim.18), channel_id=1, replica_groups=mesh['smp'=8,'proto'=64] {'smp'}, dimensions={0} | all-to-all | bytes 131072 | tf_op jit(solution)/shard_map/all_to_all | solution.py:15
  135.5 0.1 reduce_sum.140
  135.6 0.9 convolution_bitcast_fusion.2
  136.6 13.4 %all_to_all.61 = f32[64,1,128]{2,1,0:T(1,128)S(1)} all-to-all(f32[64,1,128]{2,1,0:T(1,128)S(1)} %broadcast_in_dim.19), channel_id=1, replica_groups=mesh['smp'=8,'proto'=64] {'proto'}, dimensions={0} | all-to-all | bytes 65536 | tf_op jit(solution)/shard_map/all_to_all | solution.py:15
  150.0 0.6 fusion.13
  150.6 12.9 %all_to_all.62 = f32[8,1,2048]{2,1,0:T(1,128)S(1)} all-to-all(f32[8,1,2048]{2,1,0:T(1,128)S(1)} %broadcast_in_dim.20), channel_id=1, replica_groups=mesh['smp'=8,'proto'=64] {'smp'}, dimensions={0} | all-to-all | bytes 131072 | tf_op jit(solution)/shard_map/all_to_all | solution.py:15
  163.5 0.1 reduce_sum.142
  163.6 0.9 convolution_bitcast_fusion.1
  164.6 13.4 %all_to_all.63 = f32[64,1,128]{2,1,0:T(1,128)S(1)} all-to-all(f32[64,1,128]{2,1,0:T(1,128)S(1)} %broadcast_in_dim.21), channel_id=1, replica_groups=mesh['smp'=8,'proto'=64] {'proto'}, dimensions={0} | all-to-all | bytes 65536 | tf_op jit(solution)/shard_map/all_to_all | solution.py:15
  178.0 0.0 copy-done
  178.0 1.8 exponential_reduce_fusion
  179.9 13.7 %all_to_all.64 = f32[64,1,256]{2,1,0:T(1,128)S(1)} all-to-all(f32[64,1,256]{2,1,0:T(1,128)S(1)} %broadcast_in_dim.22), channel_id=1, replica_groups=mesh['smp'=8,'proto'=64] {'proto'}, dimensions={0} | all-to-all | bytes 131072 | tf_op jit(solution)/shard_map/all_to_all | solution.py:15
  193.6 0.1 reduce_sum.145
  193.7 0.5 fusion.32
  194.2 1.5 multiply_convert_fusion
  195.8 0.0 copy-start.1
  195.8 0.8 copy-done.1
  196.6 0.0 copy-start.2
  196.6 0.9 convolution_bitcast_fusion
  197.5 16.8 %all_to_all.65 = f32[64,128,8]{1,2,0:T(8,128)S(1)} all-to-all(f32[64,128,8]{1,2,0:T(8,128)S(1)} %convolution_bitcast_fusion), channel_id=1, replica_groups=mesh['smp'=8,'proto'=64] {'proto'}, dimensions={0} | all-to-all | bytes 524288 | tf_op jit(solution)/shard_map/all_to_all | solution.py:58
  214.3 0.1 reduce_sum.146
  214.4 0.0 copy-done.2
  214.4 0.6 broadcast_in_dim.23
  215.0 5.7 %all-to-all-start.8 = ((f32[64,1,128]{2,1,0:T(1,128)}), f32[64,1,128]{2,1,0:T(1,128)S(1)}, u32[]{:S(2)}, u32[]{:S(2)}) async-start(f32[64,1,128]{2,1,0:T(1,128)} %broadcast_in_dim.23), calls=%async_computation.8 | async-start | bytes 65536 | tf_op jit(solution)/shard_map/all_to_all | solution.py:15
  220.7 3.1 %convolution_convert_fusion = bf16[2048,512]{0,1:T(8,128)(2,1)} fusion(bf16[128,2048]{1,0:T(8,128)(2,1)} %copy-done.1, f32[128]{0:T(128)S(1)} %get-tuple-element.13, bf16[512,256]{1,0:T(8,128)(2,1)S(1)} %all_gather.3), kind=kOutput, calls=%fused_computation.1 | convolution fusion | flops 269680640 | bytes 2753024 | tf_op jit(solution)/shard_map/dot_general | solution.py:109
  223.8 5.8 %all-to-all-done.8 = f32[64,1,128]{2,1,0:T(1,128)S(1)} async-done(((f32[64,1,128]{2,1,0:T(1,128)}), f32[64,1,128]{2,1,0:T(1,128)S(1)}, u32[]{:S(2)}, u32[]{:S(2)}) %all-to-all-start.8) | async-done | bytes 32800 | tf_op jit(solution)/shard_map/all_to_all | solution.py:15
  229.6 4.4 %all-to-all-start.9 = ((bf16[8,2048,64]{1,2,0:T(8,128)(2,1)}), bf16[8,2048,64]{1,2,0:T(8,128)(2,1)}, u32[]{:S(2)}, u32[]{:S(2)}) async-start(bf16[8,2048,64]{1,2,0:T(8,128)(2,1)} %bitcast.45), calls=%async_computation.9 | async-start | bytes 4194304 | tf_op jit(solution)/shard_map/all_to_all | solution.py:52
  234.0 0.6 fusion.11
  234.6 53.0 %all-to-all-done.9 = bf16[8,2048,64]{1,2,0:T(8,128)(2,1)} async-done(((bf16[8,2048,64]{1,2,0:T(8,128)(2,1)}), bf16[8,2048,64]{1,2,0:T(8,128)(2,1)}, u32[]{:S(2)}, u32[]{:S(2)}) %all-to-all-start.9) | async-done | bytes 2097184 | tf_op jit(solution)/shard_map/all_to_all | solution.py:52
  287.6 2.8 convert_reduce_fusion
  (19 shorter events, 0.4 us)
Async XLA Ops:
  0.6 177.3 %copy-start = (bf16[2048,512]{1,0:T(8,128)(2,1)S(1)}, bf16[2048,512]{1,0:T(8,128)(2,1)}, u32[]{:S(2)}) copy-start(bf16[2048,512]{1,0:T(8,128)(2,1)} %param.7) | copy-start | bytes 6291460
  195.8 0.8 copy-start.1
  196.6 17.8 %copy-start.2 = (bf16[128,8]{0,1:T(8,128)(2,1)S(1)}, bf16[128,8]{0,1:T(8,128)(2,1)}, u32[]{:S(2)}) copy-start(bf16[128,8]{0,1:T(8,128)(2,1)} %param.5) | copy-start | bytes 6148
  215.0 14.5 %all-to-all-start.8 = ((f32[64,1,128]{2,1,0:T(1,128)}), f32[64,1,128]{2,1,0:T(1,128)S(1)}, u32[]{:S(2)}, u32[]{:S(2)}) async-start(f32[64,1,128]{2,1,0:T(1,128)} %broadcast_in_dim.23), calls=%async_computation.8 | async-start | bytes 65536 | tf_op jit(solution)/shard_map/all_to_all | solution.py:15
  229.6 58.0 %all-to-all-start.9 = ((bf16[8,2048,64]{1,2,0:T(8,128)(2,1)}), bf16[8,2048,64]{1,2,0:T(8,128)(2,1)}, u32[]{:S(2)}, u32[]{:S(2)}) async-start(bf16[8,2048,64]{1,2,0:T(8,128)(2,1)} %bitcast.45), calls=%async_computation.9 | async-start | bytes 4194304 | tf_op jit(solution)/shard_map/all_to_all | solution.py:52
where the time goes:
time: 291 us; the launch traced here: 290 us
  blocking collectives  199 us (68%)
  waiting for transfers between devices  58.8 us (20%)
  matrix products  12.9 us (4%)
  starting transfers between devices  10 us (3%)
  other arithmetic  6.86 us (2%)
    all_to_all x7, blocking collectives, sent_to_all(): lax.all_to_all(jnp.broadcast_to(x[None], (count, *x.shape)), axis, 0, 0,...  111 us
    all_gather x1, blocking collectives, turned_gather(): whole = lax.all_gather(both, axis, axis=0, tiled=True)  71.8 us
    all_to_all x1, waiting for transfers between devices, sent_and_summed(): pieces = lax.all_to_all(cut_along(x, dim, count), axis, 0, 0, tiled=True)  53 us
    all_to_all x1, blocking collectives, sum_at_owner(): lax.all_to_all(pieces, axis, split_axis=0, concat_axis=0, tiled=True)  16.8 us
  transfers between devices with their start and end apart: 2, of which 2 were waited for; matrix products, arithmetic and copies ran while one was open for 1% of the time, Pallas kernels for 0%

commit v1 on v0

v1 whole, which is shorter than its diff:
```python
import jax
import jax.numpy as jnp
import numpy as np
from jax import lax
from jax.sharding import PartitionSpec as P

ITERS = 3
TEACHER_TEMP = 0.07
STUDENT_TEMP = 0.1
BOTH = ("smp", "proto")
PARTS = {"x": 4, "yh": 2, "yl": 4, "z": 8, "c": 2}


def groups(names):
    order = list(PARTS)
    index = np.arange(512).reshape(tuple(PARTS.values()))
    inner = [order.index(n) for n in names]
    outer = [i for i in range(len(order)) if i not in inner]
    size = int(np.prod([PARTS[n] for n in names]))
    return index.transpose(outer + inner).reshape(-1, size).tolist()


def gathered(x, names):
    group = groups(names)
    copies = jnp.broadcast_to(x[None], (len(group[0]), *x.shape))
    return lax.all_to_all(copies, BOTH, 0, 0, tiled=True, axis_index_groups=group)


def sent_to_protos(x):
    return lax.all_to_all(jnp.broadcast_to(x[None], (64, *x.shape)), "proto", 0, 0, tiled=True)


def unit_columns(features):
    values = features.astype(jnp.float32)
    scale = lax.rsqrt(jnp.sum(values * values, axis=0) + 1e-06)
    return (values * scale[None, :]).astype(jnp.bfloat16), scale


def on_device(teacher_features, student_features, teacher_weight, student_weight):
    f32, bf16 = jnp.float32, jnp.bfloat16
    me = lax.axis_index("smp")
    samples, protos = 1024, 131072
    raw = jnp.concatenate([teacher_features.T, student_features.T], axis=0)
    first = gathered(raw, ("yh", "yl", "z"))
    teacher_1, student_1 = first[:, :8], first[:, 8:]
    teacher_2 = gathered(teacher_1, ("x",))
    teacher_2, student_1 = lax.optimization_barrier((teacher_2, student_1))
    teacher_3 = gathered(teacher_2, ("c",))
    teacher_all = teacher_3.reshape(2, 4, 2, 4, 8, 8, 128).transpose(3, 4, 0, 5, 1, 2, 6).reshape(512, 1024)
    student_2 = lax.all_gather(
        student_1.reshape(512, 128), BOTH, axis=0, tiled=True, axis_index_groups=groups(("x", "c"))
    )
    student_all = student_2.reshape(4, 2, 2, 4, 8, 8, 128).transpose(3, 4, 1, 5, 0, 2, 6).reshape(512, 1024)

    teacher_unit, unused = unit_columns(teacher_all)
    kernel = jnp.exp(jnp.dot(teacher_weight, teacher_unit, preferred_element_type=f32) / TEACHER_TEMP)
    student_unit, student_scale = unit_columns(student_all)
    logits = jnp.dot(student_weight, student_unit, preferred_element_type=f32) / STUDENT_TEMP
    expo = jnp.exp(logits)
    local_total = jnp.sum(expo, axis=0)

    col_scale = jnp.ones((samples,), f32)
    for step in range(ITERS):
        row_scale = 1.0 / (protos * jnp.sum(kernel * col_scale[None, :], axis=1))
        part = jnp.sum(kernel * row_scale[:, None], axis=0)
        if step < ITERS - 1:
            mass = jnp.sum(sent_to_protos(part.reshape(8, 128)), axis=0).reshape(-1)
        else:
            kernel_own = lax.dynamic_slice_in_dim(kernel, me * 128, 128, 1)
            logits_own = lax.dynamic_slice_in_dim(logits, me * 128, 128, 1)
            weighted = jnp.sum(kernel_own * row_scale[:, None] * logits_own, axis=0)
            packed = jnp.concatenate([part, local_total, weighted]).reshape(17, 128)
            sums = jnp.sum(sent_to_protos(packed), axis=0)
            mass, total, weighted = sums[:8].reshape(-1), sums[8:16].reshape(-1), sums[16]
        col_scale = 1.0 / (samples * mass)
    targets = samples * kernel * row_scale[:, None] * col_scale[None, :]
    logit_grad = ((expo / total[None, :] - targets) / (samples * STUDENT_TEMP)).astype(bf16)

    total_own = lax.dynamic_slice_in_dim(total, me * 128, 128)
    col_own = lax.dynamic_slice_in_dim(col_scale, me * 128, 128)
    sample_loss = jnp.log(total_own) - samples * col_own * weighted

    grad_own = lax.dynamic_slice_in_dim(logit_grad, me * 128, 128, 1)
    features_own = lax.dynamic_slice_in_dim(student_all, me * 128, 128, 1).astype(f32)
    scale_own = lax.dynamic_slice_in_dim(student_scale, me * 128, 128)
    unit_part = lax.dot_general(
        student_weight, grad_own, (((0,), (0,)), ((), ())), preferred_element_type=f32
    )
    inner_part = jnp.sum(features_own * unit_part, axis=0)
    pieces = jnp.concatenate(
        [unit_part.reshape(64, 8, 128), jnp.broadcast_to(inner_part[None, None], (64, 1, 128))], axis=1
    )
    unit_sums = jnp.sum(lax.all_to_all(pieces, "proto", 0, 0, tiled=True), axis=0)
    unit_grad, inner_prod = unit_sums[:8], unit_sums[8]
    feats = student_features.T.astype(f32)
    grad_features = scale_own[None] * unit_grad - (scale_own**3 * inner_prod)[None] * feats

    unit_slice = lax.dynamic_slice_in_dim(student_unit, me * 64, 64, 0)
    grad_weight = lax.dot_general(
        unit_slice, logit_grad, (((1,), (1,)), ((), ())), preferred_element_type=f32
    )
    return sample_loss, grad_features.T, grad_weight.T


def solution(mesh):
    placed = (P("smp", "proto"), P("smp", "proto"), P("proto", None), P("proto", None))
    return jax.shard_map(
        on_device,
        mesh=mesh,
        in_specs=placed,
        out_specs=(P("smp"), P("smp", "proto"), P("proto", "smp")),
        check_vma=False,
    )
```

time: 291 us -> 200 us (0.69)
  the two profiles are of different devices: /device:TPU:8 before, /device:TPU:1 now
where the time goes in v1:
time: 200 us; the launch traced here: 199 us
  waiting for transfers between devices  58.7 us (29%)
  blocking collectives  49.4 us (25%)
  other arithmetic  28.7 us (14%)
  starting transfers between devices  22.6 us (11%)
  local copies, waits for them, and re-layouts  15.4 us (8%)
  between operations  14.3 us (7%)
  matrix products  9.98 us (5%)
    all_to_all x3, blocking collectives, gathered(): lax.all_to_all(copies, BOTH, 0, 0, tiled=True, axis_index_groups=group)  49.4 us
    all_to_all x3, waiting for transfers between devices, sent_to_protos(): lax.all_to_all(jnp.broadcast_to(x[None], (64, *x.shape)), 'proto', 0, 0,...  45.4 us
    all_to_all x3, starting transfers between devices, sent_to_protos(): lax.all_to_all(jnp.broadcast_to(x[None], (64, *x.shape)), 'proto', 0, 0,...  16.6 us
    all_to_all x1, waiting for transfers between devices, on_device(): lax.all_to_all(pieces, 'proto', 0, 0, tiled=True)  12.6 us
    unnamed x17, local copies, waits for them, and re-layouts  10.1 us
    reduce_sum x2, other arithmetic, on_device(): row_scale = 1.0 / (protos * jnp.sum(kernel * col_scale[None, :], axis=1))  8.26 us
    convert_element_type x1, other arithmetic, on_device(): ((expo / total[None, :] - targets) / (samples * STUDENT_TEMP)).astype(bf16)  7 us
    all_to_all x1, starting transfers between devices, on_device(): lax.all_to_all(pieces, 'proto', 0, 0, tiled=True)  5.99 us
  transfers between devices with their start and end apart: 5, of which 4 were waited for; matrix products, arithmetic and copies ran while one was open for 9% of the time, Pallas kernels for 0%

profile of v1, /device:TPU:1, one launch (start us, length us, event | category | flops | bytes accessed | tf_op | source)
XLA Modules:
  0.0 199.1 jit_solution(7027211904592664058)
XLA Ops:
  7.2 0.0 copy-start
  7.2 0.0 copy-start.7
  7.2 0.9 pad_maximum_fusion.1
  8.1 29.6 %all_to_all.35 = bf16[64,16,128]{2,1,0:T(8,128)(2,1)S(1)} all-to-all(bf16[64,16,128]{2,1,0:T(8,128)(2,1)S(1)} %broadcast_in_dim.20), channel_id=1, replica_groups={{0,2,4,6,8,10,12,14,16,18,20,22,24,26,28,30,32,34,36,38,40,42,44,46,48,..., dimensions={0} | all-to-all | bytes 524288 | tf_op jit(solution)/shard_map/all_to_all | solution.py:26
  37.7 0.7 fusion.13
  38.4 0.1 broadcast_in_dim.21
  38.5 10.7 %all_to_all.36 = bf16[4,64,8,128]{3,2,1,0:T(8,128)(2,1)S(1)} all-to-all(bf16[4,64,8,128]{3,2,1,0:T(8,128)(2,1)S(1)} %broadcast_in_dim.21), channel_id=1, replica_groups={{0,128,256,384},{1,129,257,385},{2,130,258,386},{3,131,259,387},{4,132,..., dimensions={0} | all-to-all | bytes 1048576 | tf_op jit(solution)/shard_map/all_to_all | solution.py:26
  49.2 0.1 broadcast_in_dim.22
  49.3 9.0 %all_to_all.37 = bf16[2,4,64,8,128]{4,3,2,1,0:T(8,128)(2,1)S(1)} all-to-all(bf16[2,4,64,8,128]{4,3,2,1,0:T(8,128)(2,1)S(1)} %broadcast_in_dim.22), channel_id=1, replica_groups={{0,1},{2,3},{4,5},{6,7},{8,9},{10,11},{12,13},{14,15},{16,17},{18,19},{..., dimensions={0} | all-to-all | bytes 2097152 | tf_op jit(solution)/shard_map/all_to_all | solution.py:26
  58.4 0.1 convert_element_type.53
  58.5 0.3 copy.18
  58.8 0.4 multiply_reduce_fusion.6
  59.3 0.0 copy-done.7
  59.3 2.8 %fusion.14 = (f32[2048]{0:T(1024)S(1)}, f32[1024,2048]{1,0:T(8,128)S(1)}) fusion(bf16[2048,512]{1,0:T(8,128)(2,1)S(1)} %copy-done.7, f32[512,1024]{1,0:T(8,128)S(1)} %bitcast.53, f32[1024]{0:T(1024)S(1)} %bitcast.61), kind=kOutput, calls=%fused_computation.49 | convolution fusion | flops 2152724480 | bytes 12595200 | tf_op jit(solution)/shard_map/dot_general | solution.py:56
  62.1 0.0 copy-start.1
  62.1 3.2 %copy-done.1 = f32[1024,2048]{1,0:T(8,128)} copy-done((f32[1024,2048]{1,0:T(8,128)}, f32[1024,2048]{1,0:T(8,128)S(1)}, u32[]{:S(2)}) %copy-start.1) | copy-done | bytes 8388632
  65.3 0.6 multiply_reduce_fusion.4
  65.9 0.7 broadcast_in_dim.24
  66.6 4.5 %all-to-all-start.3 = ((f32[64,8,128]{2,1,0:T(8,128)}), f32[64,8,128]{2,1,0:T(8,128)S(1)}, u32[]{:S(2)}, u32[]{:S(2)}) async-start(f32[64,8,128]{2,1,0:T(8,128)} %broadcast_in_dim.24), calls=%async_computation.3 | async-start | bytes 524288 | tf_op jit(solution)/shard_map/all_to_all | solution.py:30
  71.1 0.0 all-gather.2.cloned.1.call-start
  71.2 0.7 all-gather.2.cloned.1.call-update
  71.8 11.0 %all-to-all-done.3 = f32[64,8,128]{2,1,0:T(8,128)S(1)} async-done(((f32[64,8,128]{2,1,0:T(8,128)}), f32[64,8,128]{2,1,0:T(8,128)S(1)}, u32[]{:S(2)}, u32[]{:S(2)}) %all-to-all-start.3) | async-done | bytes 262176 | tf_op jit(solution)/shard_map/all_to_all | solution.py:30
  82.9 0.1 reduce_sum.147
  82.9 0.0 copy-start.2
  82.9 4.3 %multiply_reduce_fusion.3 = f32[2048]{0:T(1024)S(1)} fusion(f32[1024,2048]{1,0:T(8,128)} %copy-done.1, f32[1024]{0:T(1024)S(1)} %divide_bitcast_fusion.1), kind=kLoop, calls=%fused_computation.4 | loop fusion | flops 4192256 | bytes 8400896 | tf_op jit(solution)/shard_map/reduce_sum | solution.py:64
  87.2 1.7 copy-done.2
  88.9 0.6 multiply_reduce_fusion.2
  89.5 0.7 broadcast_in_dim.26
  90.3 6.0 %all-to-all-start.4 = ((f32[64,8,128]{2,1,0:T(8,128)}), f32[64,8,128]{2,1,0:T(8,128)S(1)}, u32[]{:S(2)}, u32[]{:S(2)}) async-start(f32[64,8,128]{2,1,0:T(8,128)} %broadcast_in_dim.26), calls=%async_computation.4 | async-start | bytes 524288 | tf_op jit(solution)/shard_map/all_to_all | solution.py:30
  96.2 11.6 %all-to-all-done.4 = f32[64,8,128]{2,1,0:T(8,128)S(1)} async-done(((f32[64,8,128]{2,1,0:T(8,128)}), f32[64,8,128]{2,1,0:T(8,128)S(1)}, u32[]{:S(2)}, u32[]{:S(2)}) %all-to-all-start.4) | async-done | bytes 262176 | tf_op jit(solution)/shard_map/all_to_all | solution.py:30
  107.9 0.1 reduce_sum.150
  107.9 4.0 %multiply_reduce_fusion.1 = f32[2048]{0:T(1024)S(1)} fusion(f32[1024,2048]{1,0:T(8,128)} %copy-done.1, f32[1024]{0:T(1024)S(1)} %divide_bitcast_fusion), kind=kLoop, calls=%fused_computation.2 | loop fusion | flops 4192256 | bytes 8400896 | tf_op jit(solution)/shard_map/reduce_sum | solution.py:64
  112.0 4.0 %multiply_reduce_fusion = f32[1024]{0:T(1024)S(1)} fusion(f32[1024,2048]{1,0:T(8,128)} %copy-done.1, f32[2048]{0:T(1024)S(1)} %get-tuple-element.14), kind=kLoop, calls=%fused_computation.1 | loop fusion | flops 4193280 | bytes 8400896 | tf_op jit(solution)/shard_map/reduce_sum | solution.py:65
  116.0 0.0 all-gather.2.cloned.1.call-done
  116.0 1.5 copy.19
  117.5 1.4 multiply_reduce_fusion.5
  119.0 0.2 multiply_convert_fusion.1
  119.2 0.0 copy-done
  119.2 0.0 copy-start.5
  119.2 2.7 %exponential_reduce_fusion = (f32[1024]{0:T(1024)S(1)}, f32[1024,2048]{1,0:T(8,128)S(1)}) fusion(bf16[512,1024]{1,0:T(8,128)(2,1)S(1)} %multiply_convert_fusion.1, bf16[2048,512]{1,0:T(8,128)(2,1)S(1)} %copy-done), kind=kOutput, calls=%fused_computation.7 | convolution fusion | flops 2151676928 | bytes 11538432 | tf_op jit(solution)/shard_map/dot_general | solution.py:58
  122.0 0.0 copy-start.4
  122.0 3.2 %copy-done.4 = f32[1024,2048]{1,0:T(8,128)} copy-done((f32[1024,2048]{1,0:T(8,128)}, f32[1024,2048]{1,0:T(8,128)S(1)}, u32[]{:S(2)}) %copy-start.4) | copy-done | bytes 8388632
  125.2 1.4 multiply_reduce_fusion.7
  126.6 0.0 copy-done.5
  126.6 0.9 broadcast_in_dim.28
  127.5 6.2 %all-to-all-start.5 = ((f32[64,17,128]{2,1,0:T(8,128)}), f32[64,17,128]{2,1,0:T(8,128)}, u32[]{:S(2)}, u32[]{:S(2)}) async-start(f32[64,17,128]{2,1,0:T(8,128)} %broadcast_in_dim.28), calls=%async_computation.5 | async-start | bytes 1572864 | tf_op jit(solution)/shard_map/all_to_all | solution.py:30
  133.8 0.1 copy.27
  133.9 22.8 %all-to-all-done.5 = f32[64,17,128]{2,1,0:T(8,128)} async-done(((f32[64,17,128]{2,1,0:T(8,128)}), f32[64,17,128]{2,1,0:T(8,128)}, u32[]{:S(2)}, u32[]{:S(2)}) %all-to-all-start.5) | async-done | bytes 557088 | tf_op jit(solution)/shard_map/all_to_all | solution.py:30
  156.7 1.2 reduce_sum.156
  157.9 7.0 %multiply_convert_fusion = bf16[1024,2048]{1,0:T(8,128)(2,1)S(1)} fusion(f32[1024,2048]{1,0:T(8,128)} %copy-done.1, f32[1024,2048]{1,0:T(8,128)} %copy-done.4, f32[1024]{0:T(1024)S(1)} %get-tuple-element.12, f32[2048]{0:T(1024)S(1)} %get-tuple-element.13, f32[1024]{0:T(1024)S(1)} %get-tuple-element.11), kind=kLoop, calls=%fused_computation | loop fusion | flops 12582912 | bytes 20987904 | tf_op jit(solution)/shard_map/convert_element_type | solution.py:77
  164.9 0.0 copy-start.3
  164.9 1.9 copy-done.3
  166.8 0.0 copy-start.6
  166.8 0.6 multiply_reduce_fusion.8
  167.4 0.1 copy.21
  167.5 0.8 pad_maximum_fusion
  168.4 6.0 %all-to-all-start.6 = ((f32[64,9,128]{2,1,0:T(8,128)}), f32[64,9,128]{2,1,0:T(8,128)S(1)}, u32[]{:S(2)}, u32[]{:S(2)}) async-start(f32[64,9,128]{2,1,0:T(8,128)} %pad_maximum_fusion), calls=%async_computation.6 | async-start | bytes 1048576 | tf_op jit(solution)/shard_map/all_to_all | solution.py:93
  174.4 0.6 fusion.12
  175.0 3.9 %fusion.2 = f32[2048,64]{0,1:T(8,128)} fusion(bf16[1024,2048]{1,0:T(8,128)(2,1)} %copy-done.3, bf16[512,1024]{1,0:T(8,128)(2,1)} %copy-done.5, s32[]{:T(128)S(6)} %select_n.5), kind=kOutput, calls=%fused_computation.20 | convolution fusion | flops 268435456 | bytes 4849668 | tf_op jit(solution)/shard_map/dot_general | solution.py:99
  178.9 12.6 %all-to-all-done.6 = f32[64,9,128]{2,1,0:T(8,128)S(1)} async-done(((f32[64,9,128]{2,1,0:T(8,128)}), f32[64,9,128]{2,1,0:T(8,128)S(1)}, u32[]{:S(2)}, u32[]{:S(2)}) %all-to-all-start.6) | async-done | bytes 294944 | tf_op jit(solution)/shard_map/all_to_all | solution.py:93
  191.5 0.1 reduce_sum.158
  191.6 0.1 fusion.10
  191.7 0.0 copy-done.6
  191.7 0.6 fusion.5
  (13 shorter events, 0.2 us)
Async XLA Ops:
  7.2 112.1 %copy-start = (bf16[2048,512]{1,0:T(8,128)(2,1)S(1)}, bf16[2048,512]{1,0:T(8,128)(2,1)}, u32[]{:S(2)}) copy-start(bf16[2048,512]{1,0:T(8,128)(2,1)} %param.7) | copy-start | bytes 6291460
  7.2 52.1 %copy-start.7 = (bf16[2048,512]{1,0:T(8,128)(2,1)S(1)}, bf16[2048,512]{1,0:T(8,128)(2,1)}, u32[]{:S(2)}) copy-start(bf16[2048,512]{1,0:T(8,128)(2,1)} %param.6) | copy-start | bytes 6291460
  62.1 3.2 %copy-start.1 = (f32[1024,2048]{1,0:T(8,128)}, f32[1024,2048]{1,0:T(8,128)S(1)}, u32[]{:S(2)}) copy-start(f32[1024,2048]{1,0:T(8,128)S(1)} %get-tuple-element.16) | copy-start | bytes 25165828
  66.6 16.2 %all-to-all-start.3 = ((f32[64,8,128]{2,1,0:T(8,128)}), f32[64,8,128]{2,1,0:T(8,128)S(1)}, u32[]{:S(2)}, u32[]{:S(2)}) async-start(f32[64,8,128]{2,1,0:T(8,128)} %broadcast_in_dim.24), calls=%async_computation.3 | async-start | bytes 524288 | tf_op jit(solution)/shard_map/all_to_all | solution.py:30
  71.1 44.9 %all-gather.2.cloned.1.call-start = ((), (), s32[]{:S(2)}) async-start(), calls=%async_computation.7 | async-start | bytes 1179648 | tf_op jit(solution)/shard_map/all_gather | solution.py:50
  82.9 6.0 %copy-start.2 = (f32[1024,2048]{1,0:T(8,128)S(1)}, f32[1024,2048]{1,0:T(8,128)}, u32[]{:S(2)}) copy-start(f32[1024,2048]{1,0:T(8,128)} %copy-done.1) | copy-start | bytes 25165828
  90.3 17.6 %all-to-all-start.4 = ((f32[64,8,128]{2,1,0:T(8,128)}), f32[64,8,128]{2,1,0:T(8,128)S(1)}, u32[]{:S(2)}, u32[]{:S(2)}) async-start(f32[64,8,128]{2,1,0:T(8,128)} %broadcast_in_dim.26), calls=%async_computation.4 | async-start | bytes 524288 | tf_op jit(solution)/shard_map/all_to_all | solution.py:30
  119.2 7.4 %copy-start.5 = (bf16[512,1024]{1,0:T(8,128)(2,1)}, bf16[512,1024]{1,0:T(8,128)(2,1)S(1)}, u32[]{:S(2)}) copy-start(bf16[512,1024]{1,0:T(8,128)(2,1)S(1)} %multiply_convert_fusion.1) | copy-start | bytes 3145732
  122.0 3.2 %copy-start.4 = (f32[1024,2048]{1,0:T(8,128)}, f32[1024,2048]{1,0:T(8,128)S(1)}, u32[]{:S(2)}) copy-start(f32[1024,2048]{1,0:T(8,128)S(1)} %get-tuple-element.18) | copy-start | bytes 25165828
  127.5 29.1 %all-to-all-start.5 = ((f32[64,17,128]{2,1,0:T(8,128)}), f32[64,17,128]{2,1,0:T(8,128)}, u32[]{:S(2)}, u32[]{:S(2)}) async-start(f32[64,17,128]{2,1,0:T(8,128)} %broadcast_in_dim.28), calls=%async_computation.5 | async-start | bytes 1572864 | tf_op jit(solution)/shard_map/all_to_all | solution.py:30
  164.9 1.9 copy-start.3
  166.8 24.9 %copy-start.6 = (bf16[128,8]{0,1:T(8,128)(2,1)S(1)}, bf16[128,8]{0,1:T(8,128)(2,1)}, u32[]{:S(2)}) copy-start(bf16[128,8]{0,1:T(8,128)(2,1)} %param.5) | copy-start | bytes 6148
  168.4 23.1 %all-to-all-start.6 = ((f32[64,9,128]{2,1,0:T(8,128)}), f32[64,9,128]{2,1,0:T(8,128)S(1)}, u32[]{:S(2)}, u32[]{:S(2)}) async-start(f32[64,9,128]{2,1,0:T(8,128)} %pad_maximum_fusion), calls=%async_computation.6 | async-start | bytes 1048576 | tf_op jit(solution)/shard_map/all_to_all | solution.py:93
Sparse Core Ops, SparseCore 0:
  74.1 26.1 all-gather.1

commit v2 on v1

--- a/solution.py
+++ b/solution.py
@@ -42,15 +42,10 @@
     samples, protos = 1024, 131072
     raw = jnp.concatenate([teacher_features.T, student_features.T], axis=0)
     first = gathered(raw, ("yh", "yl", "z"))
-    teacher_1, student_1 = first[:, :8], first[:, 8:]
-    teacher_2 = gathered(teacher_1, ("x",))
-    teacher_2, student_1 = lax.optimization_barrier((teacher_2, student_1))
-    teacher_3 = gathered(teacher_2, ("c",))
-    teacher_all = teacher_3.reshape(2, 4, 2, 4, 8, 8, 128).transpose(3, 4, 0, 5, 1, 2, 6).reshape(512, 1024)
-    student_2 = lax.all_gather(
-        student_1.reshape(512, 128), BOTH, axis=0, tiled=True, axis_index_groups=groups(("x", "c"))
-    )
-    student_all = student_2.reshape(4, 2, 2, 4, 8, 8, 128).transpose(3, 4, 1, 5, 0, 2, 6).reshape(512, 1024)
+    second = gathered(first, ("x",))
+    third = gathered(second, ("c",)).reshape(2, 4, 2, 4, 8, 2, 8, 128)
+    both = third.transpose(5, 3, 4, 0, 6, 1, 2, 7).reshape(2, 512, 1024)
+    teacher_all, student_all = both[0], both[1]
 
     teacher_unit, unused = unit_columns(teacher_all)
     kernel = jnp.exp(jnp.dot(teacher_weight, teacher_unit, preferred_element_type=f32) / TEACHER_TEMP)

time: 200 us -> 184 us (0.920)
  between operations: 14.3 us -> 0.88 us
  waiting for transfers between devices: 58.7 us -> 48.8 us
  blocking collectives: 49.4 us -> 54.5 us
  matrix products: 9.98 us -> 14.4 us
  local copies, waits for them, and re-layouts: 15.4 us -> 11.6 us
    all_to_all x3, waiting for transfers between devices: 45.4 us -> 36.2 us  [sent_to_protos(): lax.all_to_all(jnp.broadcast_to(x[None], (64, *x.shape)), 'proto', 0, 0,...]
    all_to_all x3, blocking collectives: 49.4 us -> 54.5 us  [gathered(): lax.all_to_all(copies, BOTH, 0, 0, tiled=True, axis_index_groups=group)]
    dot_general x1, matrix products: 2.72 us -> 7.06 us  [on_device(): jnp.dot(student_weight, student_unit, preferred_element_type=f32)]
    unnamed x17 -> x13, local copies, waits for them, and re-layouts: 10.1 us -> 6.83 us
  transfers between devices with their start and end apart: 5 -> 4, of which waited for: 4 -> 4; matrix products, arithmetic and copies ran while one was open for 9% -> 8% of each run, Pallas kernels for 0% -> 0%
where the time goes in v2:
time: 184 us
  blocking collectives  54.5 us (30%)
  waiting for transfers between devices  48.8 us (27%)
  other arithmetic  29.7 us (16%)
  starting transfers between devices  23.8 us (13%)
  matrix products  14.4 us (8%)
  local copies, waits for them, and re-layouts  11.6 us (6%)
    all_to_all x3, blocking collectives, gathered(): lax.all_to_all(copies, BOTH, 0, 0, tiled=True, axis_index_groups=group)  54.5 us
    all_to_all x3, waiting for transfers between devices, sent_to_protos(): lax.all_to_all(jnp.broadcast_to(x[None], (64, *x.shape)), 'proto', 0, 0,...  36.2 us
    all_to_all x3, starting transfers between devices, sent_to_protos(): lax.all_to_all(jnp.broadcast_to(x[None], (64, *x.shape)), 'proto', 0, 0,...  17.9 us
    all_to_all x1, waiting for transfers between devices, on_device(): lax.all_to_all(pieces, 'proto', 0, 0, tiled=True)  12.6 us
    reduce_sum x2, other arithmetic, on_device(): row_scale = 1.0 / (protos * jnp.sum(kernel * col_scale[None, :], axis=1))  8.16 us
    dot_general x1, matrix products, on_device(): jnp.dot(student_weight, student_unit, preferred_element_type=f32)  7.06 us
    convert_element_type x1, other arithmetic, on_device(): ((expo / total[None, :] - targets) / (samples * STUDENT_TEMP)).astype(bf16)  7 us
    unnamed x13, local copies, waits for them, and re-layouts  6.83 us
  transfers between devices with their start and end apart: 4, of which 4 were waited for; matrix products, arithmetic and copies ran while one was open for 8% of the time, Pallas kernels for 0%

profile of v2, /device:TPU:1, one launch (start us, length us, event | category | flops | bytes accessed | tf_op | source)
XLA Modules:
  0.0 183.7 jit_solution(14504845237158129681)
XLA Ops:
  0.6 0.0 copy-start
  0.6 0.8 pad_maximum_fusion.1
  1.5 29.5 %all_to_all.35 = bf16[64,16,128]{2,1,0:T(8,128)(2,1)S(1)} all-to-all(bf16[64,16,128]{2,1,0:T(8,128)(2,1)S(1)} %broadcast_in_dim.20), channel_id=1, replica_groups={{0,2,4,6,8,10,12,14,16,18,20,22,24,26,28,30,32,34,36,38,40,42,44,46,48,..., dimensions={0} | all-to-all | bytes 524288 | tf_op jit(solution)/shard_map/all_to_all | solution.py:26
  31.0 0.1 broadcast_in_dim.21
  31.2 15.2 %all_to_all.36 = bf16[4,64,16,128]{3,2,1,0:T(8,128)(2,1)S(1)} all-to-all(bf16[4,64,16,128]{3,2,1,0:T(8,128)(2,1)S(1)} %broadcast_in_dim.21), channel_id=1, replica_groups={{0,128,256,384},{1,129,257,385},{2,130,258,386},{3,131,259,387},{4,132,..., dimensions={0} | all-to-all | bytes 2097152 | tf_op jit(solution)/shard_map/all_to_all | solution.py:26
  46.4 0.3 broadcast_in_dim.22
  46.7 0.0 copy-start.5
  46.7 9.8 %all_to_all.37 = bf16[2,4,64,16,128]{4,3,2,1,0:T(8,128)(2,1)S(1)} all-to-all(bf16[2,4,64,16,128]{4,3,2,1,0:T(8,128)(2,1)S(1)} %broadcast_in_dim.22), channel_id=1, replica_groups={{0,1},{2,3},{4,5},{6,7},{8,9},{10,11},{12,13},{14,15},{16,17},{18,19},{..., dimensions={0} | all-to-all | bytes 4194304 | tf_op jit(solution)/shard_map/all_to_all | solution.py:26
  56.5 1.5 slice_convert_fusion
  58.0 0.3 multiply_reduce_fusion.6
  58.3 0.3 copy.15
  58.6 0.0 copy-done.5
  58.6 2.8 %fusion.13 = (f32[2048]{0:T(1024)S(1)}, f32[1024,2048]{1,0:T(8,128)S(1)}) fusion(bf16[2048,512]{1,0:T(8,128)(2,1)S(1)} %copy-done.5, f32[512,1024]{1,0:T(8,128)S(1)} %bitcast.46, f32[1024]{0:T(1024)S(1)} %bitcast.53), kind=kOutput, calls=%fused_computation.48 | convolution fusion | flops 2152724480 | bytes 12595200 | tf_op jit(solution)/shard_map/dot_general | solution.py:51
  61.5 0.0 copy-start.1
  61.5 3.2 %copy-done.1 = f32[1024,2048]{1,0:T(8,128)} copy-done((f32[1024,2048]{1,0:T(8,128)}, f32[1024,2048]{1,0:T(8,128)S(1)}, u32[]{:S(2)}) %copy-start.1) | copy-done | bytes 8388632
  64.7 0.6 multiply_reduce_fusion.4
  65.3 0.7 broadcast_in_dim.24
  66.0 5.6 %all-to-all-start.3 = ((f32[64,8,128]{2,1,0:T(8,128)}), f32[64,8,128]{2,1,0:T(8,128)S(1)}, u32[]{:S(2)}, u32[]{:S(2)}) async-start(f32[64,8,128]{2,1,0:T(8,128)} %broadcast_in_dim.24), calls=%async_computation.3 | async-start | bytes 524288 | tf_op jit(solution)/shard_map/all_to_all | solution.py:30
  71.6 1.5 copy.16
  73.1 1.2 multiply_convert_fusion.1
  74.4 8.9 %all-to-all-done.3 = f32[64,8,128]{2,1,0:T(8,128)S(1)} async-done(((f32[64,8,128]{2,1,0:T(8,128)}), f32[64,8,128]{2,1,0:T(8,128)S(1)}, u32[]{:S(2)}, u32[]{:S(2)}) %all-to-all-start.3) | async-done | bytes 262176 | tf_op jit(solution)/shard_map/all_to_all | solution.py:30
  83.2 0.1 reduce_sum.138
  83.3 0.0 copy-start.2
  83.3 4.2 %multiply_reduce_fusion.3 = f32[2048]{0:T(1024)S(1)} fusion(f32[1024,2048]{1,0:T(8,128)} %copy-done.1, f32[1024]{0:T(1024)S(1)} %divide_bitcast_fusion.1), kind=kLoop, calls=%fused_computation.4 | loop fusion | flops 4192256 | bytes 8400896 | tf_op jit(solution)/shard_map/reduce_sum | solution.py:59
  87.5 1.6 copy-done.2
  89.1 0.6 multiply_reduce_fusion.2
  89.7 0.7 broadcast_in_dim.26
  90.4 6.0 %all-to-all-start.4 = ((f32[64,8,128]{2,1,0:T(8,128)}), f32[64,8,128]{2,1,0:T(8,128)S(1)}, u32[]{:S(2)}, u32[]{:S(2)}) async-start(f32[64,8,128]{2,1,0:T(8,128)} %broadcast_in_dim.26), calls=%async_computation.4 | async-start | bytes 524288 | tf_op jit(solution)/shard_map/all_to_all | solution.py:30
  96.5 0.0 copy-done
  96.5 7.1 %exponential_reduce_fusion = (f32[1024]{0:T(1024)S(1)}, f32[1024,2048]{1,0:T(8,128)}) fusion(bf16[512,1024]{1,0:T(8,128)(2,1)} %multiply_convert_fusion.1, bf16[2048,512]{1,0:T(8,128)(2,1)S(1)} %copy-done), kind=kOutput, calls=%fused_computation.7 | convolution fusion | flops 2151676928 | bytes 11538432 | tf_op jit(solution)/shard_map/dot_general | solution.py:53
  103.5 4.6 %all-to-all-done.4 = f32[64,8,128]{2,1,0:T(8,128)S(1)} async-done(((f32[64,8,128]{2,1,0:T(8,128)}), f32[64,8,128]{2,1,0:T(8,128)S(1)}, u32[]{:S(2)}, u32[]{:S(2)}) %all-to-all-start.4) | async-done | bytes 262176 | tf_op jit(solution)/shard_map/all_to_all | solution.py:30
  108.1 0.1 reduce_sum.141
  108.2 4.0 %multiply_reduce_fusion.1 = f32[2048]{0:T(1024)S(1)} fusion(f32[1024,2048]{1,0:T(8,128)} %copy-done.1, f32[1024]{0:T(1024)S(1)} %divide_bitcast_fusion), kind=kLoop, calls=%fused_computation.2 | loop fusion | flops 4192256 | bytes 8400896 | tf_op jit(solution)/shard_map/reduce_sum | solution.py:59
  112.2 4.0 %multiply_reduce_fusion = f32[1024]{0:T(1024)S(1)} fusion(f32[1024,2048]{1,0:T(8,128)} %copy-done.1, f32[2048]{0:T(1024)S(1)} %get-tuple-element.12), kind=kLoop, calls=%fused_computation.1 | loop fusion | flops 4193280 | bytes 8400896 | tf_op jit(solution)/shard_map/reduce_sum | solution.py:60
  116.2 1.7 multiply_reduce_fusion.7
  118.0 0.9 broadcast_in_dim.28
  118.9 6.3 %all-to-all-start.5 = ((f32[64,17,128]{2,1,0:T(8,128)}), f32[64,17,128]{2,1,0:T(8,128)}, u32[]{:S(2)}, u32[]{:S(2)}) async-start(f32[64,17,128]{2,1,0:T(8,128)} %broadcast_in_dim.28), calls=%async_computation.5 | async-start | bytes 1572864 | tf_op jit(solution)/shard_map/all_to_all | solution.py:30
  125.3 0.1 copy.24
  125.4 22.8 %all-to-all-done.5 = f32[64,17,128]{2,1,0:T(8,128)} async-done(((f32[64,17,128]{2,1,0:T(8,128)}), f32[64,17,128]{2,1,0:T(8,128)}, u32[]{:S(2)}, u32[]{:S(2)}) %all-to-all-start.5) | async-done | bytes 557088 | tf_op jit(solution)/shard_map/all_to_all | solution.py:30
  148.2 1.2 reduce_sum.147
  149.4 7.0 %multiply_convert_fusion = bf16[1024,2048]{1,0:T(8,128)(2,1)S(1)} fusion(f32[1024,2048]{1,0:T(8,128)} %copy-done.1, f32[1024,2048]{1,0:T(8,128)} %get-tuple-element.16, f32[1024]{0:T(1024)S(1)} %get-tuple-element.10, f32[2048]{0:T(1024)S(1)} %get-tuple-element.11, f32[1024]{0:T(1024)S(1)} %get-tuple-element.9), kind=kLoop, calls=%fused_computation | loop fusion | flops 12582912 | bytes 20987904 | tf_op jit(solution)/shard_map/convert_element_type | solution.py:72
  156.4 0.0 copy-start.3
  156.4 1.9 %copy-done.3 = bf16[1024,2048]{1,0:T(8,128)(2,1)} copy-done((bf16[1024,2048]{1,0:T(8,128)(2,1)}, bf16[1024,2048]{1,0:T(8,128)(2,1)S(1)}, u32[]{:S(2)}) %copy-start.3) | copy-done | bytes 4194328
  158.4 0.0 copy-start.4
  158.4 0.6 multiply_reduce_fusion.8
  158.9 0.1 copy.18
  159.1 0.8 pad_maximum_fusion
  159.9 5.9 %all-to-all-start.6 = ((f32[64,9,128]{2,1,0:T(8,128)}), f32[64,9,128]{2,1,0:T(8,128)S(1)}, u32[]{:S(2)}, u32[]{:S(2)}) async-start(f32[64,9,128]{2,1,0:T(8,128)} %pad_maximum_fusion), calls=%async_computation.6 | async-start | bytes 1048576 | tf_op jit(solution)/shard_map/all_to_all | solution.py:88
  165.8 0.6 fusion.12
  166.4 3.9 %fusion.2 = f32[2048,64]{0,1:T(8,128)} fusion(bf16[1024,2048]{1,0:T(8,128)(2,1)} %copy-done.3, bf16[512,1024]{1,0:T(8,128)(2,1)} %multiply_convert_fusion.1, s32[]{:T(128)S(6)} %select_n.5), kind=kOutput, calls=%fused_computation.20 | convolution fusion | flops 268435456 | bytes 4849668 | tf_op jit(solution)/shard_map/dot_general | solution.py:94
  170.3 12.6 %all-to-all-done.6 = f32[64,9,128]{2,1,0:T(8,128)S(1)} async-done(((f32[64,9,128]{2,1,0:T(8,128)}), f32[64,9,128]{2,1,0:T(8,128)S(1)}, u32[]{:S(2)}, u32[]{:S(2)}) %all-to-all-start.6) | async-done | bytes 294944 | tf_op jit(solution)/shard_map/all_to_all | solution.py:88
  182.9 0.1 reduce_sum.149
  183.0 0.1 fusion.10
  183.1 0.0 copy-done.4
  183.1 0.6 fusion.5
  (11 shorter events, 0.2 us)
Async XLA Ops:
  0.6 95.8 %copy-start = (bf16[2048,512]{1,0:T(8,128)(2,1)S(1)}, bf16[2048,512]{1,0:T(8,128)(2,1)}, u32[]{:S(2)}) copy-start(bf16[2048,512]{1,0:T(8,128)(2,1)} %param.7) | copy-start | bytes 6291460
  46.7 11.9 %copy-start.5 = (bf16[2048,512]{1,0:T(8,128)(2,1)S(1)}, bf16[2048,512]{1,0:T(8,128)(2,1)}, u32[]{:S(2)}) copy-start(bf16[2048,512]{1,0:T(8,128)(2,1)} %param.6) | copy-start | bytes 6291460
  61.5 3.2 %copy-start.1 = (f32[1024,2048]{1,0:T(8,128)}, f32[1024,2048]{1,0:T(8,128)S(1)}, u32[]{:S(2)}) copy-start(f32[1024,2048]{1,0:T(8,128)S(1)} %get-tuple-element.14) | copy-start | bytes 25165828
  66.0 17.2 %all-to-all-start.3 = ((f32[64,8,128]{2,1,0:T(8,128)}), f32[64,8,128]{2,1,0:T(8,128)S(1)}, u32[]{:S(2)}, u32[]{:S(2)}) async-start(f32[64,8,128]{2,1,0:T(8,128)} %broadcast_in_dim.24), calls=%async_computation.3 | async-start | bytes 524288 | tf_op jit(solution)/shard_map/all_to_all | solution.py:30
  83.3 5.8 %copy-start.2 = (f32[1024,2048]{1,0:T(8,128)S(1)}, f32[1024,2048]{1,0:T(8,128)}, u32[]{:S(2)}) copy-start(f32[1024,2048]{1,0:T(8,128)} %copy-done.1) | copy-start | bytes 25165828
  90.4 17.6 %all-to-all-start.4 = ((f32[64,8,128]{2,1,0:T(8,128)}), f32[64,8,128]{2,1,0:T(8,128)S(1)}, u32[]{:S(2)}, u32[]{:S(2)}) async-start(f32[64,8,128]{2,1,0:T(8,128)} %broadcast_in_dim.26), calls=%async_computation.4 | async-start | bytes 524288 | tf_op jit(solution)/shard_map/all_to_all | solution.py:30
  118.9 29.3 %all-to-all-start.5 = ((f32[64,17,128]{2,1,0:T(8,128)}), f32[64,17,128]{2,1,0:T(8,128)}, u32[]{:S(2)}, u32[]{:S(2)}) async-start(f32[64,17,128]{2,1,0:T(8,128)} %broadcast_in_dim.28), calls=%async_computation.5 | async-start | bytes 1572864 | tf_op jit(solution)/shard_map/all_to_all | solution.py:30
  156.4 1.9 %copy-start.3 = (bf16[1024,2048]{1,0:T(8,128)(2,1)}, bf16[1024,2048]{1,0:T(8,128)(2,1)S(1)}, u32[]{:S(2)}) copy-start(bf16[1024,2048]{1,0:T(8,128)(2,1)S(1)} %multiply_convert_fusion) | copy-start | bytes 12582916
  158.4 24.7 %copy-start.4 = (bf16[128,8]{0,1:T(8,128)(2,1)S(1)}, bf16[128,8]{0,1:T(8,128)(2,1)}, u32[]{:S(2)}) copy-start(bf16[128,8]{0,1:T(8,128)(2,1)} %param.5) | copy-start | bytes 6148
  159.9 23.0 %all-to-all-start.6 = ((f32[64,9,128]{2,1,0:T(8,128)}), f32[64,9,128]{2,1,0:T(8,128)S(1)}, u32[]{:S(2)}, u32[]{:S(2)}) async-start(f32[64,9,128]{2,1,0:T(8,128)} %pad_maximum_fusion), calls=%async_computation.6 | async-start | bytes 1048576 | tf_op jit(solution)/shard_map/all_to_all | solution.py:88

commit v3 on v2

v3 whole, which is shorter than its diff:
```python
import jax
import jax.numpy as jnp
import numpy as np
from jax import lax
from jax.experimental import pallas as pl
from jax.experimental.pallas import tpu as pltpu
from jax.sharding import PartitionSpec as P

ITERS = 3
TEACHER_TEMP = 0.07
STUDENT_TEMP = 0.1
BOTH = ("smp", "proto")
PARTS = {"x": 4, "yh": 2, "yl": 4, "z": 8, "c": 2}
B, K, D = 1024, 131072, 512
ROWS = 2048
TILE = 256
BLOCKS = 8
f32, bf16 = jnp.float32, jnp.bfloat16
VMEM = pl.BlockSpec(memory_space=pltpu.VMEM)
SMEM = pl.BlockSpec(memory_space=pltpu.SMEM)
ANY = pl.BlockSpec(memory_space=pl.ANY)


def groups(names):
    order = list(PARTS)
    index = np.arange(512).reshape(tuple(PARTS.values()))
    inner = [order.index(n) for n in names]
    outer = [i for i in range(len(order)) if i not in inner]
    size = int(np.prod([PARTS[n] for n in names]))
    return index.transpose(outer + inner).reshape(-1, size).tolist()


def gathered(x, names):
    group = groups(names)
    copies = jnp.broadcast_to(x[None], (len(group[0]), *x.shape))
    return lax.all_to_all(copies, BOTH, 0, 0, tiled=True, axis_index_groups=group)


def sent_to_protos(x):
    return lax.all_to_all(x, "proto", 0, 0, tiled=True)


def far(x):
    return pltpu.with_memory_space_constraint(x, pltpu.HBM)


def limits():
    return pltpu.CompilerParams(vmem_limit_bytes=24 * 2**20)


def cost(flops=0, moved=0, exps=0):
    return pl.CostEstimate(flops=flops, bytes_accessed=moved, transcendentals=exps)


def call(body, outs, ins, out_specs=None, scratch=(), **work):
    return pl.pallas_call(
        body,
        out_shape=outs,
        in_specs=ins,
        out_specs=out_specs or [VMEM] * len(outs),
        scratch_shapes=scratch,
        compiler_params=limits(),
        cost_estimate=cost(**work),
    )


def streamed(body, outs, ins, out_specs, scratch=(), **work):
    return pl.pallas_call(
        body,
        out_shape=outs,
        grid_spec=pltpu.PrefetchScalarGridSpec(
            num_scalar_prefetch=1,
            grid=(ROWS // TILE,),
            in_specs=ins,
            out_specs=out_specs,
            scratch_shapes=scratch,
        ),
        compiler_params=limits(),
        cost_estimate=cost(**work),
    )


def whole(*dims):
    return pl.BlockSpec(dims, lambda i, me: (0,) * len(dims))


def stripe(width):
    return pl.BlockSpec((TILE, width), lambda i, me: (i, 0))


def features_of(third_ref, x, yh):
    base = pl.multiple_of(yh * 32, 32) if not isinstance(yh, int) else yh * 32
    halves = [third_ref[c, x, pl.ds(base, 32)].astype(f32) for c in range(2)]
    return [
        jnp.stack([h[:, which * 8 : which * 8 + 8] for h in halves], axis=1).reshape(D, 128)
        for which in range(2)
    ]


def unit_columns(values):
    scale = lax.rsqrt(jnp.sum(folded(values * values), axis=0, keepdims=True) + 1e-06)
    return (values * scale).astype(bf16), scale


def folded(total):
    return jnp.sum(total.reshape(-1, 8, total.shape[1]), axis=0)


def as_blocks(wide):
    row = jnp.sum(wide, axis=0, keepdims=True)
    return jnp.concatenate([row[:, s * 128 : (s + 1) * 128] for s in range(BLOCKS)], axis=0)


def as_row(blocks):
    return jnp.concatenate([blocks[s : s + 1, :] for s in range(BLOCKS)], axis=1)


def stage_out(stage_ref, out_ref, sem_ref, i, value):
    slot = lax.rem(i, 2)
    rows = pl.ds(pl.multiple_of(i * TILE, TILE), TILE)
    copy = pltpu.make_async_copy(stage_ref.at[slot], out_ref.at[rows], sem_ref.at[slot])

    @pl.when(i >= 2)
    def _():
        copy.wait()

    stage_ref[slot] = value
    copy.start()


def stage_end(stage_ref, out_ref, sem_ref):
    for slot in range(2):
        rows = pl.ds((ROWS // TILE - 2 + slot) * TILE, TILE)
        pltpu.make_async_copy(stage_ref.at[slot], out_ref.at[rows], sem_ref.at[slot]).wait()


def first_kernel(
    me_ref, third_ref, weight_ref, kernel_out, unit_out, sent_ref, scale_ref, features_ref,
    teacher_ref, student_ref, stage_ref, mass_ref, sem_ref, unit_sem,
):
    for s in range(BLOCKS):
        teacher, student = features_of(third_ref, s // 2, s % 2)
        teacher_ref[:, s * 128 : (s + 1) * 128] = unit_columns(teacher)[0]
        unit, scale = unit_columns(student)
        student_ref[:, s * 128 : (s + 1) * 128] = unit
        scale_ref[s : s + 1, :] = scale
    unit_copy = pltpu.make_async_copy(student_ref, unit_out, unit_sem)
    unit_copy.start()
    me = me_ref[0]
    features_ref[...] = features_of(third_ref, me // 2, lax.rem(me, 2))[1]
    mass_ref[...] = jnp.zeros_like(mass_ref)

    @pl.loop(0, ROWS // TILE)
    def _(i):
        rows = pl.ds(pl.multiple_of(i * TILE, TILE), TILE)
        kernel = jnp.exp(
            jnp.dot(weight_ref[rows, :], teacher_ref[...], preferred_element_type=f32) * (1.0 / TEACHER_TEMP)
        )
        stage_out(stage_ref, kernel_out, sem_ref, i, kernel)
        row_scale = 1.0 / (K * jnp.sum(kernel, axis=1, keepdims=True))
        mass_ref[...] += folded(kernel * row_scale)

    sent_ref[...] = jnp.broadcast_to(as_blocks(mass_ref[...])[None], sent_ref.shape)
    stage_end(stage_ref, kernel_out, sem_ref)
    unit_copy.wait()


def student_kernel(
    me_ref, unit_ref, weight_ref, logits_out, own_ref, total_ref, stage_ref, sum_ref, sem_ref
):
    sum_ref[...] = jnp.zeros_like(sum_ref)
    lanes = pl.ds(pl.multiple_of(me_ref[0] * 128, 128), 128)

    @pl.loop(0, ROWS // TILE)
    def _(i):
        rows = pl.ds(pl.multiple_of(i * TILE, TILE), TILE)
        logits = jnp.dot(weight_ref[rows, :], unit_ref[...], preferred_element_type=f32) * (1.0 / STUDENT_TEMP)
        stage_out(stage_ref, logits_out, sem_ref, i, logits)
        own_ref[rows, :] = stage_ref[lax.rem(i, 2), :, lanes]
        sum_ref[...] += folded(jnp.exp(logits))

    total_ref[...] = as_blocks(sum_ref[...])
    stage_end(stage_ref, logits_out, sem_ref)


def second_kernel(me_ref, got_ref, kernel_ref, total_ref, sent_ref, col_ref, mass_ref):
    i = pl.program_id(0)

    @pl.when(i == 0)
    def _():
        col_ref[...] = as_row(1.0 / (B * jnp.sum(got_ref[...], axis=0)))
        mass_ref[...] = jnp.zeros_like(mass_ref)

    kernel = kernel_ref[...]
    row_scale = 1.0 / (K * jnp.sum(kernel * col_ref[...], axis=1, keepdims=True))
    mass_ref[...] += folded(kernel * row_scale)

    @pl.when(i == ROWS // TILE - 1)
    def _():
        both = jnp.concatenate([as_blocks(mass_ref[...]), total_ref[...]], axis=0)
        sent_ref[...] = jnp.broadcast_to(both[None], sent_ref.shape)


def third_kernel(
    me_ref, got_ref, kernel_ref, scaled_ref, sent_ref, total_ref, col_out, col_ref, mass_ref
):
    i = pl.program_id(0)

    @pl.when(i == 0)
    def _():
        got = jnp.sum(got_ref[...], axis=0)
        total_ref[...] = got[8:, :]
        col = 1.0 / (B * got[:8, :])
        col_out[...] = col
        col_ref[...] = as_row(col)
        mass_ref[...] = jnp.zeros_like(mass_ref)

    kernel = kernel_ref[...]
    row_scale = 1.0 / (K * jnp.sum(kernel * col_ref[...], axis=1, keepdims=True))
    lanes = pl.ds(pl.multiple_of(me_ref[0] * 128, 128), 128)
    scaled_ref[...] = kernel_ref[:, lanes] * row_scale
    mass_ref[...] += folded(kernel * row_scale)

    @pl.when(i == ROWS // TILE - 1)
    def _():
        sent_ref[...] = jnp.broadcast_to(as_blocks(mass_ref[...])[None], sent_ref.shape)


def split_rows(value):
    high = value.astype(bf16).astype(f32)
    middle = (value - high).astype(bf16).astype(f32)
    return [high, middle, value - high - middle]


def own_kernel(
    me_ref, got_ref, scaled_ref, logits_ref, total_ref, features_ref, weight_ref, sent_ref, col_ref, grad_ref
):
    me = me_ref[0]
    col_ref[...] = 1.0 / (B * jnp.sum(got_ref[...], axis=0))
    own_col = col_ref[pl.ds(me, 1), :] * B
    own_total = 1.0 / total_ref[pl.ds(me, 1), :]
    logits = logits_ref[...]
    targets = scaled_ref[...] * own_col
    weighted = jnp.sum(folded(targets * logits), axis=0, keepdims=True)
    grad_ref[...] = ((jnp.exp(logits) * own_total - targets) * (1.0 / (B * STUDENT_TEMP))).astype(bf16)
    unit_part = lax.dot_general(
        grad_ref[...], weight_ref[...], (((0,), (0,)), ((), ())), preferred_element_type=f32
    ).T
    inner = jnp.sum(folded(features_ref[...] * unit_part), axis=0, keepdims=True)
    extra = jnp.concatenate(split_rows(inner) + split_rows(weighted) + [jnp.zeros((2, 128), f32)], axis=0)
    pieces = unit_part.reshape(64, 8, 128)
    sent_ref[...] = jnp.concatenate(
        [pieces, jnp.broadcast_to(extra[None], (64, 8, 128))], axis=1
    ).astype(bf16)


def weight_kernel(
    me_ref, kernel_ref, logits_ref, total_ref, before_ref, col_ref, unit_ref, out_ref, rows_ref
):
    @pl.when(pl.program_id(0) == 0)
    def _():
        rows_ref[0:1, :] = as_row(before_ref[...])
        rows_ref[1:2, :] = as_row(col_ref[...] * B)
        rows_ref[2:3, :] = as_row(1.0 / total_ref[...])

    kernel = kernel_ref[...]
    row_scale = 1.0 / (K * jnp.sum(kernel * rows_ref[0:1, :], axis=1, keepdims=True))
    targets = kernel * row_scale * rows_ref[1:2, :]
    probs = jnp.exp(logits_ref[...]) * rows_ref[2:3, :]
    grad = ((probs - targets) * (1.0 / (B * STUDENT_TEMP))).astype(bf16)
    out_ref[...] = lax.dot_general(unit_ref[...], grad, (((1,), (1,)), ((), ())), preferred_element_type=f32)


def final_kernel(me_ref, got_ref, features_ref, scale_ref, total_ref, features_out, loss_out):
    me = me_ref[0]
    got = jnp.sum(got_ref[...].astype(f32), axis=0)
    inner = got[8:9] + got[9:10] + got[10:11]
    weighted = got[11:12] + got[12:13] + got[13:14]
    scale = scale_ref[pl.ds(me, 1), :]
    features_out[...] = scale * got[:8] - (scale * scale * scale * inner) * features_ref[...].astype(f32)
    loss_out[...] = jnp.log(total_ref[pl.ds(me, 1), :]) - weighted


def shape(dims, dtype=f32):
    return jax.ShapeDtypeStruct(dims, dtype)


def on_device(teacher_features, student_features, teacher_weight, student_weight):
    me = lax.axis_index("smp").astype(jnp.int32).reshape(1)
    raw = jnp.concatenate([teacher_features.T, student_features.T], axis=0)
    first = gathered(raw, ("yh", "yl", "z"))
    second = gathered(first, ("x",))
    third = gathered(second, ("c",))

    pair = pltpu.SemaphoreType.DMA((2,))
    stage = pltpu.VMEM((2, TILE, B), f32)
    row, rows8 = pltpu.VMEM((1, B), f32), pltpu.VMEM((8, B), f32)
    matmul = dict(flops=2 * ROWS * B * D, moved=12 * 2**20, exps=ROWS * B)
    kernel, student_unit, sent_1, student_scale, features_own = call(
        first_kernel,
        [pltpu.HBM((ROWS, B), f32), pltpu.HBM((D, B), bf16), shape((64, 8, 128)), shape((8, 128)), shape((D, 128))],
        [SMEM, VMEM, VMEM],
        [ANY, ANY, VMEM, VMEM, VMEM],
        [pltpu.VMEM((D, B), bf16), pltpu.VMEM((D, B), bf16), stage, rows8, pair, pltpu.SemaphoreType.DMA],
        **matmul,
    )(me, third, teacher_weight)
    got_1 = sent_to_protos(sent_1)
    logits, logits_own, local_total = call(
        student_kernel,
        [pltpu.HBM((ROWS, B), f32), shape((ROWS, 128)), shape((8, 128))],
        [SMEM, VMEM, VMEM],
        [ANY, VMEM, VMEM],
        [stage, rows8, pair],
        **matmul,
    )(me, student_unit, student_weight)
    (sent_2,) = streamed(
        second_kernel,
        [shape((64, 16, 128))],
        [whole(64, 8, 128), stripe(B), whole(8, 128)],
        [whole(64, 16, 128)],
        [row, rows8],
        flops=4 * ROWS * B,
        moved=8 * 2**20,
    )(me, got_1, far(kernel), local_total)
    got_2 = sent_to_protos(sent_2)
    scaled_own, sent_3, total, col_before = streamed(
        third_kernel,
        [shape((ROWS, 128)), shape((64, 8, 128)), shape((8, 128)), shape((8, 128))],
        [whole(64, 16, 128), stripe(B)],
        [stripe(128), whole(64, 8, 128), whole(8, 128), whole(8, 128)],
        [row, rows8],
        flops=4 * ROWS * B,
        moved=8 * 2**20,
    )(me, got_2, far(kernel))
    got_3 = sent_to_protos(sent_3)
    sent_4, col_scale = call(
        own_kernel,
        [shape((64, 16, 128), bf16), shape((8, 128))],
        [SMEM] + [VMEM] * 6,
        None,
        [pltpu.VMEM((ROWS, 128), bf16)],
        flops=2 * ROWS * 128 * D,
        moved=4 * 2**20,
        exps=ROWS * 128,
    )(me, got_3, scaled_own, logits_own, total, features_own, student_weight)
    got_4 = sent_to_protos(sent_4)
    (grad_weight,) = streamed(
        weight_kernel,
        [shape((64, ROWS))],
        [stripe(B), stripe(B), whole(8, 128), whole(8, 128), whole(8, 128),
         pl.BlockSpec((64, B), lambda i, me: (me[0], 0))],
        [pl.BlockSpec((64, TILE), lambda i, me: (0, i))],
        [rows8],
        flops=2 * ROWS * B * 64,
        moved=17 * 2**20,
        exps=ROWS * B,
    )(me, far(kernel), far(logits), total, col_before, col_scale, student_unit)
    grad_features, loss = call(
        final_kernel, [shape((8, 128)), shape((1, 128))], [SMEM] + [VMEM] * 4
    )(me, got_4, student_features.T, student_scale, total)
    return loss.reshape(128), grad_features.T, grad_weight.T


def solution(mesh):
    placed = (P("smp", "proto"), P("smp", "proto"), P("proto", None), P("proto", None))
    return jax.shard_map(
        on_device,
        mesh=mesh,
        in_specs=placed,
        out_specs=(P("smp"), P("smp", "proto"), P("proto", "smp")),
        check_vma=False,
    )
```

time: 184 us -> 158 us (0.86)
  Pallas kernels: 0 us -> 38.6 us
  waiting for transfers between devices: 48.8 us -> 16 us
  other arithmetic: 29.7 us -> 0.7 us
  blocking collectives: 54.5 us -> 81.6 us
  matrix products: 14.4 us -> 0 us
  starting transfers between devices: 23.8 us -> 15.6 us
  local copies, waits for them, and re-layouts: 11.6 us -> 4.36 us
    all_to_all x0 -> x2, blocking collectives: none -> 42 us  [sent_to_protos(): return lax.all_to_all(x, 'proto', 0, 0, tiled=True)]
    pallas_call x0 -> x7, Pallas kernels: none -> 38.6 us  [the longest x1 9.98 us: on_device(): streamed(weight_kernel, [shape((64, ROWS))], [stripe(B), stripe(B), whole...]
    all_to_all x4 -> x3, waiting for transfers between devices: 48.8 us -> 16 us  [the longest x1 11.2 us: gathered(): lax.all_to_all(copies, BOTH, 0, 0, tiled=True, axis_index_groups=group)]
    reduce_sum x11 -> x0, other arithmetic: 16.9 us -> none  [the longest x2 8.16 us: on_device(): row_scale = 1.0 / (protos * jnp.sum(kernel * col_scale[None, :], axis=1))]
    all_to_all x3 -> x2, blocking collectives: 54.5 us -> 39.6 us  [gathered(): lax.all_to_all(copies, BOTH, 0, 0, tiled=True, axis_index_groups=group)]
    dot_general x4 -> x0, matrix products: 14.4 us -> none  [the longest x1 7.06 us: on_device(): jnp.dot(student_weight, student_unit, preferred_element_type=f32)]
    convert_element_type x3 -> x0, other arithmetic: 9.76 us -> none  [the longest x1 7 us: on_device(): ((expo / total[None, :] - targets) / (samples * STUDENT_TEMP)).astype(bf16)]
    all_to_all x4 -> x3, starting transfers between devices: 23.8 us -> 15.6 us  [the longest x2 11.6 us: sent_to_protos(): return lax.all_to_all(x, 'proto', 0, 0, tiled=True)]
  transfers between devices with their start and end apart: 4 -> 3, of which waited for: 4 -> 3; matrix products, arithmetic and copies ran while one was open for 8% -> 0% of each run, Pallas kernels for 0% -> 10%
where the time goes in v3:
time: 158 us
  blocking collectives  81.6 us (52%)
  Pallas kernels  38.6 us (24%)
  waiting for transfers between devices  16 us (10%)
  starting transfers between devices  15.6 us (10%)
  local copies, waits for them, and re-layouts  4.36 us (3%)
    all_to_all x2, blocking collectives, sent_to_protos(): return lax.all_to_all(x, 'proto', 0, 0, tiled=True)  42 us
    all_to_all x2, blocking collectives, gathered(): lax.all_to_all(copies, BOTH, 0, 0, tiled=True, axis_index_groups=group)  39.6 us
    all_to_all x2, starting transfers between devices, sent_to_protos(): return lax.all_to_all(x, 'proto', 0, 0, tiled=True)  11.6 us
    all_to_all x1, waiting for transfers between devices, gathered(): lax.all_to_all(copies, BOTH, 0, 0, tiled=True, axis_index_groups=group)  11.2 us
    pallas_call x1, Pallas kernels, on_device(): streamed(weight_kernel, [shape((64, ROWS))], [stripe(B), stripe(B), whole...  9.98 us
    pallas_call x1, Pallas kernels, on_device(): call(first_kernel, [pltpu.HBM((ROWS, B), f32), pltpu.HBM((D, B), bf16), s...  8.19 us
    pallas_call x1, Pallas kernels, on_device(): streamed(third_kernel, [shape((ROWS, 128)), shape((64, 8, 128)), shape((8...  6.42 us
    pallas_call x1, Pallas kernels, on_device(): streamed(second_kernel, [shape((64, 16, 128))], [whole(64, 8, 128), strip...  6.27 us
  transfers between devices with their start and end apart: 3, of which 3 were waited for; matrix products, arithmetic and copies ran while one was open for 0% of the time, Pallas kernels for 10%

profile of v3, /device:TPU:1, one launch (start us, length us, event | category | flops | bytes accessed | tf_op | source)
XLA Modules:
  0.0 157.6 jit_solution(3926996558041076993)
XLA Ops:
  0.6 0.7 pad_maximum_fusion
  1.4 29.5 %all_to_all.35 = bf16[64,16,128]{2,1,0:T(8,128)(2,1)S(1)} all-to-all(bf16[64,16,128]{2,1,0:T(8,128)(2,1)S(1)} %broadcast_in_dim.6), channel_id=1, replica_groups={{0,2,4,6,8,10,12,14,16,18,20,22,24,26,28,30,32,34,36,38,40,42,44,46,48,..., dimensions={0} | all-to-all | bytes 524288 | tf_op jit(solution)/shard_map/all_to_all | solution.py:36
  30.9 1.1 broadcast_in_dim.7
  32.0 4.0 %all-to-all-start.1 = ((bf16[4,64,16,128]{3,2,1,0:T(8,128)(2,1)}), bf16[4,64,16,128]{3,2,1,0:T(8,128)(2,1)S(1)}, u32[]{:S(2)}, u32[]{:S(2)}) async-start(bf16[4,64,16,128]{3,2,1,0:T(8,128)(2,1)} %broadcast_in_dim.7), calls=%async_computation.1 | async-start | bytes 2097152 | tf_op jit(solution)/shard_map/all_to_all | solution.py:36
  36.0 11.2 %all-to-all-done.1 = bf16[4,64,16,128]{3,2,1,0:T(8,128)(2,1)S(1)} async-done(((bf16[4,64,16,128]{3,2,1,0:T(8,128)(2,1)}), bf16[4,64,16,128]{3,2,1,0:T(8,128)(2,1)S(1)}, u32[]{:S(2)}, u32[]{:S(2)}) %all-to-all-start.1) | async-done | bytes 1048608 | tf_op jit(solution)/shard_map/all_to_all | solution.py:36
  47.2 0.3 broadcast_in_dim.8
  47.4 0.0 copy-start.7
  47.4 10.1 %all_to_all.36.third_ref = bf16[2,4,64,16,128]{4,3,2,1,0:T(8,128)(2,1)S(1)} all-to-all(bf16[2,4,64,16,128]{4,3,2,1,0:T(8,128)(2,1)S(1)} %broadcast_in_dim.8), channel_id=1, replica_groups={{0,1},{2,3},{4,5},{6,7},{8,9},{10,11},{12,13},{14,15},{16,17},{18,19},{..., dimensions={0} | all-to-all | bytes 4194304 | tf_op jit(solution)/shard_map/all_to_all | solution.py:36
  57.5 0.0 copy-done.7
  57.5 0.0 copy-start
  57.5 8.2 %shard_map.67 = (f32[2048,1024]{1,0:T(8,128)}, bf16[512,1024]{1,0:T(8,128)(2,1)}, f32[64,8,128]{2,1,0:T(8,128)}, f32[8,128]{1,0:T(8,128)S(1)}, f32[512,128]{1,0:T(8,128)S(1)}) custom-call(s32[1]{0:T(128)} %bitcast.me_ref, bf16[2,4,64,16,128]{4,3,2,1,0:T(8,128)(2,1)S(1)} %all_to_all.36.third_ref, bf16[2048,512]{1,0:T(8,128)(2,1)S(1)} %copy-done.7), custom_call_target="tpu_custom_call" | custom-call | flops 2147483648 | bytes 12582912 | tf_op jit(solution)/shard_map/pallas_call | solution.py:299
  65.7 5.6 %all-to-all-start.3 = ((f32[64,8,128]{2,1,0:T(8,128)}), f32[64,8,128]{2,1,0:T(8,128)S(1)}, u32[]{:S(2)}, u32[]{:S(2)}) async-start(f32[64,8,128]{2,1,0:T(8,128)} %get-tuple-element.19), calls=%async_computation.3 | async-start | bytes 524288 | tf_op jit(solution)/shard_map/all_to_all | solution.py:40
  71.3 0.0 copy-done
  71.3 0.0 copy-start.1
  71.3 1.2 copy-done.1
  72.5 6.2 %shard_map.68 = (f32[2048,1024]{1,0:T(8,128)}, f32[2048,128]{1,0:T(8,128)S(1)}, f32[8,128]{1,0:T(8,128)S(1)}) custom-call(s32[1]{0:T(128)} %bitcast.me_ref, bf16[512,1024]{1,0:T(8,128)(2,1)S(1)} %copy-done.1, bf16[2048,512]{1,0:T(8,128)(2,1)S(1)} %copy-done), custom_call_target="tpu_custom_call" | custom-call | flops 2147483648 | bytes 12582912 | tf_op jit(solution)/shard_map/pallas_call | solution.py:308
  78.8 0.0 copy-start.3
  78.8 1.0 copy-done.3
  79.8 3.2 %all-to-all-done.3.got_ref = f32[64,8,128]{2,1,0:T(8,128)S(1)} async-done(((f32[64,8,128]{2,1,0:T(8,128)}), f32[64,8,128]{2,1,0:T(8,128)S(1)}, u32[]{:S(2)}, u32[]{:S(2)}) %all-to-all-start.3) | async-done | bytes 262176 | tf_op jit(solution)/shard_map/all_to_all | solution.py:40
  82.9 6.3 %shard_map.69 = f32[64,16,128]{2,1,0:T(8,128)S(1)} custom-call(s32[1]{0:T(128)} %bitcast.me_ref, f32[64,8,128]{2,1,0:T(8,128)S(1)} %all-to-all-done.3.got_ref, f32[2048,1024]{1,0:T(8,128)} %get-tuple-element.20.kernel_ref, f32[8,128]{1,0:T(8,128)S(1)} %get-tuple-element.22.total_ref), custom_call_target="tpu_custom_call" | custom-call | flops 8388608 | bytes 8388608 | tf_op jit(solution)/shard_map/pallas_call | solution.py:316
  89.2 24.5 %all_to_all.37.got_ref = f32[64,16,128]{2,1,0:T(8,128)S(1)} all-to-all(f32[64,16,128]{2,1,0:T(8,128)S(1)} %shard_map.69), channel_id=1, replica_groups=mesh['smp'=8,'proto'=64] {'proto'}, dimensions={0} | all-to-all | bytes 1048576 | tf_op jit(solution)/shard_map/all_to_all | solution.py:40
  113.7 0.0 copy-start.4
  113.8 6.4 %shard_map.70 = (f32[2048,128]{1,0:T(8,128)S(1)}, f32[64,8,128]{2,1,0:T(8,128)S(1)}, f32[8,128]{1,0:T(8,128)S(1)}, f32[8,128]{1,0:T(8,128)S(1)}) custom-call(s32[1]{0:T(128)} %bitcast.me_ref, f32[64,16,128]{2,1,0:T(8,128)S(1)} %all_to_all.37.got_ref, f32[2048,1024]{1,0:T(8,128)} %get-tuple-element.20.kernel_ref), custom_call_target="tpu_custom_call" | custom-call | flops 8388608 | bytes 8388608 | tf_op jit(solution)/shard_map/pallas_call | solution.py:326
  120.2 17.5 %all_to_all.38.got_ref = f32[64,8,128]{2,1,0:T(8,128)S(1)} all-to-all(f32[64,8,128]{2,1,0:T(8,128)S(1)} %get-tuple-element.23), channel_id=1, replica_groups=mesh['smp'=8,'proto'=64] {'proto'}, dimensions={0} | all-to-all | bytes 524288 | tf_op jit(solution)/shard_map/all_to_all | solution.py:40
  137.7 0.0 copy-done.4
  137.7 0.0 copy-start.2
  137.7 0.9 shard_map.71
  138.6 0.0 copy-start.5
  138.6 0.7 copy-done.5
  139.3 6.0 %all-to-all-start.6 = ((bf16[64,16,128]{2,1,0:T(8,128)(2,1)}), bf16[64,16,128]{2,1,0:T(8,128)(2,1)S(1)}, u32[]{:S(2)}, u32[]{:S(2)}) async-start(bf16[64,16,128]{2,1,0:T(8,128)(2,1)} %copy-done.5), calls=%async_computation.6 | async-start | bytes 524288 | tf_op jit(solution)/shard_map/all_to_all | solution.py:40
  145.3 0.0 copy-done.2
  145.3 0.0 copy-start.6
  145.3 10.0 %shard_map.73 = f32[64,2048]{1,0:T(8,128)} custom-call(s32[1]{0:T(128)} %bitcast.me_ref, f32[2048,1024]{1,0:T(8,128)} %get-tuple-element.20.kernel_ref, f32[2048,1024]{1,0:T(8,128)} %get-tuple-element.32.logits_ref, f32[8,128]{1,0:T(8,128)S(1)} %get-tuple-element.26.total_ref, f32[8,128]{1,0:T(8,128)S(1)} %get-tuple-element.33.before_ref, ...), custom_call_target="tpu_custom_call" | custom-call | flops 268435456 | bytes 17825792 | tf_op jit(solution)/shard_map/pallas_call | solution.py:347
  155.3 1.6 %all-to-all-done.6.got_ref = bf16[64,16,128]{2,1,0:T(8,128)(2,1)S(1)} async-done(((bf16[64,16,128]{2,1,0:T(8,128)(2,1)}), bf16[64,16,128]{2,1,0:T(8,128)(2,1)S(1)}, u32[]{:S(2)}, u32[]{:S(2)}) %all-to-all-start.6) | async-done | bytes 262176 | tf_op jit(solution)/shard_map/all_to_all | solution.py:40
  156.9 0.0 copy-done.6
  156.9 0.7 shard_map.72
  (1 shorter events, 0.0 us)
Async XLA Ops:
  32.0 15.2 %all-to-all-start.1 = ((bf16[4,64,16,128]{3,2,1,0:T(8,128)(2,1)}), bf16[4,64,16,128]{3,2,1,0:T(8,128)(2,1)S(1)}, u32[]{:S(2)}, u32[]{:S(2)}) async-start(bf16[4,64,16,128]{3,2,1,0:T(8,128)(2,1)} %broadcast_in_dim.7), calls=%async_computation.1 | async-start | bytes 2097152 | tf_op jit(solution)/shard_map/all_to_all | solution.py:36
  47.4 10.1 %copy-start.7 = (bf16[2048,512]{1,0:T(8,128)(2,1)S(1)}, bf16[2048,512]{1,0:T(8,128)(2,1)}, u32[]{:S(2)}) copy-start(bf16[2048,512]{1,0:T(8,128)(2,1)} %weight_ref.3) | copy-start | bytes 6291460
  57.5 13.8 %copy-start = (bf16[2048,512]{1,0:T(8,128)(2,1)S(1)}, bf16[2048,512]{1,0:T(8,128)(2,1)}, u32[]{:S(2)}) copy-start(bf16[2048,512]{1,0:T(8,128)(2,1)} %weight_ref.5) | copy-start | bytes 6291460
  65.7 17.2 %all-to-all-start.3 = ((f32[64,8,128]{2,1,0:T(8,128)}), f32[64,8,128]{2,1,0:T(8,128)S(1)}, u32[]{:S(2)}, u32[]{:S(2)}) async-start(f32[64,8,128]{2,1,0:T(8,128)} %get-tuple-element.19), calls=%async_computation.3 | async-start | bytes 524288 | tf_op jit(solution)/shard_map/all_to_all | solution.py:40
  71.3 1.2 copy-start.1
  78.8 1.0 copy-start.3
  113.7 24.0 %copy-start.4 = (f32[2048,128]{1,0:T(8,128)S(1)}, f32[2048,128]{1,0:T(8,128)}, u32[]{:S(2)}) copy-start(f32[2048,128]{1,0:T(8,128)} %copy-done.3) | copy-start | bytes 3145732
  137.7 7.6 %copy-start.2 = (bf16[512,1024]{1,0:T(8,128)(2,1)S(1)}, bf16[512,1024]{1,0:T(8,128)(2,1)}, u32[]{:S(2)}) copy-start(bf16[512,1024]{1,0:T(8,128)(2,1)} %get-tuple-element.21.unit_ref) | copy-start | bytes 3145732
  138.6 0.7 copy-start.5
  139.3 17.7 %all-to-all-start.6 = ((bf16[64,16,128]{2,1,0:T(8,128)(2,1)}), bf16[64,16,128]{2,1,0:T(8,128)(2,1)S(1)}, u32[]{:S(2)}, u32[]{:S(2)}) async-start(bf16[64,16,128]{2,1,0:T(8,128)(2,1)} %copy-done.5), calls=%async_computation.6 | async-start | bytes 524288 | tf_op jit(solution)/shard_map/all_to_all | solution.py:40
  145.3 11.6 %copy-start.6 = (bf16[128,8]{0,1:T(8,128)(2,1)S(1)}, bf16[128,8]{0,1:T(8,128)(2,1)}, u32[]{:S(2)}) copy-start(bf16[128,8]{0,1:T(8,128)(2,1)} %param.5) | copy-start | bytes 6148

commit v4 on v3

--- a/solution.py
+++ b/solution.py
@@ -14,6 +14,7 @@
 B, K, D = 1024, 131072, 512
 ROWS = 2048
 TILE = 256
+WIDE = 512
 BLOCKS = 8
 f32, bf16 = jnp.float32, jnp.bfloat16
 VMEM = pl.BlockSpec(memory_space=pltpu.VMEM)
@@ -150,18 +151,24 @@
     features_ref[...] = features_of(third_ref, me // 2, lax.rem(me, 2))[1]
     mass_ref[...] = jnp.zeros_like(mass_ref)
 
-    @pl.loop(0, ROWS // TILE)
+    def copy_out(i):
+        rows = pl.ds(pl.multiple_of(i * WIDE, WIDE), WIDE)
+        return pltpu.make_async_copy(stage_ref.at[rows], kernel_out.at[rows], sem_ref.at[i])
+
+    @pl.loop(0, ROWS // WIDE)
     def _(i):
-        rows = pl.ds(pl.multiple_of(i * TILE, TILE), TILE)
+        rows = pl.ds(pl.multiple_of(i * WIDE, WIDE), WIDE)
         kernel = jnp.exp(
             jnp.dot(weight_ref[rows, :], teacher_ref[...], preferred_element_type=f32) * (1.0 / TEACHER_TEMP)
         )
-        stage_out(stage_ref, kernel_out, sem_ref, i, kernel)
+        stage_ref[rows, :] = kernel
+        copy_out(i).start()
         row_scale = 1.0 / (K * jnp.sum(kernel, axis=1, keepdims=True))
         mass_ref[...] += folded(kernel * row_scale)
 
-    sent_ref[...] = jnp.broadcast_to(as_blocks(mass_ref[...])[None], sent_ref.shape)
-    stage_end(stage_ref, kernel_out, sem_ref)
+    sent_ref[...] = jnp.broadcast_to(as_blocks(mass_ref[...]).astype(bf16)[None], sent_ref.shape)
+    for i in range(ROWS // WIDE):
+        copy_out(i).wait()
     unit_copy.wait()
 
 
@@ -183,47 +190,57 @@
     stage_end(stage_ref, logits_out, sem_ref)
 
 
-def second_kernel(me_ref, got_ref, kernel_ref, total_ref, sent_ref, col_ref, mass_ref):
-    i = pl.program_id(0)
-
-    @pl.when(i == 0)
-    def _():
-        col_ref[...] = as_row(1.0 / (B * jnp.sum(got_ref[...], axis=0)))
-        mass_ref[...] = jnp.zeros_like(mass_ref)
-
-    kernel = kernel_ref[...]
-    row_scale = 1.0 / (K * jnp.sum(kernel * col_ref[...], axis=1, keepdims=True))
-    mass_ref[...] += folded(kernel * row_scale)
-
-    @pl.when(i == ROWS // TILE - 1)
-    def _():
-        both = jnp.concatenate([as_blocks(mass_ref[...]), total_ref[...]], axis=0)
-        sent_ref[...] = jnp.broadcast_to(both[None], sent_ref.shape)
+def received(got_ref):
+    return jnp.sum(got_ref[...].astype(f32), axis=0)
+
+
+def second_kernel(got_ref, far_ref, total_ref, kernel_ref, sent_ref, kept_ref, col_ref, mass_ref, sem_ref):
+    def copy_in(i):
+        rows = pl.ds(pl.multiple_of(i * TILE, TILE), TILE)
+        return pltpu.make_async_copy(far_ref.at[rows], kernel_ref.at[rows], sem_ref.at[i])
+
+    for i in range(ROWS // TILE):
+        copy_in(i).start()
+    col_ref[...] = as_row(1.0 / (B * received(got_ref)))
+    mass_ref[...] = jnp.zeros_like(mass_ref)
+
+    @pl.loop(0, ROWS // TILE)
+    def _(i):
+        copy_in(i).wait()
+        kernel = kernel_ref[pl.ds(pl.multiple_of(i * TILE, TILE), TILE), :]
+        row_scale = 1.0 / (K * jnp.sum(kernel * col_ref[...], axis=1, keepdims=True))
+        mass_ref[...] += folded(kernel * row_scale)
+
+    mass = as_blocks(mass_ref[...]).astype(bf16).astype(f32)
+    kept_ref[...] = mass
+    total = total_ref[...]
+    high = total.astype(bf16).astype(f32)
+    packed = jnp.concatenate([mass, high, total - high], axis=0).astype(bf16)
+    sent_ref[...] = jnp.broadcast_to(packed[None], sent_ref.shape)
 
 
 def third_kernel(
-    me_ref, got_ref, kernel_ref, scaled_ref, sent_ref, total_ref, col_out, col_ref, mass_ref
-):
-    i = pl.program_id(0)
-
-    @pl.when(i == 0)
-    def _():
-        got = jnp.sum(got_ref[...], axis=0)
-        total_ref[...] = got[8:, :]
-        col = 1.0 / (B * got[:8, :])
-        col_out[...] = col
-        col_ref[...] = as_row(col)
-        mass_ref[...] = jnp.zeros_like(mass_ref)
-
-    kernel = kernel_ref[...]
-    row_scale = 1.0 / (K * jnp.sum(kernel * col_ref[...], axis=1, keepdims=True))
+    me_ref, got_ref, kernel_ref, kept_ref, scaled_ref, sent_ref, total_ref, col_out, before_ref, col_ref, mass_ref
+):
+    got = received(got_ref)
+    before_ref[...] = got[:8, :]
+    total_ref[...] = got[8:16, :] + got[16:, :]
+    col = 1.0 / (B * got[:8, :])
+    col_out[...] = col
+    col_ref[...] = as_row(col)
+    mass_ref[...] = jnp.zeros_like(mass_ref)
     lanes = pl.ds(pl.multiple_of(me_ref[0] * 128, 128), 128)
-    scaled_ref[...] = kernel_ref[:, lanes] * row_scale
-    mass_ref[...] += folded(kernel * row_scale)
-
-    @pl.when(i == ROWS // TILE - 1)
-    def _():
-        sent_ref[...] = jnp.broadcast_to(as_blocks(mass_ref[...])[None], sent_ref.shape)
+
+    @pl.loop(0, ROWS // TILE)
+    def _(i):
+        rows = pl.ds(pl.multiple_of(i * TILE, TILE), TILE)
+        kernel = kernel_ref[rows, :]
+        row_scale = 1.0 / (K * jnp.sum(kernel * col_ref[...], axis=1, keepdims=True))
+        scaled_ref[rows, :] = kernel_ref[rows, lanes] * row_scale
+        mass_ref[...] += folded(kernel * row_scale)
+
+    change = as_blocks(mass_ref[...]) - kept_ref[...]
+    sent_ref[...] = jnp.broadcast_to(change.astype(bf16)[None], sent_ref.shape)
 
 
 def split_rows(value):
@@ -233,10 +250,11 @@
 
 
 def own_kernel(
-    me_ref, got_ref, scaled_ref, logits_ref, total_ref, features_ref, weight_ref, sent_ref, col_ref, grad_ref
+    me_ref, got_ref, before_ref, scaled_ref, logits_ref, total_ref, features_ref, weight_ref, sent_ref, col_ref,
+    grad_ref,
 ):
     me = me_ref[0]
-    col_ref[...] = 1.0 / (B * jnp.sum(got_ref[...], axis=0))
+    col_ref[...] = 1.0 / (B * (before_ref[...] + received(got_ref)))
     own_col = col_ref[pl.ds(me, 1), :] * B
     own_total = 1.0 / total_ref[pl.ds(me, 1), :]
     logits = logits_ref[...]
@@ -273,7 +291,7 @@
 
 def final_kernel(me_ref, got_ref, features_ref, scale_ref, total_ref, features_out, loss_out):
     me = me_ref[0]
-    got = jnp.sum(got_ref[...].astype(f32), axis=0)
+    got = received(got_ref)
     inner = got[8:9] + got[9:10] + got[10:11]
     weighted = got[11:12] + got[12:13] + got[13:14]
     scale = scale_ref[pl.ds(me, 1), :]
@@ -298,10 +316,11 @@
     matmul = dict(flops=2 * ROWS * B * D, moved=12 * 2**20, exps=ROWS * B)
     kernel, student_unit, sent_1, student_scale, features_own = call(
         first_kernel,
-        [pltpu.HBM((ROWS, B), f32), pltpu.HBM((D, B), bf16), shape((64, 8, 128)), shape((8, 128)), shape((D, 128))],
+        [pltpu.HBM((ROWS, B), f32), pltpu.HBM((D, B), bf16), shape((64, 8, 128), bf16), shape((8, 128)), shape((D, 128))],
         [SMEM, VMEM, VMEM],
         [ANY, ANY, VMEM, VMEM, VMEM],
-        [pltpu.VMEM((D, B), bf16), pltpu.VMEM((D, B), bf16), stage, rows8, pair, pltpu.SemaphoreType.DMA],
+        [pltpu.VMEM((D, B), bf16), pltpu.VMEM((D, B), bf16), pltpu.VMEM((ROWS, B), f32), rows8,
+         pltpu.SemaphoreType.DMA((ROWS // WIDE,)), pltpu.SemaphoreType.DMA],
         **matmul,
     )(me, third, teacher_weight)
     got_1 = sent_to_protos(sent_1)
@@ -313,36 +332,36 @@
         [stage, rows8, pair],
         **matmul,
     )(me, student_unit, student_weight)
-    (sent_2,) = streamed(
+    kernel_near, sent_2, kept = call(
         second_kernel,
-        [shape((64, 16, 128))],
-        [whole(64, 8, 128), stripe(B), whole(8, 128)],
-        [whole(64, 16, 128)],
+        [pltpu.VMEM((ROWS, B), f32), shape((64, 24, 128), bf16), shape((8, 128))],
+        [VMEM, ANY, VMEM],
+        None,
+        [row, rows8, pltpu.SemaphoreType.DMA((ROWS // TILE,))],
+        flops=4 * ROWS * B,
+        moved=8 * 2**20,
+    )(got_1, far(kernel), local_total)
+    got_2 = sent_to_protos(sent_2)
+    scaled_own, sent_3, total, col_before, before = call(
+        third_kernel,
+        [shape((ROWS, 128)), shape((64, 8, 128), bf16), shape((8, 128)), shape((8, 128)), shape((8, 128))],
+        [SMEM, VMEM, VMEM, VMEM],
+        None,
         [row, rows8],
         flops=4 * ROWS * B,
         moved=8 * 2**20,
-    )(me, got_1, far(kernel), local_total)
-    got_2 = sent_to_protos(sent_2)
-    scaled_own, sent_3, total, col_before = streamed(
-        third_kernel,
-        [shape((ROWS, 128)), shape((64, 8, 128)), shape((8, 128)), shape((8, 128))],
-        [whole(64, 16, 128), stripe(B)],
-        [stripe(128), whole(64, 8, 128), whole(8, 128), whole(8, 128)],
-        [row, rows8],
-        flops=4 * ROWS * B,
-        moved=8 * 2**20,
-    )(me, got_2, far(kernel))
+    )(me, got_2, kernel_near, kept)
     got_3 = sent_to_protos(sent_3)
     sent_4, col_scale = call(
         own_kernel,
         [shape((64, 16, 128), bf16), shape((8, 128))],
-        [SMEM] + [VMEM] * 6,
+        [SMEM] + [VMEM] * 7,
         None,
         [pltpu.VMEM((ROWS, 128), bf16)],
         flops=2 * ROWS * 128 * D,
         moved=4 * 2**20,
         exps=ROWS * 128,
-    )(me, got_3, scaled_own, logits_own, total, features_own, student_weight)
+    )(me, got_3, before, scaled_own, logits_own, total, features_own, student_weight)
     got_4 = sent_to_protos(sent_4)
     (grad_weight,) = streamed(
         weight_kernel,

time: 158 us -> 144 us (0.911)
  Pallas kernels: 38.6 us -> 29.7 us
  blocking collectives: 81.6 us -> 78.8 us
  waiting for transfers between devices: 16 us -> 14.4 us
    pallas_call x2, Pallas kernels: 12.7 us -> 5.24 us  [the longest x1 3.68 us: on_device(): call(second_kernel, [pltpu.VMEM((ROWS, B), f32), shape((64, 24, 128), bf1...]
    all_to_all x2, blocking collectives: 42 us -> 39.2 us  [sent_to_protos(): return lax.all_to_all(x, 'proto', 0, 0, tiled=True)]
  transfers between devices with their start and end apart: 3 -> 3, of which waited for: 3 -> 3; matrix products, arithmetic and copies ran while one was open for 0% -> 0% of each run, Pallas kernels for 10% -> 11%
where the time goes in v4:
time: 144 us; the launch traced here: 143 us
  blocking collectives  78.8 us (55%)
  Pallas kernels  29.7 us (21%)
  starting transfers between devices  14.6 us (10%)
  waiting for transfers between devices  14.4 us (10%)
  local copies, waits for them, and re-layouts  4.35 us (3%)
    all_to_all x2, blocking collectives, gathered(): lax.all_to_all(copies, BOTH, 0, 0, tiled=True, axis_index_groups=group)  39.6 us
    all_to_all x2, blocking collectives, sent_to_protos(): return lax.all_to_all(x, 'proto', 0, 0, tiled=True)  39.2 us
    all_to_all x1, waiting for transfers between devices, gathered(): lax.all_to_all(copies, BOTH, 0, 0, tiled=True, axis_index_groups=group)  11.2 us
    all_to_all x2, starting transfers between devices, sent_to_protos(): return lax.all_to_all(x, 'proto', 0, 0, tiled=True)  10.6 us
    pallas_call x1, Pallas kernels, on_device(): streamed(weight_kernel, [shape((64, ROWS))], [stripe(B), stripe(B), whole...  9.98 us
    pallas_call x1, Pallas kernels, on_device(): call(first_kernel, [pltpu.HBM((ROWS, B), f32), pltpu.HBM((D, B), bf16), s...  6.72 us
    pallas_call x1, Pallas kernels, on_device(): call(student_kernel, [pltpu.HBM((ROWS, B), f32), shape((ROWS, 128)), shap...  6.23 us
    all_to_all x1, starting transfers between devices, gathered(): lax.all_to_all(copies, BOTH, 0, 0, tiled=True, axis_index_groups=group)  4.01 us
  transfers between devices with their start and end apart: 3, of which 3 were waited for; matrix products, arithmetic and copies ran while one was open for 0% of the time, Pallas kernels for 11%

profile of v4, /device:TPU:1, one launch (start us, length us, event | category | flops | bytes accessed | tf_op | source)
XLA Modules:
  0.0 143.3 jit_solution(731708697739449868)
XLA Ops:
  0.6 0.7 pad_maximum_fusion
  1.4 29.5 %all_to_all.35 = bf16[64,16,128]{2,1,0:T(8,128)(2,1)S(1)} all-to-all(bf16[64,16,128]{2,1,0:T(8,128)(2,1)S(1)} %broadcast_in_dim.6), channel_id=1, replica_groups={{0,2,4,6,8,10,12,14,16,18,20,22,24,26,28,30,32,34,36,38,40,42,44,46,48,..., dimensions={0} | all-to-all | bytes 524288 | tf_op jit(solution)/shard_map/all_to_all | solution.py:37
  30.9 1.1 broadcast_in_dim.7
  32.0 4.0 %all-to-all-start.1 = ((bf16[4,64,16,128]{3,2,1,0:T(8,128)(2,1)}), bf16[4,64,16,128]{3,2,1,0:T(8,128)(2,1)S(1)}, u32[]{:S(2)}, u32[]{:S(2)}) async-start(bf16[4,64,16,128]{3,2,1,0:T(8,128)(2,1)} %broadcast_in_dim.7), calls=%async_computation.1 | async-start | bytes 2097152 | tf_op jit(solution)/shard_map/all_to_all | solution.py:37
  36.0 11.2 %all-to-all-done.1 = bf16[4,64,16,128]{3,2,1,0:T(8,128)(2,1)S(1)} async-done(((bf16[4,64,16,128]{3,2,1,0:T(8,128)(2,1)}), bf16[4,64,16,128]{3,2,1,0:T(8,128)(2,1)S(1)}, u32[]{:S(2)}, u32[]{:S(2)}) %all-to-all-start.1) | async-done | bytes 1048608 | tf_op jit(solution)/shard_map/all_to_all | solution.py:37
  47.2 0.3 broadcast_in_dim.8
  47.4 0.0 copy-start.7
  47.4 10.1 %all_to_all.36.third_ref = bf16[2,4,64,16,128]{4,3,2,1,0:T(8,128)(2,1)S(1)} all-to-all(bf16[2,4,64,16,128]{4,3,2,1,0:T(8,128)(2,1)S(1)} %broadcast_in_dim.8), channel_id=1, replica_groups={{0,1},{2,3},{4,5},{6,7},{8,9},{10,11},{12,13},{14,15},{16,17},{18,19},{..., dimensions={0} | all-to-all | bytes 4194304 | tf_op jit(solution)/shard_map/all_to_all | solution.py:37
  57.5 0.0 copy-done.7
  57.5 0.0 copy-start
  57.5 6.7 %shard_map.67 = (f32[2048,1024]{1,0:T(8,128)}, bf16[512,1024]{1,0:T(8,128)(2,1)}, bf16[64,8,128]{2,1,0:T(8,128)(2,1)}, f32[8,128]{1,0:T(8,128)S(1)}, f32[512,128]{1,0:T(8,128)S(1)}) custom-call(s32[1]{0:T(128)} %bitcast.me_ref, bf16[2,4,64,16,128]{4,3,2,1,0:T(8,128)(2,1)S(1)} %all_to_all.36.third_ref, bf16[2048,512]{1,0:T(8,128)(2,1)S(1)} %copy-done.7), custom_call_target="tpu_custom_call" | custom-call | flops 2147483648 | bytes 12582912 | tf_op jit(solution)/shard_map/pallas_call | solution.py:317
  64.2 5.6 %all-to-all-start.3 = ((bf16[64,8,128]{2,1,0:T(8,128)(2,1)}), bf16[64,8,128]{2,1,0:T(8,128)(2,1)S(1)}, u32[]{:S(2)}, u32[]{:S(2)}) async-start(bf16[64,8,128]{2,1,0:T(8,128)(2,1)} %get-tuple-element.23), calls=%async_computation.3 | async-start | bytes 262144 | tf_op jit(solution)/shard_map/all_to_all | solution.py:41
  69.8 0.0 copy-done
  69.8 0.0 copy-start.1
  69.9 1.2 copy-done.1
  71.1 6.2 %shard_map.68 = (f32[2048,1024]{1,0:T(8,128)}, f32[2048,128]{1,0:T(8,128)S(1)}, f32[8,128]{1,0:T(8,128)S(1)}) custom-call(s32[1]{0:T(128)} %bitcast.me_ref, bf16[512,1024]{1,0:T(8,128)(2,1)S(1)} %copy-done.1, bf16[2048,512]{1,0:T(8,128)(2,1)S(1)} %copy-done), custom_call_target="tpu_custom_call" | custom-call | flops 2147483648 | bytes 12582912 | tf_op jit(solution)/shard_map/pallas_call | solution.py:327
  77.3 0.0 copy-start.3
  77.3 1.0 copy-done.3
  78.3 1.5 %all-to-all-done.3.got_ref = bf16[64,8,128]{2,1,0:T(8,128)(2,1)S(1)} async-done(((bf16[64,8,128]{2,1,0:T(8,128)(2,1)}), bf16[64,8,128]{2,1,0:T(8,128)(2,1)S(1)}, u32[]{:S(2)}, u32[]{:S(2)}) %all-to-all-start.3) | async-done | bytes 131104 | tf_op jit(solution)/shard_map/all_to_all | solution.py:41
  79.8 3.7 %shard_map.69 = (f32[2048,1024]{1,0:T(8,128)S(1)}, bf16[64,24,128]{2,1,0:T(8,128)(2,1)S(1)}, f32[8,128]{1,0:T(8,128)S(1)}) custom-call(bf16[64,8,128]{2,1,0:T(8,128)(2,1)S(1)} %all-to-all-done.3.got_ref, f32[2048,1024]{1,0:T(8,128)} %get-tuple-element.24.far_ref.kernel_ref, f32[8,128]{1,0:T(8,128)S(1)} %get-tuple-element.26.total_ref), custom_call_target="tpu_custom_call" | custom-call | flops 8388608 | bytes 8388608 | tf_op jit(solution)/shard_map/pallas_call | solution.py:335
  83.5 23.3 %all_to_all.37.got_ref = bf16[64,24,128]{2,1,0:T(8,128)(2,1)S(1)} all-to-all(bf16[64,24,128]{2,1,0:T(8,128)(2,1)S(1)} %get-tuple-element.27), channel_id=1, replica_groups=mesh['smp'=8,'proto'=64] {'proto'}, dimensions={0} | all-to-all | bytes 786432 | tf_op jit(solution)/shard_map/all_to_all | solution.py:41
  106.9 0.0 copy-start.4
  106.9 1.6 %shard_map.70 = (f32[2048,128]{1,0:T(8,128)S(1)}, bf16[64,8,128]{2,1,0:T(8,128)(2,1)S(1)}, f32[8,128]{1,0:T(8,128)S(1)}, f32[8,128]{1,0:T(8,128)S(1)}, f32[8,128]{1,0:T(8,128)S(1)}) custom-call(s32[1]{0:T(128)} %bitcast.me_ref, bf16[64,24,128]{2,1,0:T(8,128)(2,1)S(1)} %all_to_all.37.got_ref, f32[2048,1024]{1,0:T(8,128)S(1)} %get-tuple-element.28.kernel_ref, ...), custom_call_target="tpu_custom_call" | custom-call | flops 8388608 | bytes 8388608 | tf_op jit(solution)/shard_map/pallas_call | solution.py:345
  108.4 15.9 %all_to_all.38.got_ref = bf16[64,8,128]{2,1,0:T(8,128)(2,1)S(1)} all-to-all(bf16[64,8,128]{2,1,0:T(8,128)(2,1)S(1)} %get-tuple-element.30), channel_id=1, replica_groups=mesh['smp'=8,'proto'=64] {'proto'}, dimensions={0} | all-to-all | bytes 262144 | tf_op jit(solution)/shard_map/all_to_all | solution.py:41
  124.3 0.0 copy-done.4
  124.3 0.0 copy-start.2
  124.3 0.9 shard_map.71
  125.2 0.0 copy-start.5
  125.2 0.7 copy-done.5
  125.9 5.0 %all-to-all-start.6 = ((bf16[64,16,128]{2,1,0:T(8,128)(2,1)}), bf16[64,16,128]{2,1,0:T(8,128)(2,1)S(1)}, u32[]{:S(2)}, u32[]{:S(2)}) async-start(bf16[64,16,128]{2,1,0:T(8,128)(2,1)} %copy-done.5), calls=%async_computation.6 | async-start | bytes 524288 | tf_op jit(solution)/shard_map/all_to_all | solution.py:41
  130.9 0.0 copy-done.2
  130.9 0.0 copy-start.6
  130.9 10.0 %shard_map.73 = f32[64,2048]{1,0:T(8,128)} custom-call(s32[1]{0:T(128)} %bitcast.me_ref, f32[2048,1024]{1,0:T(8,128)} %get-tuple-element.24.far_ref.kernel_ref, f32[2048,1024]{1,0:T(8,128)} %get-tuple-element.40.logits_ref, f32[8,128]{1,0:T(8,128)S(1)} %get-tuple-element.34.total_ref, f32[8,128]{1,0:T(8,128)S(1)} %get-tuple-element.41.before_ref, ...), custom_call_target="tpu_custom_call" | custom-call | flops 268435456 | bytes 17825792 | tf_op jit(solution)/shard_map/pallas_call | solution.py:366
  140.9 1.7 %all-to-all-done.6.got_ref = bf16[64,16,128]{2,1,0:T(8,128)(2,1)S(1)} async-done(((bf16[64,16,128]{2,1,0:T(8,128)(2,1)}), bf16[64,16,128]{2,1,0:T(8,128)(2,1)S(1)}, u32[]{:S(2)}, u32[]{:S(2)}) %all-to-all-start.6) | async-done | bytes 262176 | tf_op jit(solution)/shard_map/all_to_all | solution.py:41
  142.6 0.0 copy-done.6
  142.6 0.7 shard_map.72
  (1 shorter events, 0.0 us)
Async XLA Ops:
  32.0 15.2 %all-to-all-start.1 = ((bf16[4,64,16,128]{3,2,1,0:T(8,128)(2,1)}), bf16[4,64,16,128]{3,2,1,0:T(8,128)(2,1)S(1)}, u32[]{:S(2)}, u32[]{:S(2)}) async-start(bf16[4,64,16,128]{3,2,1,0:T(8,128)(2,1)} %broadcast_in_dim.7), calls=%async_computation.1 | async-start | bytes 2097152 | tf_op jit(solution)/shard_map/all_to_all | solution.py:37
  47.4 10.1 %copy-start.7 = (bf16[2048,512]{1,0:T(8,128)(2,1)S(1)}, bf16[2048,512]{1,0:T(8,128)(2,1)}, u32[]{:S(2)}) copy-start(bf16[2048,512]{1,0:T(8,128)(2,1)} %weight_ref.3) | copy-start | bytes 6291460
  57.5 12.3 %copy-start = (bf16[2048,512]{1,0:T(8,128)(2,1)S(1)}, bf16[2048,512]{1,0:T(8,128)(2,1)}, u32[]{:S(2)}) copy-start(bf16[2048,512]{1,0:T(8,128)(2,1)} %weight_ref.5) | copy-start | bytes 6291460
  64.2 15.6 %all-to-all-start.3 = ((bf16[64,8,128]{2,1,0:T(8,128)(2,1)}), bf16[64,8,128]{2,1,0:T(8,128)(2,1)S(1)}, u32[]{:S(2)}, u32[]{:S(2)}) async-start(bf16[64,8,128]{2,1,0:T(8,128)(2,1)} %get-tuple-element.23), calls=%async_computation.3 | async-start | bytes 262144 | tf_op jit(solution)/shard_map/all_to_all | solution.py:41
  69.8 1.2 copy-start.1
  77.3 1.0 copy-start.3
  106.9 17.4 %copy-start.4 = (f32[2048,128]{1,0:T(8,128)S(1)}, f32[2048,128]{1,0:T(8,128)}, u32[]{:S(2)}) copy-start(f32[2048,128]{1,0:T(8,128)} %copy-done.3) | copy-start | bytes 3145732
  124.3 6.6 %copy-start.2 = (bf16[512,1024]{1,0:T(8,128)(2,1)S(1)}, bf16[512,1024]{1,0:T(8,128)(2,1)}, u32[]{:S(2)}) copy-start(bf16[512,1024]{1,0:T(8,128)(2,1)} %get-tuple-element.25.unit_ref) | copy-start | bytes 3145732
  125.2 0.7 copy-start.5
  125.9 16.7 %all-to-all-start.6 = ((bf16[64,16,128]{2,1,0:T(8,128)(2,1)}), bf16[64,16,128]{2,1,0:T(8,128)(2,1)S(1)}, u32[]{:S(2)}, u32[]{:S(2)}) async-start(bf16[64,16,128]{2,1,0:T(8,128)(2,1)} %copy-done.5), calls=%async_computation.6 | async-start | bytes 524288 | tf_op jit(solution)/shard_map/all_to_all | solution.py:41
  130.9 11.7 %copy-start.6 = (bf16[128,8]{0,1:T(8,128)(2,1)S(1)}, bf16[128,8]{0,1:T(8,128)(2,1)}, u32[]{:S(2)}) copy-start(bf16[128,8]{0,1:T(8,128)(2,1)} %param.5) | copy-start | bytes 6148

commit v5 on v4

--- a/solution.py
+++ b/solution.py
@@ -13,6 +13,7 @@
 PARTS = {"x": 4, "yh": 2, "yl": 4, "z": 8, "c": 2}
 B, K, D = 1024, 131072, 512
 ROWS = 2048
+SHARE = 1.0 / (1024 * 0.1)
 TILE = 256
 WIDE = 512
 BLOCKS = 8
@@ -219,17 +220,22 @@
     sent_ref[...] = jnp.broadcast_to(packed[None], sent_ref.shape)
 
 
+def split_rows(value):
+    high = value.astype(bf16).astype(f32)
+    return [high, value - high]
+
+
 def third_kernel(
-    me_ref, got_ref, kernel_ref, kept_ref, scaled_ref, sent_ref, total_ref, col_out, before_ref, col_ref, mass_ref
+    me_ref, got_ref, kernel_ref, kept_ref, logits_ref, features_ref, weight_ref,
+    sent_ref, total_ref, before_ref, col_ref, mass_ref, scaled_ref, pair_ref,
 ):
+    me = me_ref[0]
     got = received(got_ref)
     before_ref[...] = got[:8, :]
     total_ref[...] = got[8:16, :] + got[16:, :]
-    col = 1.0 / (B * got[:8, :])
-    col_out[...] = col
-    col_ref[...] = as_row(col)
+    col_ref[...] = as_row(1.0 / (B * got[:8, :]))
     mass_ref[...] = jnp.zeros_like(mass_ref)
-    lanes = pl.ds(pl.multiple_of(me_ref[0] * 128, 128), 128)
+    lanes = pl.ds(pl.multiple_of(me * 128, 128), 128)
 
     @pl.loop(0, ROWS // TILE)
     def _(i):
@@ -240,63 +246,80 @@
         mass_ref[...] += folded(kernel * row_scale)
 
     change = as_blocks(mass_ref[...]) - kept_ref[...]
-    sent_ref[...] = jnp.broadcast_to(change.astype(bf16)[None], sent_ref.shape)
-
-
-def split_rows(value):
-    high = value.astype(bf16).astype(f32)
-    middle = (value - high).astype(bf16).astype(f32)
-    return [high, middle, value - high - middle]
-
-
-def own_kernel(
-    me_ref, got_ref, before_ref, scaled_ref, logits_ref, total_ref, features_ref, weight_ref, sent_ref, col_ref,
-    grad_ref,
-):
-    me = me_ref[0]
-    col_ref[...] = 1.0 / (B * (before_ref[...] + received(got_ref)))
-    own_col = col_ref[pl.ds(me, 1), :] * B
+    logits = logits_ref[...]
+    own_col = 1.0 / before_ref[pl.ds(me, 1), :]
     own_total = 1.0 / total_ref[pl.ds(me, 1), :]
-    logits = logits_ref[...]
     targets = scaled_ref[...] * own_col
     weighted = jnp.sum(folded(targets * logits), axis=0, keepdims=True)
-    grad_ref[...] = ((jnp.exp(logits) * own_total - targets) * (1.0 / (B * STUDENT_TEMP))).astype(bf16)
-    unit_part = lax.dot_general(
-        grad_ref[...], weight_ref[...], (((0,), (0,)), ((), ())), preferred_element_type=f32
-    ).T
-    inner = jnp.sum(folded(features_ref[...] * unit_part), axis=0, keepdims=True)
-    extra = jnp.concatenate(split_rows(inner) + split_rows(weighted) + [jnp.zeros((2, 128), f32)], axis=0)
-    pieces = unit_part.reshape(64, 8, 128)
+    pair_ref[:, :128] = ((jnp.exp(logits) * own_total - targets) * SHARE).astype(bf16)
+    pair_ref[:, 128:] = (targets * SHARE).astype(bf16)
+    parts = lax.dot_general(
+        pair_ref[...], weight_ref[...], (((0,), (0,)), ((), ())), preferred_element_type=f32
+    )
+    grad_part, target_part = parts[:128, :].T, parts[128:, :].T
+    features = features_ref[...]
+    inner_grad = jnp.sum(folded(features * grad_part), axis=0, keepdims=True)
+    inner_target = jnp.sum(folded(features * target_part), axis=0, keepdims=True)
+    extra = jnp.concatenate(
+        split_rows(inner_grad) + split_rows(inner_target) + split_rows(weighted) + [jnp.zeros((2, 128), f32)],
+        axis=0,
+    )
+
+    def everywhere(rows):
+        return jnp.broadcast_to(rows[None], (64, 8, 128))
+
     sent_ref[...] = jnp.concatenate(
-        [pieces, jnp.broadcast_to(extra[None], (64, 8, 128))], axis=1
+        [everywhere(change), grad_part.reshape(64, 8, 128), target_part.reshape(64, 8, 128), everywhere(extra)],
+        axis=1,
     ).astype(bf16)
 
 
 def weight_kernel(
-    me_ref, kernel_ref, logits_ref, total_ref, before_ref, col_ref, unit_ref, out_ref, rows_ref
+    me_ref, kernel_ref, logits_ref, total_ref, before_ref, unit_ref, out_ref, targets_ref, rows_ref
 ):
     @pl.when(pl.program_id(0) == 0)
     def _():
-        rows_ref[0:1, :] = as_row(before_ref[...])
-        rows_ref[1:2, :] = as_row(col_ref[...] * B)
+        rows_ref[0:1, :] = as_row(1.0 / (B * before_ref[...]))
+        rows_ref[1:2, :] = as_row(1.0 / before_ref[...])
         rows_ref[2:3, :] = as_row(1.0 / total_ref[...])
 
     kernel = kernel_ref[...]
     row_scale = 1.0 / (K * jnp.sum(kernel * rows_ref[0:1, :], axis=1, keepdims=True))
     targets = kernel * row_scale * rows_ref[1:2, :]
     probs = jnp.exp(logits_ref[...]) * rows_ref[2:3, :]
-    grad = ((probs - targets) * (1.0 / (B * STUDENT_TEMP))).astype(bf16)
+    grad = ((probs - targets) * SHARE).astype(bf16)
+    targets_ref[...] = (targets * SHARE).astype(bf16)
     out_ref[...] = lax.dot_general(unit_ref[...], grad, (((1,), (1,)), ((), ())), preferred_element_type=f32)
 
 
-def final_kernel(me_ref, got_ref, features_ref, scale_ref, total_ref, features_out, loss_out):
+def final_kernel(
+    me_ref, got_ref, features_ref, scale_ref, total_ref, before_ref, unit_ref, near_ref, targets_far,
+    features_out, loss_out, weight_out, change_ref, targets_ref, sem_ref,
+):
+    def copy_in(i):
+        rows = pl.ds(i * WIDE, WIDE)
+        return pltpu.make_async_copy(targets_far.at[rows], targets_ref.at[rows], sem_ref.at[i])
+
+    for i in range(ROWS // WIDE):
+        copy_in(i).start()
     me = me_ref[0]
     got = received(got_ref)
-    inner = got[8:9] + got[9:10] + got[10:11]
-    weighted = got[11:12] + got[12:13] + got[13:14]
+    before = before_ref[...]
+    change_ref[...] = got[:8] / (before + got[:8])
+    own = change_ref[pl.ds(me, 1), :]
+    unit_grad = got[8:16] + own * got[16:24]
+    inner = (got[24:25] + got[25:26]) + own * (got[26:27] + got[27:28])
     scale = scale_ref[pl.ds(me, 1), :]
-    features_out[...] = scale * got[:8] - (scale * scale * scale * inner) * features_ref[...].astype(f32)
-    loss_out[...] = jnp.log(total_ref[pl.ds(me, 1), :]) - weighted
+    features_out[...] = scale * unit_grad - (scale * scale * scale * inner) * features_ref[...].astype(f32)
+    loss_out[...] = jnp.log(total_ref[pl.ds(me, 1), :]) - (1.0 - own) * (got[28:29] + got[29:30])
+    units = unit_ref[pl.ds(pl.multiple_of(me * 64, 64), 64), :].astype(f32)
+    moved = (units * as_row(change_ref[...])).astype(bf16)
+    for i in range(ROWS // WIDE):
+        copy_in(i).wait()
+        rows = pl.ds(i * WIDE, WIDE)
+        weight_out[:, rows] = near_ref[:, rows] + lax.dot_general(
+            moved, targets_ref[rows, :], (((1,), (1,)), ((), ())), preferred_element_type=f32
+        )
 
 
 def shape(dims, dtype=f32):
@@ -306,6 +329,7 @@
 def on_device(teacher_features, student_features, teacher_weight, student_weight):
     me = lax.axis_index("smp").astype(jnp.int32).reshape(1)
     raw = jnp.concatenate([teacher_features.T, student_features.T], axis=0)
+    raw, me = lax.optimization_barrier((raw, me))
     first = gathered(raw, ("yh", "yl", "z"))
     second = gathered(first, ("x",))
     third = gathered(second, ("c",))
@@ -313,6 +337,7 @@
     pair = pltpu.SemaphoreType.DMA((2,))
     stage = pltpu.VMEM((2, TILE, B), f32)
     row, rows8 = pltpu.VMEM((1, B), f32), pltpu.VMEM((8, B), f32)
+    rows8_small = pltpu.VMEM((8, 128), f32)
     matmul = dict(flops=2 * ROWS * B * D, moved=12 * 2**20, exps=ROWS * B)
     kernel, student_unit, sent_1, student_scale, features_own = call(
         first_kernel,
@@ -342,41 +367,38 @@
         moved=8 * 2**20,
     )(got_1, far(kernel), local_total)
     got_2 = sent_to_protos(sent_2)
-    scaled_own, sent_3, total, col_before, before = call(
+    sent_3, total, before = call(
         third_kernel,
-        [shape((ROWS, 128)), shape((64, 8, 128), bf16), shape((8, 128)), shape((8, 128)), shape((8, 128))],
-        [SMEM, VMEM, VMEM, VMEM],
+        [shape((64, 32, 128), bf16), shape((8, 128)), shape((8, 128))],
+        [SMEM] + [VMEM] * 6,
         None,
-        [row, rows8],
-        flops=4 * ROWS * B,
-        moved=8 * 2**20,
-    )(me, got_2, kernel_near, kept)
+        [row, rows8, pltpu.VMEM((ROWS, 128), f32), pltpu.VMEM((ROWS, 256), bf16)],
+        flops=2 * ROWS * 256 * D,
+        moved=12 * 2**20,
+        exps=ROWS * 128,
+    )(me, got_2, kernel_near, kept, logits_own, features_own, student_weight)
     got_3 = sent_to_protos(sent_3)
-    sent_4, col_scale = call(
-        own_kernel,
-        [shape((64, 16, 128), bf16), shape((8, 128))],
-        [SMEM] + [VMEM] * 7,
-        None,
-        [pltpu.VMEM((ROWS, 128), bf16)],
-        flops=2 * ROWS * 128 * D,
-        moved=4 * 2**20,
-        exps=ROWS * 128,
-    )(me, got_3, before, scaled_own, logits_own, total, features_own, student_weight)
-    got_4 = sent_to_protos(sent_4)
-    (grad_weight,) = streamed(
+    weight_near, targets = streamed(
         weight_kernel,
-        [shape((64, ROWS))],
-        [stripe(B), stripe(B), whole(8, 128), whole(8, 128), whole(8, 128),
-         pl.BlockSpec((64, B), lambda i, me: (me[0], 0))],
-        [pl.BlockSpec((64, TILE), lambda i, me: (0, i))],
+        [shape((64, ROWS)), pltpu.HBM((ROWS, B), bf16)],
+        [stripe(B), stripe(B), whole(8, 128), whole(8, 128), pl.BlockSpec((64, B), lambda i, me: (me[0], 0))],
+        [pl.BlockSpec((64, TILE), lambda i, me: (0, i)), stripe(B)],
         [rows8],
         flops=2 * ROWS * B * 64,
-        moved=17 * 2**20,
+        moved=21 * 2**20,
         exps=ROWS * B,
-    )(me, far(kernel), far(logits), total, col_before, col_scale, student_unit)
-    grad_features, loss = call(
-        final_kernel, [shape((8, 128)), shape((1, 128))], [SMEM] + [VMEM] * 4
-    )(me, got_4, student_features.T, student_scale, total)
+    )(me, far(kernel), far(logits), total, before, student_unit)
+    grad_features, loss, grad_weight = call(
+        final_kernel,
+        [shape((8, 128)), shape((1, 128)), shape((64, ROWS))],
+        [SMEM] + [VMEM] * 7 + [ANY],
+        None,
+        [rows8_small, pltpu.VMEM((ROWS, B), bf16), pltpu.SemaphoreType.DMA((ROWS // WIDE,))],
+        flops=2 * ROWS * B * 64,
+        moved=5 * 2**20,
+    )(
+        me, got_3, student_features.T, student_scale, total, before, student_unit, weight_near, far(targets)
+    )
     return loss.reshape(128), grad_features.T, grad_weight.T
 
 

time: 144 us -> 137 us (0.951)
  waiting for transfers between devices: 14.4 us -> 7.5 us
  Pallas kernels: 29.7 us -> 34.2 us
  starting transfers between devices: 14.6 us -> 11.7 us
    all_to_all x2 -> x1, blocking collectives: 39.2 us -> 23.4 us  [sent_to_protos(): return lax.all_to_all(x, 'proto', 0, 0, tiled=True)]
    all_to_all x2 -> x3, blocking collectives: 39.6 us -> 54.5 us  [gathered(): lax.all_to_all(copies, BOTH, 0, 0, tiled=True, axis_index_groups=group)]
    all_to_all x1 -> x0, waiting for transfers between devices: 11.2 us -> none  [gathered(): lax.all_to_all(copies, BOTH, 0, 0, tiled=True, axis_index_groups=group)]
    pallas_call x4 -> x3, Pallas kernels: 13.1 us -> 17.5 us  [the longest x1 11.1 us: on_device(): streamed(weight_kernel, [shape((64, ROWS)), pltpu.HBM((ROWS, B), bf16)],...]
    all_to_all x2, waiting for transfers between devices: 3.28 us -> 7.5 us  [sent_to_protos(): return lax.all_to_all(x, 'proto', 0, 0, tiled=True)]
    all_to_all x1 -> x0, starting transfers between devices: 4.01 us -> none  [gathered(): lax.all_to_all(copies, BOTH, 0, 0, tiled=True, axis_index_groups=group)]
  transfers between devices with their start and end apart: 3 -> 2, of which waited for: 3 -> 2; matrix products, arithmetic and copies ran while one was open for 0% -> 0% of each run, Pallas kernels for 11% -> 13%
where the time goes in v5:
time: 137 us; the launch traced here: 136 us
  blocking collectives  77.9 us (57%)
  Pallas kernels  34.2 us (25%)
  starting transfers between devices  11.7 us (9%)
  waiting for transfers between devices  7.5 us (5%)
  local copies, waits for them, and re-layouts  3.47 us (3%)
    all_to_all x3, blocking collectives, gathered(): lax.all_to_all(copies, BOTH, 0, 0, tiled=True, axis_index_groups=group)  54.5 us
    all_to_all x1, blocking collectives, sent_to_protos(): return lax.all_to_all(x, 'proto', 0, 0, tiled=True)  23.4 us
    all_to_all x2, starting transfers between devices, sent_to_protos(): return lax.all_to_all(x, 'proto', 0, 0, tiled=True)  11.7 us
    pallas_call x1, Pallas kernels, on_device(): streamed(weight_kernel, [shape((64, ROWS)), pltpu.HBM((ROWS, B), bf16)],...  11.1 us
    all_to_all x2, waiting for transfers between devices, sent_to_protos(): return lax.all_to_all(x, 'proto', 0, 0, tiled=True)  7.5 us
    pallas_call x1, Pallas kernels, on_device(): call(first_kernel, [pltpu.HBM((ROWS, B), f32), pltpu.HBM((D, B), bf16), s...  6.71 us
    pallas_call x1, Pallas kernels, on_device(): call(student_kernel, [pltpu.HBM((ROWS, B), f32), shape((ROWS, 128)), shap...  6.24 us
    pallas_call x1, Pallas kernels, on_device(): call(final_kernel, [shape((8, 128)), shape((1, 128)), shape((64, ROWS))],...  3.81 us
  transfers between devices with their start and end apart: 2, of which 2 were waited for; matrix products, arithmetic and copies ran while one was open for 0% of the time, Pallas kernels for 13%

profile of v5, /device:TPU:1, one launch (start us, length us, event | category | flops | bytes accessed | tf_op | source)
XLA Modules:
  0.0 136.2 jit_solution(14957813007972475594)
XLA Ops:
  0.6 0.7 pad_maximum_fusion
  1.4 29.5 %all_to_all.30 = bf16[64,16,128]{2,1,0:T(8,128)(2,1)S(1)} all-to-all(bf16[64,16,128]{2,1,0:T(8,128)(2,1)S(1)} %broadcast_in_dim.6), channel_id=1, replica_groups={{0,2,4,6,8,10,12,14,16,18,20,22,24,26,28,30,32,34,36,38,40,42,44,46,48,..., dimensions={0} | all-to-all | bytes 524288 | tf_op jit(solution)/shard_map/all_to_all | solution.py:38
  30.9 0.1 broadcast_in_dim.7
  31.0 0.0 copy-start.7
  31.0 15.4 %all_to_all.31 = bf16[4,64,16,128]{3,2,1,0:T(8,128)(2,1)S(1)} all-to-all(bf16[4,64,16,128]{3,2,1,0:T(8,128)(2,1)S(1)} %broadcast_in_dim.7), channel_id=1, replica_groups={{0,128,256,384},{1,129,257,385},{2,130,258,386},{3,131,259,387},{4,132,..., dimensions={0} | all-to-all | bytes 2097152 | tf_op jit(solution)/shard_map/all_to_all | solution.py:38
  46.4 0.3 broadcast_in_dim.8
  46.7 9.7 %all_to_all.32.third_ref = bf16[2,4,64,16,128]{4,3,2,1,0:T(8,128)(2,1)S(1)} all-to-all(bf16[2,4,64,16,128]{4,3,2,1,0:T(8,128)(2,1)S(1)} %broadcast_in_dim.8), channel_id=1, replica_groups={{0,1},{2,3},{4,5},{6,7},{8,9},{10,11},{12,13},{14,15},{16,17},{18,19},{..., dimensions={0} | all-to-all | bytes 4194304 | tf_op jit(solution)/shard_map/all_to_all | solution.py:38
  56.3 0.0 copy-done.7
  56.3 0.0 copy-start.2
  56.3 6.7 %shard_map.67 = (f32[2048,1024]{1,0:T(8,128)}, bf16[512,1024]{1,0:T(8,128)(2,1)}, bf16[64,8,128]{2,1,0:T(8,128)(2,1)}, f32[8,128]{1,0:T(8,128)S(1)}, f32[512,128]{1,0:T(8,128)S(1)}) custom-call(s32[1]{0:T(128)} %bitcast.2.me_ref, bf16[2,4,64,16,128]{4,3,2,1,0:T(8,128)(2,1)S(1)} %all_to_all.32.third_ref, bf16[2048,512]{1,0:T(8,128)(2,1)S(1)} %copy-done.7), custom_call_target="tpu_custom_call" | custom-call | flops 2147483648 | bytes 12582912 | tf_op jit(solution)/shard_map/pallas_call | solution.py:342
  63.1 5.6 %all-to-all-start.3 = ((bf16[64,8,128]{2,1,0:T(8,128)(2,1)}), bf16[64,8,128]{2,1,0:T(8,128)(2,1)S(1)}, u32[]{:S(2)}, u32[]{:S(2)}) async-start(bf16[64,8,128]{2,1,0:T(8,128)(2,1)} %get-tuple-element.26), calls=%async_computation.3 | async-start | bytes 262144 | tf_op jit(solution)/shard_map/all_to_all | solution.py:42
  68.7 0.0 copy-done.2
  68.7 0.0 copy-start
  68.7 1.2 copy-done
  69.9 6.2 %shard_map.68 = (f32[2048,1024]{1,0:T(8,128)}, f32[2048,128]{1,0:T(8,128)S(1)}, f32[8,128]{1,0:T(8,128)S(1)}) custom-call(s32[1]{0:T(128)} %bitcast.2.me_ref, bf16[512,1024]{1,0:T(8,128)(2,1)S(1)} %copy-done, bf16[2048,512]{1,0:T(8,128)(2,1)S(1)} %copy-done.2), custom_call_target="tpu_custom_call" | custom-call | flops 2147483648 | bytes 12582912 | tf_op jit(solution)/shard_map/pallas_call | solution.py:352
  76.1 0.0 copy-start.3
  76.2 1.0 copy-done.3
  77.1 1.5 %all-to-all-done.3.got_ref = bf16[64,8,128]{2,1,0:T(8,128)(2,1)S(1)} async-done(((bf16[64,8,128]{2,1,0:T(8,128)(2,1)}), bf16[64,8,128]{2,1,0:T(8,128)(2,1)S(1)}, u32[]{:S(2)}, u32[]{:S(2)}) %all-to-all-start.3) | async-done | bytes 131104 | tf_op jit(solution)/shard_map/all_to_all | solution.py:42
  78.6 0.0 copy-start.4
  78.7 3.8 %shard_map.69 = (f32[2048,1024]{1,0:T(8,128)S(1)}, bf16[64,24,128]{2,1,0:T(8,128)(2,1)S(1)}, f32[8,128]{1,0:T(8,128)S(1)}) custom-call(bf16[64,8,128]{2,1,0:T(8,128)(2,1)S(1)} %all-to-all-done.3.got_ref, f32[2048,1024]{1,0:T(8,128)} %get-tuple-element.27.far_ref.kernel_ref, f32[8,128]{1,0:T(8,128)S(1)} %get-tuple-element.29.total_ref), custom_call_target="tpu_custom_call" | custom-call | flops 8388608 | bytes 8388608 | tf_op jit(solution)/shard_map/pallas_call | solution.py:360
  82.4 23.4 %all_to_all.33.got_ref = bf16[64,24,128]{2,1,0:T(8,128)(2,1)S(1)} all-to-all(bf16[64,24,128]{2,1,0:T(8,128)(2,1)S(1)} %get-tuple-element.30), channel_id=1, replica_groups=mesh['smp'=8,'proto'=64] {'proto'}, dimensions={0} | all-to-all | bytes 786432 | tf_op jit(solution)/shard_map/all_to_all | solution.py:42
  105.8 0.0 copy-done.4
  105.8 0.0 copy-start.1
  105.8 2.6 %shard_map.70 = (bf16[64,32,128]{2,1,0:T(8,128)(2,1)S(1)}, f32[8,128]{1,0:T(8,128)S(1)}, f32[8,128]{1,0:T(8,128)S(1)}) custom-call(s32[1]{0:T(128)} %bitcast.2.me_ref, bf16[64,24,128]{2,1,0:T(8,128)(2,1)S(1)} %all_to_all.33.got_ref, f32[2048,1024]{1,0:T(8,128)S(1)} %get-tuple-element.31.kernel_ref, f32[8,128]{1,0:T(8,128)S(1)} %get-tuple-element.32.kept_ref, ...), custom_call_target="tpu_custom_call" | custom-call | flops 536870912 | bytes 12582912 | tf_op jit(solution)/shard_map/pallas_call | solution.py:370
  108.4 0.0 copy-start.5
  108.4 0.8 copy-done.5
  109.2 6.1 %all-to-all-start.5 = ((bf16[64,32,128]{2,1,0:T(8,128)(2,1)}), bf16[64,32,128]{2,1,0:T(8,128)(2,1)S(1)}, u32[]{:S(2)}, u32[]{:S(2)}) async-start(bf16[64,32,128]{2,1,0:T(8,128)(2,1)} %copy-done.5), calls=%async_computation.5 | async-start | bytes 1048576 | tf_op jit(solution)/shard_map/all_to_all | solution.py:42
  115.3 0.0 copy-done.1
  115.3 0.0 copy-start.6
  115.3 11.1 %shard_map.71 = (f32[64,2048]{1,0:T(8,128)S(1)}, bf16[2048,1024]{1,0:T(8,128)(2,1)}) custom-call(s32[1]{0:T(128)} %bitcast.2.me_ref, f32[2048,1024]{1,0:T(8,128)} %get-tuple-element.27.far_ref.kernel_ref, f32[2048,1024]{1,0:T(8,128)} %get-tuple-element.39.logits_ref, f32[8,128]{1,0:T(8,128)S(1)} %get-tuple-element.37.total_ref, ...), custom_call_target="tpu_custom_call" | custom-call | flops 268435456 | bytes 22020096 | tf_op jit(solution)/shard_map/pallas_call | solution.py:381
  126.4 6.0 %all-to-all-done.5.got_ref = bf16[64,32,128]{2,1,0:T(8,128)(2,1)S(1)} async-done(((bf16[64,32,128]{2,1,0:T(8,128)(2,1)}), bf16[64,32,128]{2,1,0:T(8,128)(2,1)S(1)}, u32[]{:S(2)}, u32[]{:S(2)}) %all-to-all-start.5) | async-done | bytes 524320 | tf_op jit(solution)/shard_map/all_to_all | solution.py:42
  132.4 0.0 copy-done.6
  132.4 3.8 %shard_map.72 = (f32[8,128]{1,0:T(8,128)}, f32[1,128]{1,0:T(1,128)}, f32[64,2048]{1,0:T(8,128)}) custom-call(s32[1]{0:T(128)} %bitcast.2.me_ref, bf16[64,32,128]{2,1,0:T(8,128)(2,1)S(1)} %all-to-all-done.5.got_ref, bf16[8,128]{1,0:T(8,128)(2,1)S(1)} %bitcast.7, f32[8,128]{1,0:T(8,128)S(1)} %get-tuple-element.36.scale_ref, ...), custom_call_target="tpu_custom_call" | custom-call | flops 268435456 | bytes 5242880 | tf_op jit(solution)/shard_map/pallas_call | solution.py:391
  (1 shorter events, 0.0 us)
Async XLA Ops:
  31.0 25.3 %copy-start.7 = (bf16[2048,512]{1,0:T(8,128)(2,1)S(1)}, bf16[2048,512]{1,0:T(8,128)(2,1)}, u32[]{:S(2)}) copy-start(bf16[2048,512]{1,0:T(8,128)(2,1)} %weight_ref.3) | copy-start | bytes 6291460
  56.3 12.3 %copy-start.2 = (bf16[2048,512]{1,0:T(8,128)(2,1)S(1)}, bf16[2048,512]{1,0:T(8,128)(2,1)}, u32[]{:S(2)}) copy-start(bf16[2048,512]{1,0:T(8,128)(2,1)} %weight_ref.5) | copy-start | bytes 6291460
  63.1 15.6 %all-to-all-start.3 = ((bf16[64,8,128]{2,1,0:T(8,128)(2,1)}), bf16[64,8,128]{2,1,0:T(8,128)(2,1)S(1)}, u32[]{:S(2)}, u32[]{:S(2)}) async-start(bf16[64,8,128]{2,1,0:T(8,128)(2,1)} %get-tuple-element.26), calls=%async_computation.3 | async-start | bytes 262144 | tf_op jit(solution)/shard_map/all_to_all | solution.py:42
  68.7 1.2 copy-start
  76.1 1.0 copy-start.3
  78.6 27.2 %copy-start.4 = (f32[2048,128]{1,0:T(8,128)S(1)}, f32[2048,128]{1,0:T(8,128)}, u32[]{:S(2)}) copy-start(f32[2048,128]{1,0:T(8,128)} %copy-done.3) | copy-start | bytes 3145732
  105.8 9.5 %copy-start.1 = (bf16[512,1024]{1,0:T(8,128)(2,1)S(1)}, bf16[512,1024]{1,0:T(8,128)(2,1)}, u32[]{:S(2)}) copy-start(bf16[512,1024]{1,0:T(8,128)(2,1)} %get-tuple-element.28.unit_ref) | copy-start | bytes 3145732
  108.4 0.8 copy-start.5
  109.2 23.2 %all-to-all-start.5 = ((bf16[64,32,128]{2,1,0:T(8,128)(2,1)}), bf16[64,32,128]{2,1,0:T(8,128)(2,1)S(1)}, u32[]{:S(2)}, u32[]{:S(2)}) async-start(bf16[64,32,128]{2,1,0:T(8,128)(2,1)} %copy-done.5), calls=%async_computation.5 | async-start | bytes 1048576 | tf_op jit(solution)/shard_map/all_to_all | solution.py:42
  115.3 17.1 %copy-start.6 = (bf16[128,8]{0,1:T(8,128)(2,1)S(1)}, bf16[128,8]{0,1:T(8,128)(2,1)}, u32[]{:S(2)}) copy-start(bf16[128,8]{0,1:T(8,128)(2,1)} %param.5) | copy-start | bytes 6148

commit v6 on v5

--- a/solution.py
+++ b/solution.py
@@ -16,6 +16,7 @@
 SHARE = 1.0 / (1024 * 0.1)
 TILE = 256
 WIDE = 512
+QUARTER = 16
 BLOCKS = 8
 f32, bf16 = jnp.float32, jnp.bfloat16
 VMEM = pl.BlockSpec(memory_space=pltpu.VMEM)
@@ -90,13 +91,10 @@
     return pl.BlockSpec((TILE, width), lambda i, me: (i, 0))
 
 
-def features_of(third_ref, x, yh):
-    base = pl.multiple_of(yh * 32, 32) if not isinstance(yh, int) else yh * 32
-    halves = [third_ref[c, x, pl.ds(base, 32)].astype(f32) for c in range(2)]
-    return [
-        jnp.stack([h[:, which * 8 : which * 8 + 8] for h in halves], axis=1).reshape(D, 128)
-        for which in range(2)
-    ]
+def features_of(cores, x, yh, which):
+    base = yh * 32 if isinstance(yh, int) else pl.multiple_of(yh * 32, 32)
+    halves = [ref[x, pl.ds(base, 32)].astype(f32)[:, which * 8 : which * 8 + 8] for ref in cores]
+    return jnp.stack(halves, axis=1).reshape(D, 128)
 
 
 def unit_columns(values):
@@ -117,47 +115,51 @@
     return jnp.concatenate([blocks[s : s + 1, :] for s in range(BLOCKS)], axis=1)
 
 
-def stage_out(stage_ref, out_ref, sem_ref, i, value):
-    slot = lax.rem(i, 2)
-    rows = pl.ds(pl.multiple_of(i * TILE, TILE), TILE)
-    copy = pltpu.make_async_copy(stage_ref.at[slot], out_ref.at[rows], sem_ref.at[slot])
-
-    @pl.when(i >= 2)
-    def _():
-        copy.wait()
-
-    stage_ref[slot] = value
-    copy.start()
-
-
-def stage_end(stage_ref, out_ref, sem_ref):
-    for slot in range(2):
-        rows = pl.ds((ROWS // TILE - 2 + slot) * TILE, TILE)
-        pltpu.make_async_copy(stage_ref.at[slot], out_ref.at[rows], sem_ref.at[slot]).wait()
-
-
 def first_kernel(
-    me_ref, third_ref, weight_ref, kernel_out, unit_out, sent_ref, scale_ref, features_ref,
-    teacher_ref, student_ref, stage_ref, mass_ref, sem_ref, unit_sem,
+    me_ref, own_ref, other_ref, weight_far, kernel_out, unit_ref, sent_out, scale_ref, features_ref,
+    teacher_ref, weight_ref, stage_ref, sent_ref, mass_ref, sem_ref, weight_sem, sent_sem,
 ):
-    for s in range(BLOCKS):
-        teacher, student = features_of(third_ref, s // 2, s % 2)
-        teacher_ref[:, s * 128 : (s + 1) * 128] = unit_columns(teacher)[0]
-        unit, scale = unit_columns(student)
-        student_ref[:, s * 128 : (s + 1) * 128] = unit
-        scale_ref[s : s + 1, :] = scale
-    unit_copy = pltpu.make_async_copy(student_ref, unit_out, unit_sem)
-    unit_copy.start()
-    me = me_ref[0]
-    features_ref[...] = features_of(third_ref, me // 2, lax.rem(me, 2))[1]
-    mass_ref[...] = jnp.zeros_like(mass_ref)
+    me, core = me_ref[0], me_ref[1]
+
+    def copy_in(i):
+        rows = pl.ds(pl.multiple_of(i * WIDE, WIDE), WIDE)
+        return pltpu.make_async_copy(weight_far.at[rows], weight_ref.at[rows], weight_sem.at[i])
+
+    for i in range(ROWS // WIDE):
+        copy_in(i).start()
+
+    def by_core(body):
+        @pl.when(core == 0)
+        def _():
+            body((own_ref, other_ref))
+
+        @pl.when(core == 1)
+        def _():
+            body((other_ref, own_ref))
+
+    def teacher_units(cores):
+        for s in range(BLOCKS):
+            values = features_of(cores, s // 2, s % 2, 0)
+            teacher_ref[:, s * 128 : (s + 1) * 128] = unit_columns(values)[0]
+
+    def student_units(cores):
+        for s in range(BLOCKS):
+            values = features_of(cores, s // 2, s % 2, 1)
+            unit, scale = unit_columns(values)
+            unit_ref[:, s * 128 : (s + 1) * 128] = unit
+            scale_ref[s : s + 1, :] = scale
+        features_ref[...] = features_of(cores, me // 2, lax.rem(me, 2), 1)
 
     def copy_out(i):
         rows = pl.ds(pl.multiple_of(i * WIDE, WIDE), WIDE)
         return pltpu.make_async_copy(stage_ref.at[rows], kernel_out.at[rows], sem_ref.at[i])
 
+    by_core(teacher_units)
+    mass_ref[...] = jnp.zeros_like(mass_ref)
+
     @pl.loop(0, ROWS // WIDE)
     def _(i):
+        copy_in(i).wait()
         rows = pl.ds(pl.multiple_of(i * WIDE, WIDE), WIDE)
         kernel = jnp.exp(
             jnp.dot(weight_ref[rows, :], teacher_ref[...], preferred_element_type=f32) * (1.0 / TEACHER_TEMP)
@@ -168,27 +170,41 @@
         mass_ref[...] += folded(kernel * row_scale)
 
     sent_ref[...] = jnp.broadcast_to(as_blocks(mass_ref[...]).astype(bf16)[None], sent_ref.shape)
+    sent_copy = pltpu.make_async_copy(sent_ref, sent_out, sent_sem)
+    sent_copy.start()
+    by_core(student_units)
+    sent_copy.wait()
     for i in range(ROWS // WIDE):
         copy_out(i).wait()
-    unit_copy.wait()
 
 
 def student_kernel(
-    me_ref, unit_ref, weight_ref, logits_out, own_ref, total_ref, stage_ref, sum_ref, sem_ref
+    me_ref, unit_ref, weight_ref, logits_out, own_out, total_ref, stage_ref, own_ref, sum_ref, sem_ref, own_sem
 ):
     sum_ref[...] = jnp.zeros_like(sum_ref)
     lanes = pl.ds(pl.multiple_of(me_ref[0] * 128, 128), 128)
 
-    @pl.loop(0, ROWS // TILE)
+    def copies(i):
+        rows = pl.ds(pl.multiple_of(i * WIDE, WIDE), WIDE)
+        return (
+            pltpu.make_async_copy(stage_ref.at[rows], logits_out.at[rows], sem_ref.at[i]),
+            pltpu.make_async_copy(own_ref.at[rows], own_out.at[rows], own_sem.at[i]),
+        )
+
+    @pl.loop(0, ROWS // WIDE)
     def _(i):
-        rows = pl.ds(pl.multiple_of(i * TILE, TILE), TILE)
+        rows = pl.ds(pl.multiple_of(i * WIDE, WIDE), WIDE)
         logits = jnp.dot(weight_ref[rows, :], unit_ref[...], preferred_element_type=f32) * (1.0 / STUDENT_TEMP)
-        stage_out(stage_ref, logits_out, sem_ref, i, logits)
-        own_ref[rows, :] = stage_ref[lax.rem(i, 2), :, lanes]
+        stage_ref[rows, :] = logits
+        own_ref[rows, :] = stage_ref[rows, lanes]
+        for copy in copies(i):
+            copy.start()
         sum_ref[...] += folded(jnp.exp(logits))
 
     total_ref[...] = as_blocks(sum_ref[...])
-    stage_end(stage_ref, logits_out, sem_ref)
+    for i in range(ROWS // WIDE):
+        for copy in copies(i):
+            copy.wait()
 
 
 def received(got_ref):
@@ -227,7 +243,7 @@
 
 def third_kernel(
     me_ref, got_ref, kernel_ref, kept_ref, logits_ref, features_ref, weight_ref,
-    sent_ref, total_ref, before_ref, col_ref, mass_ref, scaled_ref, pair_ref,
+    sent_out, total_ref, before_ref, col_ref, mass_ref, scaled_ref, pair_ref, sent_ref, sem_ref,
 ):
     me = me_ref[0]
     got = received(got_ref)
@@ -266,12 +282,21 @@
     )
 
     def everywhere(rows):
-        return jnp.broadcast_to(rows[None], (64, 8, 128))
-
-    sent_ref[...] = jnp.concatenate(
-        [everywhere(change), grad_part.reshape(64, 8, 128), target_part.reshape(64, 8, 128), everywhere(extra)],
-        axis=1,
-    ).astype(bf16)
+        return jnp.broadcast_to(rows[None], (QUARTER, 8, 128))
+
+    def copy_out(i):
+        part = pl.ds(i * QUARTER, QUARTER)
+        return pltpu.make_async_copy(sent_ref.at[part], sent_out.at[part], sem_ref.at[i])
+
+    grad_part, target_part = grad_part.reshape(64, 8, 128), target_part.reshape(64, 8, 128)
+    for i in range(64 // QUARTER):
+        part = slice(i * QUARTER, (i + 1) * QUARTER)
+        sent_ref[part] = jnp.concatenate(
+            [everywhere(change), grad_part[part], target_part[part], everywhere(extra)], axis=1
+        ).astype(bf16)
+        copy_out(i).start()
+    for i in range(64 // QUARTER):
+        copy_out(i).wait()
 
 
 def weight_kernel(
@@ -294,7 +319,7 @@
 
 def final_kernel(
     me_ref, got_ref, features_ref, scale_ref, total_ref, before_ref, unit_ref, near_ref, targets_far,
-    features_out, loss_out, weight_out, change_ref, targets_ref, sem_ref,
+    features_out, loss_out, weight_out, change_ref, targets_ref, weight_ref, sem_ref, out_sem,
 ):
     def copy_in(i):
         rows = pl.ds(i * WIDE, WIDE)
@@ -314,12 +339,20 @@
     loss_out[...] = jnp.log(total_ref[pl.ds(me, 1), :]) - (1.0 - own) * (got[28:29] + got[29:30])
     units = unit_ref[pl.ds(pl.multiple_of(me * 64, 64), 64), :].astype(f32)
     moved = (units * as_row(change_ref[...])).astype(bf16)
+
+    def copy_out(i):
+        rows = pl.ds(i * WIDE, WIDE)
+        return pltpu.make_async_copy(weight_ref.at[:, rows], weight_out.at[:, rows], out_sem.at[i])
+
     for i in range(ROWS // WIDE):
         copy_in(i).wait()
         rows = pl.ds(i * WIDE, WIDE)
-        weight_out[:, rows] = near_ref[:, rows] + lax.dot_general(
+        weight_ref[:, rows] = near_ref[:, rows] + lax.dot_general(
             moved, targets_ref[rows, :], (((1,), (1,)), ((), ())), preferred_element_type=f32
         )
+        copy_out(i).start()
+    for i in range(ROWS // WIDE):
+        copy_out(i).wait()
 
 
 def shape(dims, dtype=f32):
@@ -327,34 +360,36 @@
 
 
 def on_device(teacher_features, student_features, teacher_weight, student_weight):
-    me = lax.axis_index("smp").astype(jnp.int32).reshape(1)
+    core = lax.rem(lax.axis_index("proto"), 2)
+    me = jnp.stack([lax.axis_index("smp"), core]).astype(jnp.int32)
     raw = jnp.concatenate([teacher_features.T, student_features.T], axis=0)
     raw, me = lax.optimization_barrier((raw, me))
     first = gathered(raw, ("yh", "yl", "z"))
     second = gathered(first, ("x",))
-    third = gathered(second, ("c",))
-
-    pair = pltpu.SemaphoreType.DMA((2,))
-    stage = pltpu.VMEM((2, TILE, B), f32)
+    other = lax.ppermute(second, "proto", [(i, i ^ 1) for i in range(64)])
+
+    stage = pltpu.VMEM((ROWS, B), f32)
+    wide_sems, near_sems = pltpu.SemaphoreType.DMA((ROWS // WIDE,)), pltpu.SemaphoreType.DMA((ROWS // TILE,))
     row, rows8 = pltpu.VMEM((1, B), f32), pltpu.VMEM((8, B), f32)
     rows8_small = pltpu.VMEM((8, 128), f32)
     matmul = dict(flops=2 * ROWS * B * D, moved=12 * 2**20, exps=ROWS * B)
     kernel, student_unit, sent_1, student_scale, features_own = call(
         first_kernel,
-        [pltpu.HBM((ROWS, B), f32), pltpu.HBM((D, B), bf16), shape((64, 8, 128), bf16), shape((8, 128)), shape((D, 128))],
-        [SMEM, VMEM, VMEM],
-        [ANY, ANY, VMEM, VMEM, VMEM],
-        [pltpu.VMEM((D, B), bf16), pltpu.VMEM((D, B), bf16), pltpu.VMEM((ROWS, B), f32), rows8,
-         pltpu.SemaphoreType.DMA((ROWS // WIDE,)), pltpu.SemaphoreType.DMA],
+        [pltpu.HBM((ROWS, B), f32), shape((D, B), bf16), pltpu.HBM((64, 8, 128), bf16), shape((8, 128)),
+         shape((D, 128))],
+        [SMEM, VMEM, VMEM, ANY],
+        [ANY, VMEM, ANY, VMEM, VMEM],
+        [pltpu.VMEM((D, B), bf16), pltpu.VMEM((ROWS, D), bf16), stage, pltpu.VMEM((64, 8, 128), bf16), rows8,
+         wide_sems, wide_sems, pltpu.SemaphoreType.DMA],
         **matmul,
-    )(me, third, teacher_weight)
+    )(me, second, other, far(teacher_weight))
     got_1 = sent_to_protos(sent_1)
     logits, logits_own, local_total = call(
         student_kernel,
-        [pltpu.HBM((ROWS, B), f32), shape((ROWS, 128)), shape((8, 128))],
+        [pltpu.HBM((ROWS, B), f32), pltpu.HBM((ROWS, 128), f32), shape((8, 128))],
         [SMEM, VMEM, VMEM],
-        [ANY, VMEM, VMEM],
-        [stage, rows8, pair],
+        [ANY, ANY, VMEM],
+        [stage, pltpu.VMEM((ROWS, 128), f32), rows8, wide_sems, wide_sems],
         **matmul,
     )(me, student_unit, student_weight)
     kernel_near, sent_2, kept = call(
@@ -362,17 +397,18 @@
         [pltpu.VMEM((ROWS, B), f32), shape((64, 24, 128), bf16), shape((8, 128))],
         [VMEM, ANY, VMEM],
         None,
-        [row, rows8, pltpu.SemaphoreType.DMA((ROWS // TILE,))],
+        [row, rows8, near_sems],
         flops=4 * ROWS * B,
         moved=8 * 2**20,
     )(got_1, far(kernel), local_total)
     got_2 = sent_to_protos(sent_2)
     sent_3, total, before = call(
         third_kernel,
-        [shape((64, 32, 128), bf16), shape((8, 128)), shape((8, 128))],
+        [pltpu.HBM((64, 32, 128), bf16), shape((8, 128)), shape((8, 128))],
         [SMEM] + [VMEM] * 6,
-        None,
-        [row, rows8, pltpu.VMEM((ROWS, 128), f32), pltpu.VMEM((ROWS, 256), bf16)],
+        [ANY, VMEM, VMEM],
+        [row, rows8, pltpu.VMEM((ROWS, 128), f32), pltpu.VMEM((ROWS, 256), bf16),
+         pltpu.VMEM((64, 32, 128), bf16), pltpu.SemaphoreType.DMA((64 // QUARTER,))],
         flops=2 * ROWS * 256 * D,
         moved=12 * 2**20,
         exps=ROWS * 128,
@@ -390,10 +426,10 @@
     )(me, far(kernel), far(logits), total, before, student_unit)
     grad_features, loss, grad_weight = call(
         final_kernel,
-        [shape((8, 128)), shape((1, 128)), shape((64, ROWS))],
+        [shape((8, 128)), shape((1, 128)), pltpu.HBM((64, ROWS), f32)],
         [SMEM] + [VMEM] * 7 + [ANY],
-        None,
-        [rows8_small, pltpu.VMEM((ROWS, B), bf16), pltpu.SemaphoreType.DMA((ROWS // WIDE,))],
+        [VMEM, VMEM, ANY],
+        [rows8_small, pltpu.VMEM((ROWS, B), bf16), pltpu.VMEM((64, ROWS), f32), wide_sems, wide_sems],
         flops=2 * ROWS * B * 64,
         moved=5 * 2**20,
     )(

time: 137 us -> 134 us (0.978)
  blocking collectives: 77.9 us -> 64.7 us
  starting transfers between devices: 11.7 us -> 18.2 us
  waiting for transfers between devices: 7.5 us -> 12.7 us
  local copies, waits for them, and re-layouts: 3.47 us -> 0.19 us
  Pallas kernels: 34.2 us -> 35.9 us
    all_to_all x3 -> x2, blocking collectives: 54.5 us -> 44.7 us  [gathered(): lax.all_to_all(copies, BOTH, 0, 0, tiled=True, axis_index_groups=group)]
    ppermute x0 -> x1, starting transfers between devices: none -> 6.53 us  [on_device(): other = lax.ppermute(second, 'proto', [(i, i ^ 1) for i in range(64)])]
    all_to_all x1, blocking collectives: 23.4 us -> 19.9 us  [sent_to_protos(): return lax.all_to_all(x, 'proto', 0, 0, tiled=True)]
    unnamed x16 -> x6, local copies, waits for them, and re-layouts: 3.03 us -> 0.01 us
    all_to_all x2, waiting for transfers between devices: 7.5 us -> 10.4 us  [sent_to_protos(): return lax.all_to_all(x, 'proto', 0, 0, tiled=True)]
    ppermute x0 -> x1, waiting for transfers between devices: none -> 2.26 us  [on_device(): other = lax.ppermute(second, 'proto', [(i, i ^ 1) for i in range(64)])]
  transfers between devices with their start and end apart: 2 -> 3, of which waited for: 2 -> 3; matrix products, arithmetic and copies ran while one was open for 0% -> 0% of each run, Pallas kernels for 13% -> 13%
where the time goes in v6:
time: 134 us; the launch traced here: 133 us
  blocking collectives  64.7 us (48%)
  Pallas kernels  35.9 us (27%)
  starting transfers between devices  18.2 us (14%)
  waiting for transfers between devices  12.7 us (9%)
    all_to_all x2, blocking collectives, gathered(): lax.all_to_all(copies, BOTH, 0, 0, tiled=True, axis_index_groups=group)  44.7 us
    all_to_all x1, blocking collectives, sent_to_protos(): return lax.all_to_all(x, 'proto', 0, 0, tiled=True)  19.9 us
    all_to_all x2, starting transfers between devices, sent_to_protos(): return lax.all_to_all(x, 'proto', 0, 0, tiled=True)  11.7 us
    pallas_call x1, Pallas kernels, on_device(): streamed(weight_kernel, [shape((64, ROWS)), pltpu.HBM((ROWS, B), bf16)],...  11.7 us
    all_to_all x2, waiting for transfers between devices, sent_to_protos(): return lax.all_to_all(x, 'proto', 0, 0, tiled=True)  10.4 us
    pallas_call x1, Pallas kernels, on_device(): call(first_kernel, [pltpu.HBM((ROWS, B), f32), shape((D, B), bf16), pltpu...  6.59 us
    ppermute x1, starting transfers between devices, on_device(): other = lax.ppermute(second, 'proto', [(i, i ^ 1) for i in range(64)])  6.53 us
    pallas_call x1, Pallas kernels, on_device(): call(student_kernel, [pltpu.HBM((ROWS, B), f32), pltpu.HBM((ROWS, 128), f...  5.02 us
  transfers between devices with their start and end apart: 3, of which 3 were waited for; matrix products, arithmetic and copies ran while one was open for 0% of the time, Pallas kernels for 13%

profile of v6, /device:TPU:1, one launch (start us, length us, event | category | flops | bytes accessed | tf_op | source)
XLA Modules:
  0.0 133.2 jit_solution(14692772305952388366)
XLA Ops:
  0.6 0.0 copy-start
  0.6 0.1 pad_add_fusion.me_ref
  0.7 0.8 pad_maximum_fusion
  1.6 29.5 %all_to_all.25 = bf16[64,16,128]{2,1,0:T(8,128)(2,1)S(1)} all-to-all(bf16[64,16,128]{2,1,0:T(8,128)(2,1)S(1)} %broadcast_in_dim.4), channel_id=1, replica_groups={{0,2,4,6,8,10,12,14,16,18,20,22,24,26,28,30,32,34,36,38,40,42,44,46,48,..., dimensions={0} | all-to-all | bytes 524288 | tf_op jit(solution)/shard_map/all_to_all | solution.py:39
  31.1 0.1 broadcast_in_dim.5
  31.2 15.2 %all_to_all.26.own_ref = bf16[4,64,16,128]{3,2,1,0:T(8,128)(2,1)S(1)} all-to-all(bf16[4,64,16,128]{3,2,1,0:T(8,128)(2,1)S(1)} %broadcast_in_dim.5), channel_id=1, replica_groups={{0,128,256,384},{1,129,257,385},{2,130,258,386},{3,131,259,387},{4,132,..., dimensions={0} | all-to-all | bytes 2097152 | tf_op jit(solution)/shard_map/all_to_all | solution.py:39
  46.5 6.5 %collective-permute-start = (bf16[4,64,16,128]{3,2,1,0:T(8,128)(2,1)S(1)}, bf16[4,64,16,128]{3,2,1,0:T(8,128)(2,1)S(1)}, u32[]{:S(2)}, u32[]{:S(2)}) collective-permute-start(bf16[4,64,16,128]{3,2,1,0:T(8,128)(2,1)S(1)} %all_to_all.26.own_ref), channel_id=1, source_target_pairs={{0,1},{1,0},{2,3},{3,2},{4,5},{5,4},{6,7},{7,6},{8,9},{9,8},{10,11... | collective-permute-start | bytes 3145736 | tf_op jit(solution)/shard_map/ppermute | solution.py:369
  53.0 2.3 %collective-permute-done.other_ref = bf16[4,64,16,128]{3,2,1,0:T(8,128)(2,1)S(1)} collective-permute-done((bf16[4,64,16,128]{3,2,1,0:T(8,128)(2,1)S(1)}, bf16[4,64,16,128]{3,2,1,0:T(8,128)(2,1)S(1)}, u32[]{:S(2)}, u32[]{:S(2)}) %collective-permute-start) | collective-permute-done | bytes 1048608 | tf_op jit(solution)/shard_map/ppermute | solution.py:369
  55.3 6.6 %shard_map.67 = (f32[2048,1024]{1,0:T(8,128)}, bf16[512,1024]{1,0:T(8,128)(2,1)S(1)}, bf16[64,8,128]{2,1,0:T(8,128)(2,1)}, f32[8,128]{1,0:T(8,128)S(1)}, f32[512,128]{1,0:T(8,128)S(1)}) custom-call(s32[2]{0:T(128)S(1)} %pad_add_fusion.me_ref, bf16[4,64,16,128]{3,2,1,0:T(8,128)(2,1)S(1)} %all_to_all.26.own_ref, ...), custom_call_target="tpu_custom_call" | custom-call | flops 2147483648 | bytes 12582912 | tf_op jit(solution)/shard_map/pallas_call | solution.py:376
  61.9 5.6 %all-to-all-start.2 = ((bf16[64,8,128]{2,1,0:T(8,128)(2,1)}), bf16[64,8,128]{2,1,0:T(8,128)(2,1)S(1)}, u32[]{:S(2)}, u32[]{:S(2)}) async-start(bf16[64,8,128]{2,1,0:T(8,128)(2,1)} %get-tuple-element.26), calls=%async_computation.2 | async-start | bytes 262144 | tf_op jit(solution)/shard_map/all_to_all | solution.py:43
  67.5 0.0 copy-done
  67.5 5.0 %shard_map.68 = (f32[2048,1024]{1,0:T(8,128)}, f32[2048,128]{1,0:T(8,128)}, f32[8,128]{1,0:T(8,128)S(1)}) custom-call(s32[2]{0:T(128)S(1)} %pad_add_fusion.me_ref, bf16[512,1024]{1,0:T(8,128)(2,1)S(1)} %get-tuple-element.28.unit_ref, bf16[2048,512]{1,0:T(8,128)(2,1)S(1)} %copy-done), custom_call_target="tpu_custom_call" | custom-call | flops 2147483648 | bytes 12582912 | tf_op jit(solution)/shard_map/pallas_call | solution.py:387
  72.5 4.9 %all-to-all-done.2.got_ref = bf16[64,8,128]{2,1,0:T(8,128)(2,1)S(1)} async-done(((bf16[64,8,128]{2,1,0:T(8,128)(2,1)}), bf16[64,8,128]{2,1,0:T(8,128)(2,1)S(1)}, u32[]{:S(2)}, u32[]{:S(2)}) %all-to-all-start.2) | async-done | bytes 131104 | tf_op jit(solution)/shard_map/all_to_all | solution.py:43
  77.5 0.0 copy-start.1
  77.5 3.8 %shard_map.69 = (f32[2048,1024]{1,0:T(8,128)S(1)}, bf16[64,24,128]{2,1,0:T(8,128)(2,1)S(1)}, f32[8,128]{1,0:T(8,128)S(1)}) custom-call(bf16[64,8,128]{2,1,0:T(8,128)(2,1)S(1)} %all-to-all-done.2.got_ref, f32[2048,1024]{1,0:T(8,128)} %get-tuple-element.27.far_ref.kernel_ref, f32[8,128]{1,0:T(8,128)S(1)} %get-tuple-element.29.total_ref), custom_call_target="tpu_custom_call" | custom-call | flops 8388608 | bytes 8388608 | tf_op jit(solution)/shard_map/pallas_call | solution.py:395
  81.2 19.9 %all_to_all.27.got_ref = bf16[64,24,128]{2,1,0:T(8,128)(2,1)S(1)} all-to-all(bf16[64,24,128]{2,1,0:T(8,128)(2,1)S(1)} %get-tuple-element.30), channel_id=1, replica_groups=mesh['smp'=8,'proto'=64] {'proto'}, dimensions={0} | all-to-all | bytes 786432 | tf_op jit(solution)/shard_map/all_to_all | solution.py:43
  101.2 0.0 copy-done.1
  101.2 4.0 %shard_map.70 = (bf16[64,32,128]{2,1,0:T(8,128)(2,1)}, f32[8,128]{1,0:T(8,128)S(1)}, f32[8,128]{1,0:T(8,128)S(1)}) custom-call(s32[2]{0:T(128)S(1)} %pad_add_fusion.me_ref, bf16[64,24,128]{2,1,0:T(8,128)(2,1)S(1)} %all_to_all.27.got_ref, f32[2048,1024]{1,0:T(8,128)S(1)} %get-tuple-element.31.kernel_ref, f32[8,128]{1,0:T(8,128)S(1)} %get-tuple-element.32.kept_ref, ...), custom_call_target="tpu_custom_call" | custom-call | flops 536870912 | bytes 12582912 | tf_op jit(solution)/shard_map/pallas_call | solution.py:405
  105.1 6.1 %all-to-all-start.4 = ((bf16[64,32,128]{2,1,0:T(8,128)(2,1)}), bf16[64,32,128]{2,1,0:T(8,128)(2,1)S(1)}, u32[]{:S(2)}, u32[]{:S(2)}) async-start(bf16[64,32,128]{2,1,0:T(8,128)(2,1)} %get-tuple-element.35), calls=%async_computation.4 | async-start | bytes 1048576 | tf_op jit(solution)/shard_map/all_to_all | solution.py:43
  111.2 0.0 copy-start.2
  111.3 11.7 %shard_map.71 = (f32[64,2048]{1,0:T(8,128)S(1)}, bf16[2048,1024]{1,0:T(8,128)(2,1)}) custom-call(s32[2]{0:T(128)S(1)} %pad_add_fusion.me_ref, f32[2048,1024]{1,0:T(8,128)} %get-tuple-element.27.far_ref.kernel_ref, f32[2048,1024]{1,0:T(8,128)} %get-tuple-element.39.logits_ref, f32[8,128]{1,0:T(8,128)S(1)} %get-tuple-element.37.total_ref, ...), custom_call_target="tpu_custom_call" | custom-call | flops 268435456 | bytes 22020096 | tf_op jit(solution)/shard_map/pallas_call | solution.py:417
  122.9 5.5 %all-to-all-done.4.got_ref = bf16[64,32,128]{2,1,0:T(8,128)(2,1)S(1)} async-done(((bf16[64,32,128]{2,1,0:T(8,128)(2,1)}), bf16[64,32,128]{2,1,0:T(8,128)(2,1)S(1)}, u32[]{:S(2)}, u32[]{:S(2)}) %all-to-all-start.4) | async-done | bytes 524320 | tf_op jit(solution)/shard_map/all_to_all | solution.py:43
  128.4 0.0 copy-done.2
  128.4 4.8 %shard_map.72 = (f32[8,128]{1,0:T(8,128)}, f32[1,128]{1,0:T(1,128)}, f32[64,2048]{1,0:T(8,128)}) custom-call(s32[2]{0:T(128)S(1)} %pad_add_fusion.me_ref, bf16[64,32,128]{2,1,0:T(8,128)(2,1)S(1)} %all-to-all-done.4.got_ref, bf16[8,128]{1,0:T(8,128)(2,1)S(1)} %bitcast.8, f32[8,128]{1,0:T(8,128)S(1)} %get-tuple-element.36.scale_ref, ...), custom_call_target="tpu_custom_call" | custom-call | flops 268435456 | bytes 5242880 | tf_op jit(solution)/shard_map/pallas_call | solution.py:427
  (1 shorter events, 0.0 us)
Async XLA Ops:
  0.6 66.8 %copy-start = (bf16[2048,512]{1,0:T(8,128)(2,1)S(1)}, bf16[2048,512]{1,0:T(8,128)(2,1)}, u32[]{:S(2)}) copy-start(bf16[2048,512]{1,0:T(8,128)(2,1)} %weight_ref.3) | copy-start | bytes 6291460
  46.5 8.8 %collective-permute-start = (bf16[4,64,16,128]{3,2,1,0:T(8,128)(2,1)S(1)}, bf16[4,64,16,128]{3,2,1,0:T(8,128)(2,1)S(1)}, u32[]{:S(2)}, u32[]{:S(2)}) collective-permute-start(bf16[4,64,16,128]{3,2,1,0:T(8,128)(2,1)S(1)} %all_to_all.26.own_ref), channel_id=1, source_target_pairs={{0,1},{1,0},{2,3},{3,2},{4,5},{5,4},{6,7},{7,6},{8,9},{9,8},{10,11... | collective-permute-start | bytes 3145736 | tf_op jit(solution)/shard_map/ppermute | solution.py:369
  61.9 15.6 %all-to-all-start.2 = ((bf16[64,8,128]{2,1,0:T(8,128)(2,1)}), bf16[64,8,128]{2,1,0:T(8,128)(2,1)S(1)}, u32[]{:S(2)}, u32[]{:S(2)}) async-start(bf16[64,8,128]{2,1,0:T(8,128)(2,1)} %get-tuple-element.26), calls=%async_computation.2 | async-start | bytes 262144 | tf_op jit(solution)/shard_map/all_to_all | solution.py:43
  77.5 23.7 %copy-start.1 = (f32[2048,128]{1,0:T(8,128)S(1)}, f32[2048,128]{1,0:T(8,128)}, u32[]{:S(2)}) copy-start(f32[2048,128]{1,0:T(8,128)} %get-tuple-element.33.logits_ref) | copy-start | bytes 3145732
  105.1 23.2 %all-to-all-start.4 = ((bf16[64,32,128]{2,1,0:T(8,128)(2,1)}), bf16[64,32,128]{2,1,0:T(8,128)(2,1)S(1)}, u32[]{:S(2)}, u32[]{:S(2)}) async-start(bf16[64,32,128]{2,1,0:T(8,128)(2,1)} %get-tuple-element.35), calls=%async_computation.4 | async-start | bytes 1048576 | tf_op jit(solution)/shard_map/all_to_all | solution.py:43
  111.2 17.1 %copy-start.2 = (bf16[128,8]{0,1:T(8,128)(2,1)S(1)}, bf16[128,8]{0,1:T(8,128)(2,1)}, u32[]{:S(2)}) copy-start(bf16[128,8]{0,1:T(8,128)(2,1)} %param.5) | copy-start | bytes 6148

commit v7 on v6

--- a/solution.py
+++ b/solution.py
@@ -16,7 +16,6 @@
 SHARE = 1.0 / (1024 * 0.1)
 TILE = 256
 WIDE = 512
-QUARTER = 16
 BLOCKS = 8
 f32, bf16 = jnp.float32, jnp.bfloat16
 VMEM = pl.BlockSpec(memory_space=pltpu.VMEM)
@@ -115,18 +114,22 @@
     return jnp.concatenate([blocks[s : s + 1, :] for s in range(BLOCKS)], axis=1)
 
 
+def fetch_kernel(far_ref, near_ref, sem_ref):
+    copies = []
+    for i in range(ROWS // WIDE):
+        rows = pl.ds(i * WIDE, WIDE)
+        copies.append(pltpu.make_async_copy(far_ref.at[rows], near_ref.at[rows], sem_ref.at[i]))
+    for copy in copies:
+        copy.start()
+    for copy in copies:
+        copy.wait()
+
+
 def first_kernel(
-    me_ref, own_ref, other_ref, weight_far, kernel_out, unit_ref, sent_out, scale_ref, features_ref,
-    teacher_ref, weight_ref, stage_ref, sent_ref, mass_ref, sem_ref, weight_sem, sent_sem,
+    me_ref, own_ref, other_ref, weight_ref, kernel_out, unit_ref, sent_out, scale_ref, features_ref,
+    teacher_ref, stage_ref, sent_ref, mass_ref, sem_ref, sent_sem,
 ):
     me, core = me_ref[0], me_ref[1]
-
-    def copy_in(i):
-        rows = pl.ds(pl.multiple_of(i * WIDE, WIDE), WIDE)
-        return pltpu.make_async_copy(weight_far.at[rows], weight_ref.at[rows], weight_sem.at[i])
-
-    for i in range(ROWS // WIDE):
-        copy_in(i).start()
 
     def by_core(body):
         @pl.when(core == 0)
@@ -159,7 +162,6 @@
 
     @pl.loop(0, ROWS // WIDE)
     def _(i):
-        copy_in(i).wait()
         rows = pl.ds(pl.multiple_of(i * WIDE, WIDE), WIDE)
         kernel = jnp.exp(
             jnp.dot(weight_ref[rows, :], teacher_ref[...], preferred_element_type=f32) * (1.0 / TEACHER_TEMP)
@@ -243,7 +245,7 @@
 
 def third_kernel(
     me_ref, got_ref, kernel_ref, kept_ref, logits_ref, features_ref, weight_ref,
-    sent_out, total_ref, before_ref, col_ref, mass_ref, scaled_ref, pair_ref, sent_ref, sem_ref,
+    sent_ref, total_ref, before_ref, col_ref, mass_ref, scaled_ref, pair_ref,
 ):
     me = me_ref[0]
     got = received(got_ref)
@@ -282,21 +284,12 @@
     )
 
     def everywhere(rows):
-        return jnp.broadcast_to(rows[None], (QUARTER, 8, 128))
-
-    def copy_out(i):
-        part = pl.ds(i * QUARTER, QUARTER)
-        return pltpu.make_async_copy(sent_ref.at[part], sent_out.at[part], sem_ref.at[i])
-
-    grad_part, target_part = grad_part.reshape(64, 8, 128), target_part.reshape(64, 8, 128)
-    for i in range(64 // QUARTER):
-        part = slice(i * QUARTER, (i + 1) * QUARTER)
-        sent_ref[part] = jnp.concatenate(
-            [everywhere(change), grad_part[part], target_part[part], everywhere(extra)], axis=1
-        ).astype(bf16)
-        copy_out(i).start()
-    for i in range(64 // QUARTER):
-        copy_out(i).wait()
+        return jnp.broadcast_to(rows[None], (64, 8, 128))
+
+    sent_ref[...] = jnp.concatenate(
+        [everywhere(change), grad_part.reshape(64, 8, 128), target_part.reshape(64, 8, 128), everywhere(extra)],
+        axis=1,
+    ).astype(bf16)
 
 
 def weight_kernel(
@@ -319,7 +312,7 @@
 
 def final_kernel(
     me_ref, got_ref, features_ref, scale_ref, total_ref, before_ref, unit_ref, near_ref, targets_far,
-    features_out, loss_out, weight_out, change_ref, targets_ref, weight_ref, sem_ref, out_sem,
+    features_out, loss_out, weight_out, change_ref, targets_ref, sem_ref,
 ):
     def copy_in(i):
         rows = pl.ds(i * WIDE, WIDE)
@@ -339,20 +332,12 @@
     loss_out[...] = jnp.log(total_ref[pl.ds(me, 1), :]) - (1.0 - own) * (got[28:29] + got[29:30])
     units = unit_ref[pl.ds(pl.multiple_of(me * 64, 64), 64), :].astype(f32)
     moved = (units * as_row(change_ref[...])).astype(bf16)
-
-    def copy_out(i):
-        rows = pl.ds(i * WIDE, WIDE)
-        return pltpu.make_async_copy(weight_ref.at[:, rows], weight_out.at[:, rows], out_sem.at[i])
-
     for i in range(ROWS // WIDE):
         copy_in(i).wait()
         rows = pl.ds(i * WIDE, WIDE)
-        weight_ref[:, rows] = near_ref[:, rows] + lax.dot_general(
+        weight_out[:, rows] = near_ref[:, rows] + lax.dot_general(
             moved, targets_ref[rows, :], (((1,), (1,)), ((), ())), preferred_element_type=f32
         )
-        copy_out(i).start()
-    for i in range(ROWS // WIDE):
-        copy_out(i).wait()
 
 
 def shape(dims, dtype=f32):
@@ -366,6 +351,7 @@
     raw, me = lax.optimization_barrier((raw, me))
     first = gathered(raw, ("yh", "yl", "z"))
     second = gathered(first, ("x",))
+    second, teacher_weight = lax.optimization_barrier((second, teacher_weight))
     other = lax.ppermute(second, "proto", [(i, i ^ 1) for i in range(64)])
 
     stage = pltpu.VMEM((ROWS, B), f32)
@@ -373,16 +359,19 @@
     row, rows8 = pltpu.VMEM((1, B), f32), pltpu.VMEM((8, B), f32)
     rows8_small = pltpu.VMEM((8, 128), f32)
     matmul = dict(flops=2 * ROWS * B * D, moved=12 * 2**20, exps=ROWS * B)
+    (weight_near,) = call(
+        fetch_kernel, [pltpu.VMEM((ROWS, D), bf16)], [ANY], None, [wide_sems], moved=4 * 2**20
+    )(far(teacher_weight))
     kernel, student_unit, sent_1, student_scale, features_own = call(
         first_kernel,
         [pltpu.HBM((ROWS, B), f32), shape((D, B), bf16), pltpu.HBM((64, 8, 128), bf16), shape((8, 128)),
          shape((D, 128))],
-        [SMEM, VMEM, VMEM, ANY],
+        [SMEM, VMEM, VMEM, VMEM],
         [ANY, VMEM, ANY, VMEM, VMEM],
-        [pltpu.VMEM((D, B), bf16), pltpu.VMEM((ROWS, D), bf16), stage, pltpu.VMEM((64, 8, 128), bf16), rows8,
-         wide_sems, wide_sems, pltpu.SemaphoreType.DMA],
+        [pltpu.VMEM((D, B), bf16), stage, pltpu.VMEM((64, 8, 128), bf16), rows8, wide_sems,
+         pltpu.SemaphoreType.DMA],
         **matmul,
-    )(me, second, other, far(teacher_weight))
+    )(me, second, other, weight_near)
     got_1 = sent_to_protos(sent_1)
     logits, logits_own, local_total = call(
         student_kernel,
@@ -404,11 +393,10 @@
     got_2 = sent_to_protos(sent_2)
     sent_3, total, before = call(
         third_kernel,
-        [pltpu.HBM((64, 32, 128), bf16), shape((8, 128)), shape((8, 128))],
+        [shape((64, 32, 128), bf16), shape((8, 128)), shape((8, 128))],
         [SMEM] + [VMEM] * 6,
-        [ANY, VMEM, VMEM],
-        [row, rows8, pltpu.VMEM((ROWS, 128), f32), pltpu.VMEM((ROWS, 256), bf16),
-         pltpu.VMEM((64, 32, 128), bf16), pltpu.SemaphoreType.DMA((64 // QUARTER,))],
+        None,
+        [row, rows8, pltpu.VMEM((ROWS, 128), f32), pltpu.VMEM((ROWS, 256), bf16)],
         flops=2 * ROWS * 256 * D,
         moved=12 * 2**20,
         exps=ROWS * 128,
@@ -426,10 +414,10 @@
     )(me, far(kernel), far(logits), total, before, student_unit)
     grad_features, loss, grad_weight = call(
         final_kernel,
-        [shape((8, 128)), shape((1, 128)), pltpu.HBM((64, ROWS), f32)],
+        [shape((8, 128)), shape((1, 128)), shape((64, ROWS))],
         [SMEM] + [VMEM] * 7 + [ANY],
-        [VMEM, VMEM, ANY],
-        [rows8_small, pltpu.VMEM((ROWS, B), bf16), pltpu.VMEM((64, ROWS), f32), wide_sems, wide_sems],
+        None,
+        [rows8_small, pltpu.VMEM((ROWS, B), bf16), wide_sems],
         flops=2 * ROWS * B * 64,
         moved=5 * 2**20,
     )(

time: 134 us -> 133 us (level)
  waiting for transfers between devices: 12.7 us -> 11.1 us
    ppermute x1, waiting for transfers between devices: 2.26 us -> 0.69 us  [on_device(): other = lax.ppermute(second, 'proto', [(i, i ^ 1) for i in range(64)])]
    pallas_call x2 -> x3, Pallas kernels: 8.81 us -> 9.09 us  [the longest x1 4.36 us: on_device(): call(final_kernel, [shape((8, 128)), shape((1, 128)), shape((64, ROWS))],...]
  transfers between devices with their start and end apart: 3 -> 3, of which waited for: 3 -> 3; matrix products, arithmetic and copies ran while one was open for 0% -> 0% of each run, Pallas kernels for 13% -> 14%
where the time goes in v7:
time: 133 us; the launch traced here: 132 us
  blocking collectives  64.7 us (49%)
  Pallas kernels  35.6 us (27%)
  starting transfers between devices  18.2 us (14%)
  waiting for transfers between devices  11.1 us (8%)
    all_to_all x2, blocking collectives, gathered(): lax.all_to_all(copies, BOTH, 0, 0, tiled=True, axis_index_groups=group)  44.7 us
    all_to_all x1, blocking collectives, sent_to_protos(): return lax.all_to_all(x, 'proto', 0, 0, tiled=True)  19.9 us
    all_to_all x2, starting transfers between devices, sent_to_protos(): return lax.all_to_all(x, 'proto', 0, 0, tiled=True)  11.7 us
    pallas_call x1, Pallas kernels, on_device(): streamed(weight_kernel, [shape((64, ROWS)), pltpu.HBM((ROWS, B), bf16)],...  11.7 us
    all_to_all x2, waiting for transfers between devices, sent_to_protos(): return lax.all_to_all(x, 'proto', 0, 0, tiled=True)  10.4 us
    ppermute x1, starting transfers between devices, on_device(): other = lax.ppermute(second, 'proto', [(i, i ^ 1) for i in range(64)])  6.53 us
    pallas_call x1, Pallas kernels, on_device(): call(first_kernel, [pltpu.HBM((ROWS, B), f32), shape((D, B), bf16), pltpu...  6.06 us
    pallas_call x1, Pallas kernels, on_device(): call(student_kernel, [pltpu.HBM((ROWS, B), f32), pltpu.HBM((ROWS, 128), f...  5.01 us
  transfers between devices with their start and end apart: 3, of which 3 were waited for; matrix products, arithmetic and copies ran while one was open for 0% of the time, Pallas kernels for 14%

profile of v7, /device:TPU:1, one launch (start us, length us, event | category | flops | bytes accessed | tf_op | source)
XLA Modules:
  0.0 132.1 jit_solution(12680069554527989496)
XLA Ops:
  0.6 0.1 pad_add_fusion.me_ref
  0.7 0.7 pad_maximum_fusion
  1.5 29.5 %all_to_all.25 = bf16[64,16,128]{2,1,0:T(8,128)(2,1)S(1)} all-to-all(bf16[64,16,128]{2,1,0:T(8,128)(2,1)S(1)} %broadcast_in_dim.4), channel_id=1, replica_groups={{0,2,4,6,8,10,12,14,16,18,20,22,24,26,28,30,32,34,36,38,40,42,44,46,48,..., dimensions={0} | all-to-all | bytes 524288 | tf_op jit(solution)/shard_map/all_to_all | solution.py:38
  30.9 0.1 broadcast_in_dim.5
  31.1 15.2 %all_to_all.26.own_ref = bf16[4,64,16,128]{3,2,1,0:T(8,128)(2,1)S(1)} all-to-all(bf16[4,64,16,128]{3,2,1,0:T(8,128)(2,1)S(1)} %broadcast_in_dim.5), channel_id=1, replica_groups={{0,128,256,384},{1,129,257,385},{2,130,258,386},{3,131,259,387},{4,132,..., dimensions={0} | all-to-all | bytes 2097152 | tf_op jit(solution)/shard_map/all_to_all | solution.py:38
  46.3 6.5 %collective-permute-start = (bf16[4,64,16,128]{3,2,1,0:T(8,128)(2,1)S(1)}, bf16[4,64,16,128]{3,2,1,0:T(8,128)(2,1)S(1)}, u32[]{:S(2)}, u32[]{:S(2)}) collective-permute-start(bf16[4,64,16,128]{3,2,1,0:T(8,128)(2,1)S(1)} %all_to_all.26.own_ref), channel_id=1, source_target_pairs={{0,1},{1,0},{2,3},{3,2},{4,5},{5,4},{6,7},{7,6},{8,9},{9,8},{10,11... | collective-permute-start | bytes 3145736 | tf_op jit(solution)/shard_map/ppermute | solution.py:355
  52.8 1.6 %shard_map.67.weight_ref = bf16[2048,512]{1,0:T(8,128)(2,1)S(1)} custom-call(bf16[2048,512]{1,0:T(8,128)(2,1)} %far_ref), custom_call_target="tpu_custom_call" | custom-call | bytes 4194304 | tf_op jit(solution)/shard_map/pallas_call | solution.py:362
  54.4 0.0 copy-start
  54.4 0.7 collective-permute-done.other_ref
  55.1 6.1 %shard_map.68 = (f32[2048,1024]{1,0:T(8,128)}, bf16[512,1024]{1,0:T(8,128)(2,1)S(1)}, bf16[64,8,128]{2,1,0:T(8,128)(2,1)}, f32[8,128]{1,0:T(8,128)S(1)}, f32[512,128]{1,0:T(8,128)S(1)}) custom-call(s32[2]{0:T(128)S(1)} %pad_add_fusion.me_ref, bf16[4,64,16,128]{3,2,1,0:T(8,128)(2,1)S(1)} %all_to_all.26.own_ref, ...), custom_call_target="tpu_custom_call" | custom-call | flops 2147483648 | bytes 12582912 | tf_op jit(solution)/shard_map/pallas_call | solution.py:365
  61.2 5.6 %all-to-all-start.2 = ((bf16[64,8,128]{2,1,0:T(8,128)(2,1)}), bf16[64,8,128]{2,1,0:T(8,128)(2,1)S(1)}, u32[]{:S(2)}, u32[]{:S(2)}) async-start(bf16[64,8,128]{2,1,0:T(8,128)(2,1)} %get-tuple-element.30), calls=%async_computation.2 | async-start | bytes 262144 | tf_op jit(solution)/shard_map/all_to_all | solution.py:42
  66.8 0.0 copy-done
  66.8 5.0 %shard_map.69 = (f32[2048,1024]{1,0:T(8,128)}, f32[2048,128]{1,0:T(8,128)}, f32[8,128]{1,0:T(8,128)S(1)}) custom-call(s32[2]{0:T(128)S(1)} %pad_add_fusion.me_ref, bf16[512,1024]{1,0:T(8,128)(2,1)S(1)} %get-tuple-element.32.unit_ref, bf16[2048,512]{1,0:T(8,128)(2,1)S(1)} %copy-done), custom_call_target="tpu_custom_call" | custom-call | flops 2147483648 | bytes 12582912 | tf_op jit(solution)/shard_map/pallas_call | solution.py:376
  71.8 5.0 %all-to-all-done.2.got_ref = bf16[64,8,128]{2,1,0:T(8,128)(2,1)S(1)} async-done(((bf16[64,8,128]{2,1,0:T(8,128)(2,1)}), bf16[64,8,128]{2,1,0:T(8,128)(2,1)S(1)}, u32[]{:S(2)}, u32[]{:S(2)}) %all-to-all-start.2) | async-done | bytes 131104 | tf_op jit(solution)/shard_map/all_to_all | solution.py:42
  76.8 0.0 copy-start.1
  76.8 3.8 %shard_map.70 = (f32[2048,1024]{1,0:T(8,128)S(1)}, bf16[64,24,128]{2,1,0:T(8,128)(2,1)S(1)}, f32[8,128]{1,0:T(8,128)S(1)}) custom-call(bf16[64,8,128]{2,1,0:T(8,128)(2,1)S(1)} %all-to-all-done.2.got_ref, f32[2048,1024]{1,0:T(8,128)} %get-tuple-element.31.far_ref.kernel_ref, f32[8,128]{1,0:T(8,128)S(1)} %get-tuple-element.33.total_ref), custom_call_target="tpu_custom_call" | custom-call | flops 8388608 | bytes 8388608 | tf_op jit(solution)/shard_map/pallas_call | solution.py:384
  80.5 19.9 %all_to_all.27.got_ref = bf16[64,24,128]{2,1,0:T(8,128)(2,1)S(1)} all-to-all(bf16[64,24,128]{2,1,0:T(8,128)(2,1)S(1)} %get-tuple-element.34), channel_id=1, replica_groups=mesh['smp'=8,'proto'=64] {'proto'}, dimensions={0} | all-to-all | bytes 786432 | tf_op jit(solution)/shard_map/all_to_all | solution.py:42
  100.5 0.0 copy-done.1
  100.5 3.2 %shard_map.71 = (bf16[64,32,128]{2,1,0:T(8,128)(2,1)S(1)}, f32[8,128]{1,0:T(8,128)S(1)}, f32[8,128]{1,0:T(8,128)S(1)}) custom-call(s32[2]{0:T(128)S(1)} %pad_add_fusion.me_ref, bf16[64,24,128]{2,1,0:T(8,128)(2,1)S(1)} %all_to_all.27.got_ref, f32[2048,1024]{1,0:T(8,128)S(1)} %get-tuple-element.35.kernel_ref, f32[8,128]{1,0:T(8,128)S(1)} %get-tuple-element.36.kept_ref, ...), custom_call_target="tpu_custom_call" | custom-call | flops 536870912 | bytes 12582912 | tf_op jit(solution)/shard_map/pallas_call | solution.py:394
  103.7 0.0 copy-start.2
  103.7 0.8 copy-done.2
  104.5 6.1 %all-to-all-start.4 = ((bf16[64,32,128]{2,1,0:T(8,128)(2,1)}), bf16[64,32,128]{2,1,0:T(8,128)(2,1)S(1)}, u32[]{:S(2)}, u32[]{:S(2)}) async-start(bf16[64,32,128]{2,1,0:T(8,128)(2,1)} %copy-done.2), calls=%async_computation.4 | async-start | bytes 1048576 | tf_op jit(solution)/shard_map/all_to_all | solution.py:42
  110.6 0.0 copy-start.3
  110.6 11.7 %shard_map.72 = (f32[64,2048]{1,0:T(8,128)S(1)}, bf16[2048,1024]{1,0:T(8,128)(2,1)}) custom-call(s32[2]{0:T(128)S(1)} %pad_add_fusion.me_ref, f32[2048,1024]{1,0:T(8,128)} %get-tuple-element.31.far_ref.kernel_ref, f32[2048,1024]{1,0:T(8,128)} %get-tuple-element.43.logits_ref, f32[8,128]{1,0:T(8,128)S(1)} %get-tuple-element.41.total_ref, ...), custom_call_target="tpu_custom_call" | custom-call | flops 268435456 | bytes 22020096 | tf_op jit(solution)/shard_map/pallas_call | solution.py:405
  122.2 5.5 %all-to-all-done.4.got_ref = bf16[64,32,128]{2,1,0:T(8,128)(2,1)S(1)} async-done(((bf16[64,32,128]{2,1,0:T(8,128)(2,1)}), bf16[64,32,128]{2,1,0:T(8,128)(2,1)S(1)}, u32[]{:S(2)}, u32[]{:S(2)}) %all-to-all-start.4) | async-done | bytes 524320 | tf_op jit(solution)/shard_map/all_to_all | solution.py:42
  127.7 0.0 copy-done.3
  127.7 4.4 %shard_map.73 = (f32[8,128]{1,0:T(8,128)}, f32[1,128]{1,0:T(1,128)}, f32[64,2048]{1,0:T(8,128)}) custom-call(s32[2]{0:T(128)S(1)} %pad_add_fusion.me_ref, bf16[64,32,128]{2,1,0:T(8,128)(2,1)S(1)} %all-to-all-done.4.got_ref, bf16[8,128]{1,0:T(8,128)(2,1)S(1)} %bitcast.8, f32[8,128]{1,0:T(8,128)S(1)} %get-tuple-element.40.scale_ref, ...), custom_call_target="tpu_custom_call" | custom-call | flops 268435456 | bytes 5242880 | tf_op jit(solution)/shard_map/pallas_call | solution.py:415
  (1 shorter events, 0.0 us)
Async XLA Ops:
  46.3 8.8 %collective-permute-start = (bf16[4,64,16,128]{3,2,1,0:T(8,128)(2,1)S(1)}, bf16[4,64,16,128]{3,2,1,0:T(8,128)(2,1)S(1)}, u32[]{:S(2)}, u32[]{:S(2)}) collective-permute-start(bf16[4,64,16,128]{3,2,1,0:T(8,128)(2,1)S(1)} %all_to_all.26.own_ref), channel_id=1, source_target_pairs={{0,1},{1,0},{2,3},{3,2},{4,5},{5,4},{6,7},{7,6},{8,9},{9,8},{10,11... | collective-permute-start | bytes 3145736 | tf_op jit(solution)/shard_map/ppermute | solution.py:355
  54.4 12.4 %copy-start = (bf16[2048,512]{1,0:T(8,128)(2,1)S(1)}, bf16[2048,512]{1,0:T(8,128)(2,1)}, u32[]{:S(2)}) copy-start(bf16[2048,512]{1,0:T(8,128)(2,1)} %weight_ref.3) | copy-start | bytes 6291460
  61.2 15.6 %all-to-all-start.2 = ((bf16[64,8,128]{2,1,0:T(8,128)(2,1)}), bf16[64,8,128]{2,1,0:T(8,128)(2,1)S(1)}, u32[]{:S(2)}, u32[]{:S(2)}) async-start(bf16[64,8,128]{2,1,0:T(8,128)(2,1)} %get-tuple-element.30), calls=%async_computation.2 | async-start | bytes 262144 | tf_op jit(solution)/shard_map/all_to_all | solution.py:42
  76.8 23.7 %copy-start.1 = (f32[2048,128]{1,0:T(8,128)S(1)}, f32[2048,128]{1,0:T(8,128)}, u32[]{:S(2)}) copy-start(f32[2048,128]{1,0:T(8,128)} %get-tuple-element.37.logits_ref) | copy-start | bytes 3145732
  103.7 0.8 copy-start.2
  104.5 23.2 %all-to-all-start.4 = ((bf16[64,32,128]{2,1,0:T(8,128)(2,1)}), bf16[64,32,128]{2,1,0:T(8,128)(2,1)S(1)}, u32[]{:S(2)}, u32[]{:S(2)}) async-start(bf16[64,32,128]{2,1,0:T(8,128)(2,1)} %copy-done.2), calls=%async_computation.4 | async-start | bytes 1048576 | tf_op jit(solution)/shard_map/all_to_all | solution.py:42
  110.6 17.1 %copy-start.3 = (bf16[128,8]{0,1:T(8,128)(2,1)S(1)}, bf16[128,8]{0,1:T(8,128)(2,1)}, u32[]{:S(2)}) copy-start(bf16[128,8]{0,1:T(8,128)(2,1)} %param.5) | copy-start | bytes 6148

commit v8 on v7

--- a/solution.py
+++ b/solution.py
@@ -16,10 +16,10 @@
 SHARE = 1.0 / (1024 * 0.1)
 TILE = 256
 WIDE = 512
+HALF = 4
 BLOCKS = 8
 f32, bf16 = jnp.float32, jnp.bfloat16
 VMEM = pl.BlockSpec(memory_space=pltpu.VMEM)
-SMEM = pl.BlockSpec(memory_space=pltpu.SMEM)
 ANY = pl.BlockSpec(memory_space=pl.ANY)
 
 
@@ -70,24 +70,21 @@
     return pl.pallas_call(
         body,
         out_shape=outs,
-        grid_spec=pltpu.PrefetchScalarGridSpec(
-            num_scalar_prefetch=1,
-            grid=(ROWS // TILE,),
-            in_specs=ins,
-            out_specs=out_specs,
-            scratch_shapes=scratch,
-        ),
+        grid=(ROWS // TILE,),
+        in_specs=ins,
+        out_specs=out_specs,
+        scratch_shapes=scratch,
         compiler_params=limits(),
         cost_estimate=cost(**work),
     )
 
 
 def whole(*dims):
-    return pl.BlockSpec(dims, lambda i, me: (0,) * len(dims))
+    return pl.BlockSpec(dims, lambda i: (0,) * len(dims))
 
 
 def stripe(width):
-    return pl.BlockSpec((TILE, width), lambda i, me: (i, 0))
+    return pl.BlockSpec((TILE, width), lambda i: (i, 0))
 
 
 def features_of(cores, x, yh, which):
@@ -126,10 +123,10 @@
 
 
 def first_kernel(
-    me_ref, own_ref, other_ref, weight_ref, kernel_out, unit_ref, sent_out, scale_ref, features_ref,
+    own_ref, other_ref, weight_ref, kernel_out, unit_ref, sent_out, scale_ref, features_ref,
     teacher_ref, stage_ref, sent_ref, mass_ref, sem_ref, sent_sem,
 ):
-    me, core = me_ref[0], me_ref[1]
+    me, core = lax.axis_index("smp"), lax.rem(lax.axis_index("proto"), 2)
 
     def by_core(body):
         @pl.when(core == 0)
@@ -181,10 +178,10 @@
 
 
 def student_kernel(
-    me_ref, unit_ref, weight_ref, logits_out, own_out, total_ref, stage_ref, own_ref, sum_ref, sem_ref, own_sem
+    unit_ref, weight_ref, logits_out, own_out, total_ref, stage_ref, own_ref, sum_ref, sem_ref, own_sem
 ):
     sum_ref[...] = jnp.zeros_like(sum_ref)
-    lanes = pl.ds(pl.multiple_of(me_ref[0] * 128, 128), 128)
+    lanes = pl.ds(pl.multiple_of(lax.axis_index("smp") * 128, 128), 128)
 
     def copies(i):
         rows = pl.ds(pl.multiple_of(i * WIDE, WIDE), WIDE)
@@ -244,10 +241,10 @@
 
 
 def third_kernel(
-    me_ref, got_ref, kernel_ref, kept_ref, logits_ref, features_ref, weight_ref,
+    got_ref, kernel_ref, kept_ref, logits_ref, features_ref, weight_ref,
     sent_ref, total_ref, before_ref, col_ref, mass_ref, scaled_ref, pair_ref,
 ):
-    me = me_ref[0]
+    me = lax.axis_index("smp")
     got = received(got_ref)
     before_ref[...] = got[:8, :]
     total_ref[...] = got[8:16, :] + got[16:, :]
@@ -293,7 +290,7 @@
 
 
 def weight_kernel(
-    me_ref, kernel_ref, logits_ref, total_ref, before_ref, unit_ref, out_ref, targets_ref, rows_ref
+    kernel_ref, logits_ref, total_ref, before_ref, unit_ref, out_ref, near_ref, far_ref, slice_ref, rows_ref
 ):
     @pl.when(pl.program_id(0) == 0)
     def _():
@@ -306,21 +303,32 @@
     targets = kernel * row_scale * rows_ref[1:2, :]
     probs = jnp.exp(logits_ref[...]) * rows_ref[2:3, :]
     grad = ((probs - targets) * SHARE).astype(bf16)
-    targets_ref[...] = (targets * SHARE).astype(bf16)
-    out_ref[...] = lax.dot_general(unit_ref[...], grad, (((1,), (1,)), ((), ())), preferred_element_type=f32)
+    shared = (targets * SHARE).astype(bf16)
+
+    @pl.when(pl.program_id(0) < HALF)
+    def _():
+        near_ref[...] = shared
+
+    @pl.when(pl.program_id(0) >= HALF)
+    def _():
+        far_ref[...] = shared
+
+    units = unit_ref[pl.ds(pl.multiple_of(lax.axis_index("smp") * 64, 64), 64), :]
+    slice_ref[...] = units
+    out_ref[...] = lax.dot_general(units, grad, (((1,), (1,)), ((), ())), preferred_element_type=f32)
 
 
 def final_kernel(
-    me_ref, got_ref, features_ref, scale_ref, total_ref, before_ref, unit_ref, near_ref, targets_far,
+    got_ref, features_ref, scale_ref, total_ref, before_ref, unit_ref, near_ref, held_ref, targets_far,
     features_out, loss_out, weight_out, change_ref, targets_ref, sem_ref,
 ):
     def copy_in(i):
-        rows = pl.ds(i * WIDE, WIDE)
+        rows = pl.ds(i * TILE, TILE)
         return pltpu.make_async_copy(targets_far.at[rows], targets_ref.at[rows], sem_ref.at[i])
 
-    for i in range(ROWS // WIDE):
+    for i in range(ROWS // TILE - HALF):
         copy_in(i).start()
-    me = me_ref[0]
+    me = lax.axis_index("smp")
     got = received(got_ref)
     before = before_ref[...]
     change_ref[...] = got[:8] / (before + got[:8])
@@ -330,14 +338,19 @@
     scale = scale_ref[pl.ds(me, 1), :]
     features_out[...] = scale * unit_grad - (scale * scale * scale * inner) * features_ref[...].astype(f32)
     loss_out[...] = jnp.log(total_ref[pl.ds(me, 1), :]) - (1.0 - own) * (got[28:29] + got[29:30])
-    units = unit_ref[pl.ds(pl.multiple_of(me * 64, 64), 64), :].astype(f32)
-    moved = (units * as_row(change_ref[...])).astype(bf16)
-    for i in range(ROWS // WIDE):
+    moved = (unit_ref[...].astype(f32) * as_row(change_ref[...])).astype(bf16)
+
+    def correct(start, targets):
+        rows = pl.ds(start, targets.shape[0])
+        weight_out[:, rows] = near_ref[:, rows] + lax.dot_general(
+            moved, targets, (((1,), (1,)), ((), ())), preferred_element_type=f32
+        )
+
+    for i in range(HALF):
+        correct(i * TILE, held_ref[pl.ds(i * TILE, TILE), :])
+    for i in range(ROWS // TILE - HALF):
         copy_in(i).wait()
-        rows = pl.ds(i * WIDE, WIDE)
-        weight_out[:, rows] = near_ref[:, rows] + lax.dot_general(
-            moved, targets_ref[rows, :], (((1,), (1,)), ((), ())), preferred_element_type=f32
-        )
+        correct((HALF + i) * TILE, targets_ref[pl.ds(i * TILE, TILE), :])
 
 
 def shape(dims, dtype=f32):
@@ -345,10 +358,7 @@
 
 
 def on_device(teacher_features, student_features, teacher_weight, student_weight):
-    core = lax.rem(lax.axis_index("proto"), 2)
-    me = jnp.stack([lax.axis_index("smp"), core]).astype(jnp.int32)
     raw = jnp.concatenate([teacher_features.T, student_features.T], axis=0)
-    raw, me = lax.optimization_barrier((raw, me))
     first = gathered(raw, ("yh", "yl", "z"))
     second = gathered(first, ("x",))
     second, teacher_weight = lax.optimization_barrier((second, teacher_weight))
@@ -366,21 +376,21 @@
         first_kernel,
         [pltpu.HBM((ROWS, B), f32), shape((D, B), bf16), pltpu.HBM((64, 8, 128), bf16), shape((8, 128)),
          shape((D, 128))],
-        [SMEM, VMEM, VMEM, VMEM],
+        [VMEM, VMEM, VMEM],
         [ANY, VMEM, ANY, VMEM, VMEM],
         [pltpu.VMEM((D, B), bf16), stage, pltpu.VMEM((64, 8, 128), bf16), rows8, wide_sems,
          pltpu.SemaphoreType.DMA],
         **matmul,
-    )(me, second, other, weight_near)
+    )(second, other, weight_near)
     got_1 = sent_to_protos(sent_1)
     logits, logits_own, local_total = call(
         student_kernel,
         [pltpu.HBM((ROWS, B), f32), pltpu.HBM((ROWS, 128), f32), shape((8, 128))],
-        [SMEM, VMEM, VMEM],
+        [VMEM, VMEM],
         [ANY, ANY, VMEM],
         [stage, pltpu.VMEM((ROWS, 128), f32), rows8, wide_sems, wide_sems],
         **matmul,
-    )(me, student_unit, student_weight)
+    )(student_unit, student_weight)
     kernel_near, sent_2, kept = call(
         second_kernel,
         [pltpu.VMEM((ROWS, B), f32), shape((64, 24, 128), bf16), shape((8, 128))],
@@ -394,34 +404,38 @@
     sent_3, total, before = call(
         third_kernel,
         [shape((64, 32, 128), bf16), shape((8, 128)), shape((8, 128))],
-        [SMEM] + [VMEM] * 6,
+        [VMEM] * 6,
         None,
         [row, rows8, pltpu.VMEM((ROWS, 128), f32), pltpu.VMEM((ROWS, 256), bf16)],
         flops=2 * ROWS * 256 * D,
         moved=12 * 2**20,
         exps=ROWS * 128,
-    )(me, got_2, kernel_near, kept, logits_own, features_own, student_weight)
+    )(got_2, kernel_near, kept, logits_own, features_own, student_weight)
     got_3 = sent_to_protos(sent_3)
-    weight_near, targets = streamed(
+    partial, targets_near, targets_far, unit_slice = streamed(
         weight_kernel,
-        [shape((64, ROWS)), pltpu.HBM((ROWS, B), bf16)],
-        [stripe(B), stripe(B), whole(8, 128), whole(8, 128), pl.BlockSpec((64, B), lambda i, me: (me[0], 0))],
-        [pl.BlockSpec((64, TILE), lambda i, me: (0, i)), stripe(B)],
+        [shape((64, ROWS)), pltpu.VMEM((HALF * TILE, B), bf16), pltpu.HBM((ROWS - HALF * TILE, B), bf16),
+         shape((64, B), bf16)],
+        [stripe(B), stripe(B), whole(8, 128), whole(8, 128), whole(D, B)],
+        [pl.BlockSpec((64, TILE), lambda i: (0, i)),
+         pl.BlockSpec((TILE, B), lambda i: (jnp.minimum(i, HALF - 1), 0)),
+         pl.BlockSpec((TILE, B), lambda i: (jnp.maximum(i - HALF, 0), 0)), whole(64, B)],
         [rows8],
         flops=2 * ROWS * B * 64,
         moved=21 * 2**20,
         exps=ROWS * B,
-    )(me, far(kernel), far(logits), total, before, student_unit)
+    )(far(kernel), far(logits), total, before, student_unit)
     grad_features, loss, grad_weight = call(
         final_kernel,
         [shape((8, 128)), shape((1, 128)), shape((64, ROWS))],
-        [SMEM] + [VMEM] * 7 + [ANY],
+        [VMEM] * 8 + [ANY],
         None,
-        [rows8_small, pltpu.VMEM((ROWS, B), bf16), wide_sems],
+        [rows8_small, pltpu.VMEM((ROWS - HALF * TILE, B), bf16), near_sems],
         flops=2 * ROWS * B * 64,
         moved=5 * 2**20,
     )(
-        me, got_3, student_features.T, student_scale, total, before, student_unit, weight_near, far(targets)
+        got_3, student_features.T, student_scale, total, before, unit_slice, partial, targets_near,
+        far(targets_far),
     )
     return loss.reshape(128), grad_features.T, grad_weight.T
 

time: 133 us -> 131 us (0.985)
  transfers between devices with their start and end apart: 3 -> 3, of which waited for: 3 -> 3; matrix products, arithmetic and copies ran while one was open for 0% -> 0% of each run, Pallas kernels for 14% -> 13%
where the time goes in v8:
time: 131 us; the launch traced here: 130 us
  blocking collectives  64.1 us (49%)
  Pallas kernels  34.3 us (26%)
  starting transfers between devices  18.2 us (14%)
  waiting for transfers between devices  10.6 us (8%)
  local copies, waits for them, and re-layouts  1.41 us (1%)
    all_to_all x2, blocking collectives, gathered(): lax.all_to_all(copies, BOTH, 0, 0, tiled=True, axis_index_groups=group)  44.7 us
    all_to_all x1, blocking collectives, sent_to_protos(): return lax.all_to_all(x, 'proto', 0, 0, tiled=True)  19.4 us
    all_to_all x2, starting transfers between devices, sent_to_protos(): return lax.all_to_all(x, 'proto', 0, 0, tiled=True)  11.7 us
    pallas_call x1, Pallas kernels, on_device(): streamed(weight_kernel, [shape((64, ROWS)), pltpu.VMEM((HALF * TILE, B),...  11.5 us
    all_to_all x2, waiting for transfers between devices, sent_to_protos(): return lax.all_to_all(x, 'proto', 0, 0, tiled=True)  9.91 us
    ppermute x1, starting transfers between devices, on_device(): other = lax.ppermute(second, 'proto', [(i, i ^ 1) for i in range(64)])  6.53 us
    pallas_call x1, Pallas kernels, on_device(): call(first_kernel, [pltpu.HBM((ROWS, B), f32), shape((D, B), bf16), pltpu...  5.48 us
    pallas_call x1, Pallas kernels, on_device(): call(student_kernel, [pltpu.HBM((ROWS, B), f32), pltpu.HBM((ROWS, 128), f...  4.47 us
  transfers between devices with their start and end apart: 3, of which 3 were waited for; matrix products, arithmetic and copies ran while one was open for 0% of the time, Pallas kernels for 13%

profile of v8, /device:TPU:1, one launch (start us, length us, event | category | flops | bytes accessed | tf_op | source)
XLA Modules:
  0.0 130.1 jit_solution(9092022869001672815)
XLA Ops:
  0.6 0.7 pad_maximum_fusion
  1.4 29.5 %all_to_all.25 = bf16[64,16,128]{2,1,0:T(8,128)(2,1)S(1)} all-to-all(bf16[64,16,128]{2,1,0:T(8,128)(2,1)S(1)} %broadcast_in_dim.4), channel_id=1, replica_groups={{0,2,4,6,8,10,12,14,16,18,20,22,24,26,28,30,32,34,36,38,40,42,44,46,48,..., dimensions={0} | all-to-all | bytes 524288 | tf_op jit(solution)/shard_map/all_to_all | solution.py:38
  30.9 0.1 broadcast_in_dim.5
  31.0 15.2 %all_to_all.26.own_ref = bf16[4,64,16,128]{3,2,1,0:T(8,128)(2,1)S(1)} all-to-all(bf16[4,64,16,128]{3,2,1,0:T(8,128)(2,1)S(1)} %broadcast_in_dim.5), channel_id=1, replica_groups={{0,128,256,384},{1,129,257,385},{2,130,258,386},{3,131,259,387},{4,132,..., dimensions={0} | all-to-all | bytes 2097152 | tf_op jit(solution)/shard_map/all_to_all | solution.py:38
  46.2 6.5 %collective-permute-start = (bf16[4,64,16,128]{3,2,1,0:T(8,128)(2,1)S(1)}, bf16[4,64,16,128]{3,2,1,0:T(8,128)(2,1)S(1)}, u32[]{:S(2)}, u32[]{:S(2)}) collective-permute-start(bf16[4,64,16,128]{3,2,1,0:T(8,128)(2,1)S(1)} %all_to_all.26.own_ref), channel_id=1, source_target_pairs={{0,1},{1,0},{2,3},{3,2},{4,5},{5,4},{6,7},{7,6},{8,9},{9,8},{10,11... | collective-permute-start | bytes 3145736 | tf_op jit(solution)/shard_map/ppermute | solution.py:365
  52.8 1.6 %shard_map.67.weight_ref = bf16[2048,512]{1,0:T(8,128)(2,1)S(1)} custom-call(bf16[2048,512]{1,0:T(8,128)(2,1)} %far_ref), custom_call_target="tpu_custom_call" | custom-call | bytes 4194304 | tf_op jit(solution)/shard_map/pallas_call | solution.py:372
  54.3 0.0 copy-start
  54.3 0.7 collective-permute-done.other_ref
  55.0 5.5 %shard_map.68 = (f32[2048,1024]{1,0:T(8,128)}, bf16[512,1024]{1,0:T(8,128)(2,1)S(1)}, bf16[64,8,128]{2,1,0:T(8,128)(2,1)}, f32[8,128]{1,0:T(8,128)S(1)}, f32[512,128]{1,0:T(8,128)S(1)}) custom-call(bf16[4,64,16,128]{3,2,1,0:T(8,128)(2,1)S(1)} %all_to_all.26.own_ref, bf16[4,64,16,128]{3,2,1,0:T(8,128)(2,1)S(1)} %collective-permute-done.other_ref, ...), custom_call_target="tpu_custom_call" | custom-call | flops 2147483648 | bytes 12582912 | tf_op jit(solution)/shard_map/pallas_call | solution.py:375
  60.5 0.0 copy-start.1
  60.5 5.6 %all-to-all-start.2 = ((bf16[64,8,128]{2,1,0:T(8,128)(2,1)}), bf16[64,8,128]{2,1,0:T(8,128)(2,1)S(1)}, u32[]{:S(2)}, u32[]{:S(2)}) async-start(bf16[64,8,128]{2,1,0:T(8,128)(2,1)} %get-tuple-element.28), calls=%async_computation.2 | async-start | bytes 262144 | tf_op jit(solution)/shard_map/all_to_all | solution.py:42
  66.1 0.0 copy-done
  66.2 4.5 %shard_map.69 = (f32[2048,1024]{1,0:T(8,128)}, f32[2048,128]{1,0:T(8,128)}, f32[8,128]{1,0:T(8,128)S(1)}) custom-call(bf16[512,1024]{1,0:T(8,128)(2,1)S(1)} %get-tuple-element.30.unit_ref, bf16[2048,512]{1,0:T(8,128)(2,1)S(1)} %copy-done), custom_call_target="tpu_custom_call" | custom-call | flops 2147483648 | bytes 12582912 | tf_op jit(solution)/shard_map/pallas_call | solution.py:386
  70.6 0.0 copy-done.1
  70.6 5.5 %all-to-all-done.2.got_ref = bf16[64,8,128]{2,1,0:T(8,128)(2,1)S(1)} async-done(((bf16[64,8,128]{2,1,0:T(8,128)(2,1)}), bf16[64,8,128]{2,1,0:T(8,128)(2,1)S(1)}, u32[]{:S(2)}, u32[]{:S(2)}) %all-to-all-start.2) | async-done | bytes 131104 | tf_op jit(solution)/shard_map/all_to_all | solution.py:42
  76.1 0.0 copy-start.3
  76.1 3.8 %shard_map.70 = (f32[2048,1024]{1,0:T(8,128)S(1)}, bf16[64,24,128]{2,1,0:T(8,128)(2,1)S(1)}, f32[8,128]{1,0:T(8,128)S(1)}) custom-call(bf16[64,8,128]{2,1,0:T(8,128)(2,1)S(1)} %all-to-all-done.2.got_ref, f32[2048,1024]{1,0:T(8,128)} %get-tuple-element.29.far_ref.kernel_ref, f32[8,128]{1,0:T(8,128)S(1)} %get-tuple-element.31.total_ref), custom_call_target="tpu_custom_call" | custom-call | flops 8388608 | bytes 8388608 | tf_op jit(solution)/shard_map/pallas_call | solution.py:394
  79.9 19.4 %all_to_all.27.got_ref = bf16[64,24,128]{2,1,0:T(8,128)(2,1)S(1)} all-to-all(bf16[64,24,128]{2,1,0:T(8,128)(2,1)S(1)} %get-tuple-element.32), channel_id=1, replica_groups=mesh['smp'=8,'proto'=64] {'proto'}, dimensions={0} | all-to-all | bytes 786432 | tf_op jit(solution)/shard_map/all_to_all | solution.py:42
  99.3 0.0 copy-done.3
  99.3 3.4 %shard_map.71 = (bf16[64,32,128]{2,1,0:T(8,128)(2,1)}, f32[8,128]{1,0:T(8,128)S(1)}, f32[8,128]{1,0:T(8,128)S(1)}) custom-call(bf16[64,24,128]{2,1,0:T(8,128)(2,1)S(1)} %all_to_all.27.got_ref, f32[2048,1024]{1,0:T(8,128)S(1)} %get-tuple-element.33.kernel_ref, f32[8,128]{1,0:T(8,128)S(1)} %get-tuple-element.34.kept_ref, f32[2048,128]{1,0:T(8,128)S(1)} %copy-done.3, ...), custom_call_target="tpu_custom_call" | custom-call | flops 536870912 | bytes 12582912 | tf_op jit(solution)/shard_map/pallas_call | solution.py:404
  102.7 6.1 %all-to-all-start.4 = ((bf16[64,32,128]{2,1,0:T(8,128)(2,1)}), bf16[64,32,128]{2,1,0:T(8,128)(2,1)S(1)}, u32[]{:S(2)}, u32[]{:S(2)}) async-start(bf16[64,32,128]{2,1,0:T(8,128)(2,1)} %get-tuple-element.37), calls=%async_computation.4 | async-start | bytes 1048576 | tf_op jit(solution)/shard_map/all_to_all | solution.py:42
  108.8 0.0 copy-start.2
  108.8 1.2 copy-done.2
  110.0 0.0 copy-start.4
  110.0 11.5 %shard_map.72 = (f32[64,2048]{1,0:T(8,128)S(1)}, bf16[1024,1024]{1,0:T(8,128)(2,1)S(1)}, bf16[1024,1024]{1,0:T(8,128)(2,1)}, bf16[64,1024]{1,0:T(8,128)(2,1)S(1)}) custom-call(f32[2048,1024]{1,0:T(8,128)} %get-tuple-element.29.far_ref.kernel_ref, f32[2048,1024]{1,0:T(8,128)} %get-tuple-element.41.logits_ref, f32[8,128]{1,0:T(8,128)S(1)} %get-tuple-element.39.total_ref, ...), custom_call_target="tpu_custom_call" | custom-call | flops 268435456 | bytes 22020096 | tf_op jit(solution)/shard_map/pallas_call | solution.py:415
  121.5 4.4 %all-to-all-done.4.got_ref = bf16[64,32,128]{2,1,0:T(8,128)(2,1)S(1)} async-done(((bf16[64,32,128]{2,1,0:T(8,128)(2,1)}), bf16[64,32,128]{2,1,0:T(8,128)(2,1)S(1)}, u32[]{:S(2)}, u32[]{:S(2)}) %all-to-all-start.4) | async-done | bytes 524320 | tf_op jit(solution)/shard_map/all_to_all | solution.py:42
  126.0 0.0 copy-done.4
  126.0 4.2 %shard_map.73 = (f32[8,128]{1,0:T(8,128)}, f32[1,128]{1,0:T(1,128)}, f32[64,2048]{1,0:T(8,128)}) custom-call(bf16[64,32,128]{2,1,0:T(8,128)(2,1)S(1)} %all-to-all-done.4.got_ref, bf16[8,128]{1,0:T(8,128)(2,1)S(1)} %bitcast.6, f32[8,128]{1,0:T(8,128)S(1)} %get-tuple-element.38.scale_ref, f32[8,128]{1,0:T(8,128)S(1)} %get-tuple-element.39.total_ref, ...), custom_call_target="tpu_custom_call" | custom-call | flops 268435456 | bytes 5242880 | tf_op jit(solution)/shard_map/pallas_call | solution.py:428
  (1 shorter events, 0.0 us)
Async XLA Ops:
  46.2 8.8 %collective-permute-start = (bf16[4,64,16,128]{3,2,1,0:T(8,128)(2,1)S(1)}, bf16[4,64,16,128]{3,2,1,0:T(8,128)(2,1)S(1)}, u32[]{:S(2)}, u32[]{:S(2)}) collective-permute-start(bf16[4,64,16,128]{3,2,1,0:T(8,128)(2,1)S(1)} %all_to_all.26.own_ref), channel_id=1, source_target_pairs={{0,1},{1,0},{2,3},{3,2},{4,5},{5,4},{6,7},{7,6},{8,9},{9,8},{10,11... | collective-permute-start | bytes 3145736 | tf_op jit(solution)/shard_map/ppermute | solution.py:365
  54.3 11.8 %copy-start = (bf16[2048,512]{1,0:T(8,128)(2,1)S(1)}, bf16[2048,512]{1,0:T(8,128)(2,1)}, u32[]{:S(2)}) copy-start(bf16[2048,512]{1,0:T(8,128)(2,1)} %weight_ref.3) | copy-start | bytes 6291460
  60.5 10.1 %copy-start.1 = (bf16[512,1024]{1,0:T(8,128)(2,1)}, bf16[512,1024]{1,0:T(8,128)(2,1)S(1)}, u32[]{:S(2)}) copy-start(bf16[512,1024]{1,0:T(8,128)(2,1)S(1)} %get-tuple-element.30.unit_ref) | copy-start | bytes 3145732
  60.5 15.6 %all-to-all-start.2 = ((bf16[64,8,128]{2,1,0:T(8,128)(2,1)}), bf16[64,8,128]{2,1,0:T(8,128)(2,1)S(1)}, u32[]{:S(2)}, u32[]{:S(2)}) async-start(bf16[64,8,128]{2,1,0:T(8,128)(2,1)} %get-tuple-element.28), calls=%async_computation.2 | async-start | bytes 262144 | tf_op jit(solution)/shard_map/all_to_all | solution.py:42
  76.1 23.2 %copy-start.3 = (f32[2048,128]{1,0:T(8,128)S(1)}, f32[2048,128]{1,0:T(8,128)}, u32[]{:S(2)}) copy-start(f32[2048,128]{1,0:T(8,128)} %get-tuple-element.35.logits_ref) | copy-start | bytes 3145732
  102.7 23.2 %all-to-all-start.4 = ((bf16[64,32,128]{2,1,0:T(8,128)(2,1)}), bf16[64,32,128]{2,1,0:T(8,128)(2,1)S(1)}, u32[]{:S(2)}, u32[]{:S(2)}) async-start(bf16[64,32,128]{2,1,0:T(8,128)(2,1)} %get-tuple-element.37), calls=%async_computation.4 | async-start | bytes 1048576 | tf_op jit(solution)/shard_map/all_to_all | solution.py:42
  108.8 1.2 copy-start.2
  110.0 15.9 %copy-start.4 = (bf16[128,8]{0,1:T(8,128)(2,1)S(1)}, bf16[128,8]{0,1:T(8,128)(2,1)}, u32[]{:S(2)}) copy-start(bf16[128,8]{0,1:T(8,128)(2,1)} %param.5) | copy-start | bytes 6148

commit v9 on v8

--- a/solution.py
+++ b/solution.py
@@ -230,8 +230,10 @@
     mass = as_blocks(mass_ref[...]).astype(bf16).astype(f32)
     kept_ref[...] = mass
     total = total_ref[...]
-    high = total.astype(bf16).astype(f32)
-    packed = jnp.concatenate([mass, high, total - high], axis=0).astype(bf16)
+    step = jnp.exp2(jnp.floor(jnp.log2(total)) - 7.0)
+    place = lax.axis_index("proto").astype(f32)
+    spread = total + step * ((place + 0.5) * (1.0 / 64) - 0.5)
+    packed = jnp.concatenate([mass, spread], axis=0).astype(bf16)
     sent_ref[...] = jnp.broadcast_to(packed[None], sent_ref.shape)
 
 
@@ -247,7 +249,7 @@
     me = lax.axis_index("smp")
     got = received(got_ref)
     before_ref[...] = got[:8, :]
-    total_ref[...] = got[8:16, :] + got[16:, :]
+    total_ref[...] = got[8:, :]
     col_ref[...] = as_row(1.0 / (B * got[:8, :]))
     mass_ref[...] = jnp.zeros_like(mass_ref)
     lanes = pl.ds(pl.multiple_of(me * 128, 128), 128)
@@ -393,7 +395,7 @@
     )(student_unit, student_weight)
     kernel_near, sent_2, kept = call(
         second_kernel,
-        [pltpu.VMEM((ROWS, B), f32), shape((64, 24, 128), bf16), shape((8, 128))],
+        [pltpu.VMEM((ROWS, B), f32), shape((64, 16, 128), bf16), shape((8, 128))],
         [VMEM, ANY, VMEM],
         None,
         [row, rows8, near_sems],

time: 131 us -> 128 us (0.977)
  blocking collectives: 64.1 us -> 61.4 us
    all_to_all x1, blocking collectives: 19.4 us -> 16.7 us  [sent_to_protos(): return lax.all_to_all(x, 'proto', 0, 0, tiled=True)]
  transfers between devices with their start and end apart: 3 -> 3, of which waited for: 3 -> 3; matrix products, arithmetic and copies ran while one was open for 0% -> 0% of each run, Pallas kernels for 13% -> 14%
where the time goes in v9:
time: 128 us; the launch traced here: 127 us
  blocking collectives  61.4 us (48%)
  Pallas kernels  34.3 us (27%)
  starting transfers between devices  18.1 us (14%)
  waiting for transfers between devices  10.6 us (8%)
  local copies, waits for them, and re-layouts  1.41 us (1%)
    all_to_all x2, blocking collectives, gathered(): lax.all_to_all(copies, BOTH, 0, 0, tiled=True, axis_index_groups=group)  44.7 us
    all_to_all x1, blocking collectives, sent_to_protos(): return lax.all_to_all(x, 'proto', 0, 0, tiled=True)  16.7 us
    all_to_all x2, starting transfers between devices, sent_to_protos(): return lax.all_to_all(x, 'proto', 0, 0, tiled=True)  11.6 us
    pallas_call x1, Pallas kernels, on_device(): streamed(weight_kernel, [shape((64, ROWS)), pltpu.VMEM((HALF * TILE, B),...  11.5 us
    all_to_all x2, waiting for transfers between devices, sent_to_protos(): return lax.all_to_all(x, 'proto', 0, 0, tiled=True)  9.91 us
    ppermute x1, starting transfers between devices, on_device(): other = lax.ppermute(second, 'proto', [(i, i ^ 1) for i in range(64)])  6.53 us
    pallas_call x1, Pallas kernels, on_device(): call(first_kernel, [pltpu.HBM((ROWS, B), f32), shape((D, B), bf16), pltpu...  5.48 us
    pallas_call x1, Pallas kernels, on_device(): call(student_kernel, [pltpu.HBM((ROWS, B), f32), pltpu.HBM((ROWS, 128), f...  4.47 us
  transfers between devices with their start and end apart: 3, of which 3 were waited for; matrix products, arithmetic and copies ran while one was open for 0% of the time, Pallas kernels for 14%

profile of v9, /device:TPU:1, one launch (start us, length us, event | category | flops | bytes accessed | tf_op | source)
XLA Modules:
  0.0 127.3 jit_solution(11020994464283549890)
XLA Ops:
  0.6 0.7 pad_maximum_fusion
  1.4 29.5 %all_to_all.25 = bf16[64,16,128]{2,1,0:T(8,128)(2,1)S(1)} all-to-all(bf16[64,16,128]{2,1,0:T(8,128)(2,1)S(1)} %broadcast_in_dim.4), channel_id=1, replica_groups={{0,2,4,6,8,10,12,14,16,18,20,22,24,26,28,30,32,34,36,38,40,42,44,46,48,..., dimensions={0} | all-to-all | bytes 524288 | tf_op jit(solution)/shard_map/all_to_all | solution.py:38
  30.9 0.1 broadcast_in_dim.5
  31.0 15.2 %all_to_all.26.own_ref = bf16[4,64,16,128]{3,2,1,0:T(8,128)(2,1)S(1)} all-to-all(bf16[4,64,16,128]{3,2,1,0:T(8,128)(2,1)S(1)} %broadcast_in_dim.5), channel_id=1, replica_groups={{0,128,256,384},{1,129,257,385},{2,130,258,386},{3,131,259,387},{4,132,..., dimensions={0} | all-to-all | bytes 2097152 | tf_op jit(solution)/shard_map/all_to_all | solution.py:38
  46.2 6.5 %collective-permute-start = (bf16[4,64,16,128]{3,2,1,0:T(8,128)(2,1)S(1)}, bf16[4,64,16,128]{3,2,1,0:T(8,128)(2,1)S(1)}, u32[]{:S(2)}, u32[]{:S(2)}) collective-permute-start(bf16[4,64,16,128]{3,2,1,0:T(8,128)(2,1)S(1)} %all_to_all.26.own_ref), channel_id=1, source_target_pairs={{0,1},{1,0},{2,3},{3,2},{4,5},{5,4},{6,7},{7,6},{8,9},{9,8},{10,11... | collective-permute-start | bytes 3145736 | tf_op jit(solution)/shard_map/ppermute | solution.py:367
  52.8 1.6 %shard_map.67.weight_ref = bf16[2048,512]{1,0:T(8,128)(2,1)S(1)} custom-call(bf16[2048,512]{1,0:T(8,128)(2,1)} %far_ref), custom_call_target="tpu_custom_call" | custom-call | bytes 4194304 | tf_op jit(solution)/shard_map/pallas_call | solution.py:374
  54.3 0.0 copy-start
  54.3 0.7 collective-permute-done.other_ref
  55.0 5.5 %shard_map.68 = (f32[2048,1024]{1,0:T(8,128)}, bf16[512,1024]{1,0:T(8,128)(2,1)S(1)}, bf16[64,8,128]{2,1,0:T(8,128)(2,1)}, f32[8,128]{1,0:T(8,128)S(1)}, f32[512,128]{1,0:T(8,128)S(1)}) custom-call(bf16[4,64,16,128]{3,2,1,0:T(8,128)(2,1)S(1)} %all_to_all.26.own_ref, bf16[4,64,16,128]{3,2,1,0:T(8,128)(2,1)S(1)} %collective-permute-done.other_ref, ...), custom_call_target="tpu_custom_call" | custom-call | flops 2147483648 | bytes 12582912 | tf_op jit(solution)/shard_map/pallas_call | solution.py:377
  60.5 0.0 copy-start.1
  60.5 5.6 %all-to-all-start.2 = ((bf16[64,8,128]{2,1,0:T(8,128)(2,1)}), bf16[64,8,128]{2,1,0:T(8,128)(2,1)S(1)}, u32[]{:S(2)}, u32[]{:S(2)}) async-start(bf16[64,8,128]{2,1,0:T(8,128)(2,1)} %get-tuple-element.28), calls=%async_computation.2 | async-start | bytes 262144 | tf_op jit(solution)/shard_map/all_to_all | solution.py:42
  66.1 0.0 copy-done
  66.2 4.5 %shard_map.69 = (f32[2048,1024]{1,0:T(8,128)}, f32[2048,128]{1,0:T(8,128)}, f32[8,128]{1,0:T(8,128)S(1)}) custom-call(bf16[512,1024]{1,0:T(8,128)(2,1)S(1)} %get-tuple-element.30.unit_ref, bf16[2048,512]{1,0:T(8,128)(2,1)S(1)} %copy-done), custom_call_target="tpu_custom_call" | custom-call | flops 2147483648 | bytes 12582912 | tf_op jit(solution)/shard_map/pallas_call | solution.py:388
  70.6 0.0 copy-done.1
  70.6 5.5 %all-to-all-done.2.got_ref = bf16[64,8,128]{2,1,0:T(8,128)(2,1)S(1)} async-done(((bf16[64,8,128]{2,1,0:T(8,128)(2,1)}), bf16[64,8,128]{2,1,0:T(8,128)(2,1)S(1)}, u32[]{:S(2)}, u32[]{:S(2)}) %all-to-all-start.2) | async-done | bytes 131104 | tf_op jit(solution)/shard_map/all_to_all | solution.py:42
  76.1 0.0 copy-start.3
  76.1 3.8 %shard_map.70 = (f32[2048,1024]{1,0:T(8,128)S(1)}, bf16[64,16,128]{2,1,0:T(8,128)(2,1)S(1)}, f32[8,128]{1,0:T(8,128)S(1)}) custom-call(bf16[64,8,128]{2,1,0:T(8,128)(2,1)S(1)} %all-to-all-done.2.got_ref, f32[2048,1024]{1,0:T(8,128)} %get-tuple-element.29.far_ref.kernel_ref, f32[8,128]{1,0:T(8,128)S(1)} %get-tuple-element.31.total_ref), custom_call_target="tpu_custom_call" | custom-call | flops 8388608 | bytes 8388608 | tf_op jit(solution)/shard_map/pallas_call | solution.py:396
  79.9 16.7 %all_to_all.27.got_ref = bf16[64,16,128]{2,1,0:T(8,128)(2,1)S(1)} all-to-all(bf16[64,16,128]{2,1,0:T(8,128)(2,1)S(1)} %get-tuple-element.32), channel_id=1, replica_groups=mesh['smp'=8,'proto'=64] {'proto'}, dimensions={0} | all-to-all | bytes 524288 | tf_op jit(solution)/shard_map/all_to_all | solution.py:42
  96.6 0.0 copy-done.3
  96.6 3.4 %shard_map.71 = (bf16[64,32,128]{2,1,0:T(8,128)(2,1)}, f32[8,128]{1,0:T(8,128)S(1)}, f32[8,128]{1,0:T(8,128)S(1)}) custom-call(bf16[64,16,128]{2,1,0:T(8,128)(2,1)S(1)} %all_to_all.27.got_ref, f32[2048,1024]{1,0:T(8,128)S(1)} %get-tuple-element.33.kernel_ref, f32[8,128]{1,0:T(8,128)S(1)} %get-tuple-element.34.kept_ref, f32[2048,128]{1,0:T(8,128)S(1)} %copy-done.3, ...), custom_call_target="tpu_custom_call" | custom-call | flops 536870912 | bytes 12582912 | tf_op jit(solution)/shard_map/pallas_call | solution.py:406
  100.0 6.0 %all-to-all-start.4 = ((bf16[64,32,128]{2,1,0:T(8,128)(2,1)}), bf16[64,32,128]{2,1,0:T(8,128)(2,1)S(1)}, u32[]{:S(2)}, u32[]{:S(2)}) async-start(bf16[64,32,128]{2,1,0:T(8,128)(2,1)} %get-tuple-element.37), calls=%async_computation.4 | async-start | bytes 1048576 | tf_op jit(solution)/shard_map/all_to_all | solution.py:42
  106.0 0.0 copy-start.2
  106.0 1.2 copy-done.2
  107.2 0.0 copy-start.4
  107.2 11.5 %shard_map.72 = (f32[64,2048]{1,0:T(8,128)S(1)}, bf16[1024,1024]{1,0:T(8,128)(2,1)S(1)}, bf16[1024,1024]{1,0:T(8,128)(2,1)}, bf16[64,1024]{1,0:T(8,128)(2,1)S(1)}) custom-call(f32[2048,1024]{1,0:T(8,128)} %get-tuple-element.29.far_ref.kernel_ref, f32[2048,1024]{1,0:T(8,128)} %get-tuple-element.41.logits_ref, f32[8,128]{1,0:T(8,128)S(1)} %get-tuple-element.39.total_ref, ...), custom_call_target="tpu_custom_call" | custom-call | flops 268435456 | bytes 22020096 | tf_op jit(solution)/shard_map/pallas_call | solution.py:417
  118.7 4.4 %all-to-all-done.4.got_ref = bf16[64,32,128]{2,1,0:T(8,128)(2,1)S(1)} async-done(((bf16[64,32,128]{2,1,0:T(8,128)(2,1)}), bf16[64,32,128]{2,1,0:T(8,128)(2,1)S(1)}, u32[]{:S(2)}, u32[]{:S(2)}) %all-to-all-start.4) | async-done | bytes 524320 | tf_op jit(solution)/shard_map/all_to_all | solution.py:42
  123.2 0.0 copy-done.4
  123.2 4.2 %shard_map.73 = (f32[8,128]{1,0:T(8,128)}, f32[1,128]{1,0:T(1,128)}, f32[64,2048]{1,0:T(8,128)}) custom-call(bf16[64,32,128]{2,1,0:T(8,128)(2,1)S(1)} %all-to-all-done.4.got_ref, bf16[8,128]{1,0:T(8,128)(2,1)S(1)} %bitcast.6, f32[8,128]{1,0:T(8,128)S(1)} %get-tuple-element.38.scale_ref, f32[8,128]{1,0:T(8,128)S(1)} %get-tuple-element.39.total_ref, ...), custom_call_target="tpu_custom_call" | custom-call | flops 268435456 | bytes 5242880 | tf_op jit(solution)/shard_map/pallas_call | solution.py:430
  (1 shorter events, 0.0 us)
Async XLA Ops:
  46.2 8.8 %collective-permute-start = (bf16[4,64,16,128]{3,2,1,0:T(8,128)(2,1)S(1)}, bf16[4,64,16,128]{3,2,1,0:T(8,128)(2,1)S(1)}, u32[]{:S(2)}, u32[]{:S(2)}) collective-permute-start(bf16[4,64,16,128]{3,2,1,0:T(8,128)(2,1)S(1)} %all_to_all.26.own_ref), channel_id=1, source_target_pairs={{0,1},{1,0},{2,3},{3,2},{4,5},{5,4},{6,7},{7,6},{8,9},{9,8},{10,11... | collective-permute-start | bytes 3145736 | tf_op jit(solution)/shard_map/ppermute | solution.py:367
  54.3 11.8 %copy-start = (bf16[2048,512]{1,0:T(8,128)(2,1)S(1)}, bf16[2048,512]{1,0:T(8,128)(2,1)}, u32[]{:S(2)}) copy-start(bf16[2048,512]{1,0:T(8,128)(2,1)} %weight_ref.3) | copy-start | bytes 6291460
  60.5 10.1 %copy-start.1 = (bf16[512,1024]{1,0:T(8,128)(2,1)}, bf16[512,1024]{1,0:T(8,128)(2,1)S(1)}, u32[]{:S(2)}) copy-start(bf16[512,1024]{1,0:T(8,128)(2,1)S(1)} %get-tuple-element.30.unit_ref) | copy-start | bytes 3145732
  60.5 15.6 %all-to-all-start.2 = ((bf16[64,8,128]{2,1,0:T(8,128)(2,1)}), bf16[64,8,128]{2,1,0:T(8,128)(2,1)S(1)}, u32[]{:S(2)}, u32[]{:S(2)}) async-start(bf16[64,8,128]{2,1,0:T(8,128)(2,1)} %get-tuple-element.28), calls=%async_computation.2 | async-start | bytes 262144 | tf_op jit(solution)/shard_map/all_to_all | solution.py:42
  76.1 20.5 %copy-start.3 = (f32[2048,128]{1,0:T(8,128)S(1)}, f32[2048,128]{1,0:T(8,128)}, u32[]{:S(2)}) copy-start(f32[2048,128]{1,0:T(8,128)} %get-tuple-element.35.logits_ref) | copy-start | bytes 3145732
  100.0 23.1 %all-to-all-start.4 = ((bf16[64,32,128]{2,1,0:T(8,128)(2,1)}), bf16[64,32,128]{2,1,0:T(8,128)(2,1)S(1)}, u32[]{:S(2)}, u32[]{:S(2)}) async-start(bf16[64,32,128]{2,1,0:T(8,128)(2,1)} %get-tuple-element.37), calls=%async_computation.4 | async-start | bytes 1048576 | tf_op jit(solution)/shard_map/all_to_all | solution.py:42
  106.0 1.2 copy-start.2
  107.2 15.9 %copy-start.4 = (bf16[128,8]{0,1:T(8,128)(2,1)S(1)}, bf16[128,8]{0,1:T(8,128)(2,1)}, u32[]{:S(2)}) copy-start(bf16[128,8]{0,1:T(8,128)(2,1)} %param.5) | copy-start | bytes 6148

commit v10 on v9

--- a/solution.py
+++ b/solution.py
@@ -17,6 +17,7 @@
 TILE = 256
 WIDE = 512
 HALF = 4
+FAR = 1536
 BLOCKS = 8
 f32, bf16 = jnp.float32, jnp.bfloat16
 VMEM = pl.BlockSpec(memory_space=pltpu.VMEM)
@@ -54,13 +55,14 @@
     return pl.CostEstimate(flops=flops, bytes_accessed=moved, transcendentals=exps)
 
 
-def call(body, outs, ins, out_specs=None, scratch=(), **work):
+def call(body, outs, ins, out_specs=None, scratch=(), aliases=None, **work):
     return pl.pallas_call(
         body,
         out_shape=outs,
         in_specs=ins,
         out_specs=out_specs or [VMEM] * len(outs),
         scratch_shapes=scratch,
+        input_output_aliases=aliases or {},
         compiler_params=limits(),
         cost_estimate=cost(**work),
     )
@@ -123,7 +125,7 @@
 
 
 def first_kernel(
-    own_ref, other_ref, weight_ref, kernel_out, unit_ref, sent_out, scale_ref, features_ref,
+    own_ref, other_ref, weight_ref, kernel_out, near_ref, unit_ref, sent_out, scale_ref, features_ref,
     teacher_ref, stage_ref, sent_ref, mass_ref, sem_ref, sent_sem,
 ):
     me, core = lax.axis_index("smp"), lax.rem(lax.axis_index("proto"), 2)
@@ -157,29 +159,42 @@
     by_core(teacher_units)
     mass_ref[...] = jnp.zeros_like(mass_ref)
 
-    @pl.loop(0, ROWS // WIDE)
-    def _(i):
-        rows = pl.ds(pl.multiple_of(i * WIDE, WIDE), WIDE)
+    def tile(rows, kept_ref, kept_rows):
         kernel = jnp.exp(
             jnp.dot(weight_ref[rows, :], teacher_ref[...], preferred_element_type=f32) * (1.0 / TEACHER_TEMP)
         )
-        stage_ref[rows, :] = kernel
-        copy_out(i).start()
+        kept_ref[kept_rows, :] = kernel
         row_scale = 1.0 / (K * jnp.sum(kernel, axis=1, keepdims=True))
         mass_ref[...] += folded(kernel * row_scale)
 
+    @pl.loop(0, FAR // WIDE)
+    def _(i):
+        rows = pl.ds(pl.multiple_of(i * WIDE, WIDE), WIDE)
+        tile(rows, stage_ref, rows)
+        copy_out(i).start()
+
+    tile(pl.ds(FAR, ROWS - FAR), near_ref, pl.ds(0, ROWS - FAR))
     sent_ref[...] = jnp.broadcast_to(as_blocks(mass_ref[...]).astype(bf16)[None], sent_ref.shape)
     sent_copy = pltpu.make_async_copy(sent_ref, sent_out, sent_sem)
     sent_copy.start()
     by_core(student_units)
     sent_copy.wait()
+    for i in range(FAR // WIDE):
+        copy_out(i).wait()
+
+
+def student_kernel(
+    unit_ref, weight_far, near_ref, kernel_ref, logits_out, own_out, total_ref, kernel_out,
+    weight_ref, stage_ref, own_ref, sum_ref, sem_ref, own_sem, weight_sem, near_sem,
+):
+    def copy_in(i):
+        rows = pl.ds(pl.multiple_of(i * WIDE, WIDE), WIDE)
+        return pltpu.make_async_copy(weight_far.at[rows], weight_ref.at[rows], weight_sem.at[i])
+
     for i in range(ROWS // WIDE):
-        copy_out(i).wait()
-
-
-def student_kernel(
-    unit_ref, weight_ref, logits_out, own_out, total_ref, stage_ref, own_ref, sum_ref, sem_ref, own_sem
-):
+        copy_in(i).start()
+    near_copy = pltpu.make_async_copy(near_ref, kernel_out.at[pl.ds(FAR, ROWS - FAR)], near_sem)
+    near_copy.start()
     sum_ref[...] = jnp.zeros_like(sum_ref)
     lanes = pl.ds(pl.multiple_of(lax.axis_index("smp") * 128, 128), 128)
 
@@ -192,6 +207,7 @@
 
     @pl.loop(0, ROWS // WIDE)
     def _(i):
+        copy_in(i).wait()
         rows = pl.ds(pl.multiple_of(i * WIDE, WIDE), WIDE)
         logits = jnp.dot(weight_ref[rows, :], unit_ref[...], preferred_element_type=f32) * (1.0 / STUDENT_TEMP)
         stage_ref[rows, :] = logits
@@ -204,28 +220,40 @@
     for i in range(ROWS // WIDE):
         for copy in copies(i):
             copy.wait()
+    near_copy.wait()
 
 
 def received(got_ref):
     return jnp.sum(got_ref[...].astype(f32), axis=0)
 
 
-def second_kernel(got_ref, far_ref, total_ref, kernel_ref, sent_ref, kept_ref, col_ref, mass_ref, sem_ref):
+def second_kernel(
+    got_ref, far_ref, near_ref, total_ref, kernel_ref, sent_ref, kept_ref, col_ref, mass_ref, sem_ref
+):
     def copy_in(i):
         rows = pl.ds(pl.multiple_of(i * TILE, TILE), TILE)
         return pltpu.make_async_copy(far_ref.at[rows], kernel_ref.at[rows], sem_ref.at[i])
 
-    for i in range(ROWS // TILE):
+    for i in range(FAR // TILE):
         copy_in(i).start()
     col_ref[...] = as_row(1.0 / (B * received(got_ref)))
     mass_ref[...] = jnp.zeros_like(mass_ref)
 
-    @pl.loop(0, ROWS // TILE)
+    def add(kernel):
+        row_scale = 1.0 / (K * jnp.sum(kernel * col_ref[...], axis=1, keepdims=True))
+        mass_ref[...] += folded(kernel * row_scale)
+
+    @pl.loop(0, (ROWS - FAR) // TILE)
+    def _(i):
+        start = pl.multiple_of(i * TILE, TILE)
+        kernel = near_ref[pl.ds(start, TILE), :]
+        kernel_ref[pl.ds(FAR + start, TILE), :] = kernel
+        add(kernel)
+
+    @pl.loop(0, FAR // TILE)
     def _(i):
         copy_in(i).wait()
-        kernel = kernel_ref[pl.ds(pl.multiple_of(i * TILE, TILE), TILE), :]
-        row_scale = 1.0 / (K * jnp.sum(kernel * col_ref[...], axis=1, keepdims=True))
-        mass_ref[...] += folded(kernel * row_scale)
+        add(kernel_ref[pl.ds(pl.multiple_of(i * TILE, TILE), TILE), :])
 
     mass = as_blocks(mass_ref[...]).astype(bf16).astype(f32)
     kept_ref[...] = mass
@@ -243,9 +271,15 @@
 
 
 def third_kernel(
-    got_ref, kernel_ref, kept_ref, logits_ref, features_ref, weight_ref,
-    sent_ref, total_ref, before_ref, col_ref, mass_ref, scaled_ref, pair_ref,
-):
+    got_ref, kernel_ref, kept_ref, features_ref, logits_far, weight_far,
+    sent_ref, total_ref, before_ref, col_ref, mass_ref, scaled_ref, pair_ref, logits_ref, weight_ref, sem_ref,
+):
+    copies = [pltpu.make_async_copy(logits_far, logits_ref, sem_ref.at[0])]
+    for i in range(ROWS // WIDE):
+        rows = pl.ds(i * WIDE, WIDE)
+        copies.append(pltpu.make_async_copy(weight_far.at[rows], weight_ref.at[rows], sem_ref.at[1 + i]))
+    for copy in copies:
+        copy.start()
     me = lax.axis_index("smp")
     got = received(got_ref)
     before_ref[...] = got[:8, :]
@@ -263,6 +297,7 @@
         mass_ref[...] += folded(kernel * row_scale)
 
     change = as_blocks(mass_ref[...]) - kept_ref[...]
+    copies[0].wait()
     logits = logits_ref[...]
     own_col = 1.0 / before_ref[pl.ds(me, 1), :]
     own_total = 1.0 / total_ref[pl.ds(me, 1), :]
@@ -270,6 +305,8 @@
     weighted = jnp.sum(folded(targets * logits), axis=0, keepdims=True)
     pair_ref[:, :128] = ((jnp.exp(logits) * own_total - targets) * SHARE).astype(bf16)
     pair_ref[:, 128:] = (targets * SHARE).astype(bf16)
+    for copy in copies[1:]:
+        copy.wait()
     parts = lax.dot_general(
         pair_ref[...], weight_ref[...], (((0,), (0,)), ((), ())), preferred_element_type=f32
     )
@@ -374,45 +411,49 @@
     (weight_near,) = call(
         fetch_kernel, [pltpu.VMEM((ROWS, D), bf16)], [ANY], None, [wide_sems], moved=4 * 2**20
     )(far(teacher_weight))
-    kernel, student_unit, sent_1, student_scale, features_own = call(
+    kernel, kernel_end, student_unit, sent_1, student_scale, features_own = call(
         first_kernel,
-        [pltpu.HBM((ROWS, B), f32), shape((D, B), bf16), pltpu.HBM((64, 8, 128), bf16), shape((8, 128)),
+        [pltpu.HBM((ROWS, B), f32), pltpu.VMEM((ROWS - FAR, B), f32), shape((D, B), bf16),
+         pltpu.HBM((64, 8, 128), bf16), shape((8, 128)),
          shape((D, 128))],
         [VMEM, VMEM, VMEM],
-        [ANY, VMEM, ANY, VMEM, VMEM],
-        [pltpu.VMEM((D, B), bf16), stage, pltpu.VMEM((64, 8, 128), bf16), rows8, wide_sems,
+        [ANY, VMEM, VMEM, ANY, VMEM, VMEM],
+        [pltpu.VMEM((D, B), bf16), pltpu.VMEM((FAR, B), f32), pltpu.VMEM((64, 8, 128), bf16), rows8, wide_sems,
          pltpu.SemaphoreType.DMA],
         **matmul,
     )(second, other, weight_near)
     got_1 = sent_to_protos(sent_1)
-    logits, logits_own, local_total = call(
+    logits, logits_own, local_total, kernel = call(
         student_kernel,
-        [pltpu.HBM((ROWS, B), f32), pltpu.HBM((ROWS, 128), f32), shape((8, 128))],
-        [VMEM, VMEM],
-        [ANY, ANY, VMEM],
-        [stage, pltpu.VMEM((ROWS, 128), f32), rows8, wide_sems, wide_sems],
+        [pltpu.HBM((ROWS, B), f32), pltpu.HBM((ROWS, 128), f32), shape((8, 128)), pltpu.HBM((ROWS, B), f32)],
+        [VMEM, ANY, VMEM, ANY],
+        [ANY, ANY, VMEM, ANY],
+        [pltpu.VMEM((ROWS, D), bf16), stage, pltpu.VMEM((ROWS, 128), f32), rows8, wide_sems, wide_sems, wide_sems,
+         pltpu.SemaphoreType.DMA],
+        {3: 3},
         **matmul,
-    )(student_unit, student_weight)
+    )(student_unit, far(student_weight), kernel_end, far(kernel))
     kernel_near, sent_2, kept = call(
         second_kernel,
         [pltpu.VMEM((ROWS, B), f32), shape((64, 16, 128), bf16), shape((8, 128))],
-        [VMEM, ANY, VMEM],
+        [VMEM, ANY, VMEM, VMEM],
         None,
         [row, rows8, near_sems],
         flops=4 * ROWS * B,
         moved=8 * 2**20,
-    )(got_1, far(kernel), local_total)
+    )(got_1, far(kernel), kernel_end, local_total)
     got_2 = sent_to_protos(sent_2)
     sent_3, total, before = call(
         third_kernel,
         [shape((64, 32, 128), bf16), shape((8, 128)), shape((8, 128))],
-        [VMEM] * 6,
+        [VMEM] * 4 + [ANY] * 2,
         None,
-        [row, rows8, pltpu.VMEM((ROWS, 128), f32), pltpu.VMEM((ROWS, 256), bf16)],
+        [row, rows8, pltpu.VMEM((ROWS, 128), f32), pltpu.VMEM((ROWS, 256), bf16), pltpu.VMEM((ROWS, 128), f32),
+         pltpu.VMEM((ROWS, D), bf16), pltpu.SemaphoreType.DMA((1 + ROWS // WIDE,))],
         flops=2 * ROWS * 256 * D,
         moved=12 * 2**20,
         exps=ROWS * 128,
-    )(got_2, kernel_near, kept, logits_own, features_own, student_weight)
+    )(got_2, kernel_near, kept, features_own, far(logits_own), far(student_weight))
     got_3 = sent_to_protos(sent_3)
     partial, targets_near, targets_far, unit_slice = streamed(
         weight_kernel,
@@ -426,7 +467,7 @@
         flops=2 * ROWS * B * 64,
         moved=21 * 2**20,
         exps=ROWS * B,
-    )(far(kernel), far(logits), total, before, student_unit)
+    )(far(kernel), far(logits), total, before, far(student_unit))
     grad_features, loss, grad_weight = call(
         final_kernel,
         [shape((8, 128)), shape((1, 128)), shape((64, ROWS))],

time: 128 us -> 129 us (level)
  blocking collectives: 61.4 us -> 62.9 us
    pallas_call x1, Pallas kernels: 4.47 us -> 5.97 us  [on_device(): call(student_kernel, [pltpu.HBM((ROWS, B), f32), pltpu.HBM((ROWS, 128), f...]
    all_to_all x1, blocking collectives: 16.7 us -> 18.2 us  [sent_to_protos(): return lax.all_to_all(x, 'proto', 0, 0, tiled=True)]
  transfers between devices with their start and end apart: 3 -> 3, of which waited for: 3 -> 3; matrix products, arithmetic and copies ran while one was open for 0% -> 0% of each run, Pallas kernels for 14% -> 15%
where the time goes in v10:
time: 129 us; the launch traced here: 128 us
  blocking collectives  62.9 us (49%)
  Pallas kernels  35.3 us (27%)
  starting transfers between devices  18.1 us (14%)
  waiting for transfers between devices  9.98 us (8%)
    all_to_all x2, blocking collectives, gathered(): lax.all_to_all(copies, BOTH, 0, 0, tiled=True, axis_index_groups=group)  44.7 us
    all_to_all x1, blocking collectives, sent_to_protos(): return lax.all_to_all(x, 'proto', 0, 0, tiled=True)  18.2 us
    pallas_call x1, Pallas kernels, on_device(): streamed(weight_kernel, [shape((64, ROWS)), pltpu.VMEM((HALF * TILE, B),...  11.9 us
    all_to_all x2, starting transfers between devices, sent_to_protos(): return lax.all_to_all(x, 'proto', 0, 0, tiled=True)  11.6 us
    all_to_all x2, waiting for transfers between devices, sent_to_protos(): return lax.all_to_all(x, 'proto', 0, 0, tiled=True)  9.27 us
    ppermute x1, starting transfers between devices, on_device(): other = lax.ppermute(second, 'proto', [(i, i ^ 1) for i in range(64)])  6.53 us
    pallas_call x1, Pallas kernels, on_device(): call(student_kernel, [pltpu.HBM((ROWS, B), f32), pltpu.HBM((ROWS, 128), f...  5.97 us
    pallas_call x1, Pallas kernels, on_device(): call(first_kernel, [pltpu.HBM((ROWS, B), f32), pltpu.VMEM((ROWS - FAR, B)...  4.96 us
  transfers between devices with their start and end apart: 3, of which 3 were waited for; matrix products, arithmetic and copies ran while one was open for 0% of the time, Pallas kernels for 15%

profile of v10, /device:TPU:1, one launch (start us, length us, event | category | flops | bytes accessed | tf_op | source)
XLA Modules:
  0.0 127.9 jit_solution(14096304979751785242)
XLA Ops:
  0.6 0.7 pad_maximum_fusion
  1.4 29.5 %all_to_all.25 = bf16[64,16,128]{2,1,0:T(8,128)(2,1)S(1)} all-to-all(bf16[64,16,128]{2,1,0:T(8,128)(2,1)S(1)} %broadcast_in_dim.4), channel_id=1, replica_groups={{0,2,4,6,8,10,12,14,16,18,20,22,24,26,28,30,32,34,36,38,40,42,44,46,48,..., dimensions={0} | all-to-all | bytes 524288 | tf_op jit(solution)/shard_map/all_to_all | solution.py:39
  30.9 0.1 broadcast_in_dim.5
  31.0 15.2 %all_to_all.26.own_ref = bf16[4,64,16,128]{3,2,1,0:T(8,128)(2,1)S(1)} all-to-all(bf16[4,64,16,128]{3,2,1,0:T(8,128)(2,1)S(1)} %broadcast_in_dim.5), channel_id=1, replica_groups={{0,128,256,384},{1,129,257,385},{2,130,258,386},{3,131,259,387},{4,132,..., dimensions={0} | all-to-all | bytes 2097152 | tf_op jit(solution)/shard_map/all_to_all | solution.py:39
  46.2 6.5 %collective-permute-start = (bf16[4,64,16,128]{3,2,1,0:T(8,128)(2,1)S(1)}, bf16[4,64,16,128]{3,2,1,0:T(8,128)(2,1)S(1)}, u32[]{:S(2)}, u32[]{:S(2)}) collective-permute-start(bf16[4,64,16,128]{3,2,1,0:T(8,128)(2,1)S(1)} %all_to_all.26.own_ref), channel_id=1, source_target_pairs={{0,1},{1,0},{2,3},{3,2},{4,5},{5,4},{6,7},{7,6},{8,9},{9,8},{10,11... | collective-permute-start | bytes 3145736 | tf_op jit(solution)/shard_map/ppermute | solution.py:404
  52.8 1.6 %shard_map.67.weight_ref = bf16[2048,512]{1,0:T(8,128)(2,1)S(1)} custom-call(bf16[2048,512]{1,0:T(8,128)(2,1)} %far_ref), custom_call_target="tpu_custom_call" | custom-call | bytes 4194304 | tf_op jit(solution)/shard_map/pallas_call | solution.py:411
  54.3 0.7 collective-permute-done.other_ref
  55.0 5.0 %shard_map.68 = (f32[2048,1024]{1,0:T(8,128)}, f32[512,1024]{1,0:T(8,128)S(1)}, bf16[512,1024]{1,0:T(8,128)(2,1)S(1)}, bf16[64,8,128]{2,1,0:T(8,128)(2,1)}, f32[...) custom-call(bf16[4,64,16,128]{3,2,1,0:T(8,128)(2,1)S(1)} %all_to_all.26.own_ref, ...), custom_call_target="tpu_custom_call" | custom-call | flops 2147483648 | bytes 12582912 | tf_op jit(solution)/shard_map/pallas_call | solution.py:414
  60.0 0.0 copy-start
  60.0 5.6 %all-to-all-start.2 = ((bf16[64,8,128]{2,1,0:T(8,128)(2,1)}), bf16[64,8,128]{2,1,0:T(8,128)(2,1)S(1)}, u32[]{:S(2)}, u32[]{:S(2)}) async-start(bf16[64,8,128]{2,1,0:T(8,128)(2,1)} %get-tuple-element.30), calls=%async_computation.2 | async-start | bytes 262144 | tf_op jit(solution)/shard_map/all_to_all | solution.py:43
  65.6 6.0 %shard_map.69 = (f32[2048,1024]{1,0:T(8,128)}, f32[2048,128]{1,0:T(8,128)}, f32[8,128]{1,0:T(8,128)S(1)}, f32[2048,1024]{1,0:T(8,128)}) custom-call(bf16[512,1024]{1,0:T(8,128)(2,1)S(1)} %get-tuple-element.31.unit_ref, bf16[2048,512]{1,0:T(8,128)(2,1)} %weight_far.3, f32[512,1024]{1,0:T(8,128)S(1)} %get-tuple-element.32.near_ref, ...), custom_call_target="tpu_custom_call", output_to_operand_aliasing={{3}: (3, {})} | custom-call | flops 2147483648 | bytes 12582912 | tf_op jit(solution)/shard_map/pallas_call | solution.py:426
  71.6 0.0 copy-done
  71.6 4.0 %all-to-all-done.2.got_ref = bf16[64,8,128]{2,1,0:T(8,128)(2,1)S(1)} async-done(((bf16[64,8,128]{2,1,0:T(8,128)(2,1)}), bf16[64,8,128]{2,1,0:T(8,128)(2,1)S(1)}, u32[]{:S(2)}, u32[]{:S(2)}) %all-to-all-start.2) | async-done | bytes 131104 | tf_op jit(solution)/shard_map/all_to_all | solution.py:43
  75.6 3.1 %shard_map.70 = (f32[2048,1024]{1,0:T(8,128)S(1)}, bf16[64,16,128]{2,1,0:T(8,128)(2,1)S(1)}, f32[8,128]{1,0:T(8,128)S(1)}) custom-call(bf16[64,8,128]{2,1,0:T(8,128)(2,1)S(1)} %all-to-all-done.2.got_ref, f32[2048,1024]{1,0:T(8,128)} %get-tuple-element.34.far_ref.kernel_ref, f32[512,1024]{1,0:T(8,128)S(1)} %get-tuple-element.32.near_ref, ...), custom_call_target="tpu_custom_call" | custom-call | flops 8388608 | bytes 8388608 | tf_op jit(solution)/shard_map/pallas_call | solution.py:436
  78.7 18.2 %all_to_all.27.got_ref = bf16[64,16,128]{2,1,0:T(8,128)(2,1)S(1)} all-to-all(bf16[64,16,128]{2,1,0:T(8,128)(2,1)S(1)} %get-tuple-element.36), channel_id=1, replica_groups=mesh['smp'=8,'proto'=64] {'proto'}, dimensions={0} | all-to-all | bytes 524288 | tf_op jit(solution)/shard_map/all_to_all | solution.py:43
  96.9 3.7 %shard_map.71 = (bf16[64,32,128]{2,1,0:T(8,128)(2,1)}, f32[8,128]{1,0:T(8,128)S(1)}, f32[8,128]{1,0:T(8,128)S(1)}) custom-call(bf16[64,16,128]{2,1,0:T(8,128)(2,1)S(1)} %all_to_all.27.got_ref, f32[2048,1024]{1,0:T(8,128)S(1)} %get-tuple-element.37.kernel_ref, f32[8,128]{1,0:T(8,128)S(1)} %get-tuple-element.38.kept_ref, ...), custom_call_target="tpu_custom_call" | custom-call | flops 536870912 | bytes 12582912 | tf_op jit(solution)/shard_map/pallas_call | solution.py:446
  100.6 6.0 %all-to-all-start.4 = ((bf16[64,32,128]{2,1,0:T(8,128)(2,1)}), bf16[64,32,128]{2,1,0:T(8,128)(2,1)S(1)}, u32[]{:S(2)}, u32[]{:S(2)}) async-start(bf16[64,32,128]{2,1,0:T(8,128)(2,1)} %get-tuple-element.41), calls=%async_computation.4 | async-start | bytes 1048576 | tf_op jit(solution)/shard_map/all_to_all | solution.py:43
  106.6 0.0 copy-start.1
  106.6 11.9 %shard_map.72 = (f32[64,2048]{1,0:T(8,128)S(1)}, bf16[1024,1024]{1,0:T(8,128)(2,1)S(1)}, bf16[1024,1024]{1,0:T(8,128)(2,1)}, bf16[64,1024]{1,0:T(8,128)(2,1)S(1)}) custom-call(f32[2048,1024]{1,0:T(8,128)} %get-tuple-element.34.far_ref.kernel_ref, f32[2048,1024]{1,0:T(8,128)} %get-tuple-element.45.logits_ref, f32[8,128]{1,0:T(8,128)S(1)} %get-tuple-element.43.total_ref, ...), custom_call_target="tpu_custom_call" | custom-call | flops 268435456 | bytes 22020096 | tf_op jit(solution)/shard_map/pallas_call | solution.py:458
  118.5 5.3 %all-to-all-done.4.got_ref = bf16[64,32,128]{2,1,0:T(8,128)(2,1)S(1)} async-done(((bf16[64,32,128]{2,1,0:T(8,128)(2,1)}), bf16[64,32,128]{2,1,0:T(8,128)(2,1)S(1)}, u32[]{:S(2)}, u32[]{:S(2)}) %all-to-all-start.4) | async-done | bytes 524320 | tf_op jit(solution)/shard_map/all_to_all | solution.py:43
  123.7 0.0 copy-done.1
  123.7 4.2 %shard_map.73 = (f32[8,128]{1,0:T(8,128)}, f32[1,128]{1,0:T(1,128)}, f32[64,2048]{1,0:T(8,128)}) custom-call(bf16[64,32,128]{2,1,0:T(8,128)(2,1)S(1)} %all-to-all-done.4.got_ref, bf16[8,128]{1,0:T(8,128)(2,1)S(1)} %bitcast.6, f32[8,128]{1,0:T(8,128)S(1)} %get-tuple-element.42.scale_ref, f32[8,128]{1,0:T(8,128)S(1)} %get-tuple-element.43.total_ref, ...), custom_call_target="tpu_custom_call" | custom-call | flops 268435456 | bytes 5242880 | tf_op jit(solution)/shard_map/pallas_call | solution.py:471
  (1 shorter events, 0.0 us)
Async XLA Ops:
  46.2 8.8 %collective-permute-start = (bf16[4,64,16,128]{3,2,1,0:T(8,128)(2,1)S(1)}, bf16[4,64,16,128]{3,2,1,0:T(8,128)(2,1)S(1)}, u32[]{:S(2)}, u32[]{:S(2)}) collective-permute-start(bf16[4,64,16,128]{3,2,1,0:T(8,128)(2,1)S(1)} %all_to_all.26.own_ref), channel_id=1, source_target_pairs={{0,1},{1,0},{2,3},{3,2},{4,5},{5,4},{6,7},{7,6},{8,9},{9,8},{10,11... | collective-permute-start | bytes 3145736 | tf_op jit(solution)/shard_map/ppermute | solution.py:404
  60.0 11.6 %copy-start = (bf16[512,1024]{1,0:T(8,128)(2,1)}, bf16[512,1024]{1,0:T(8,128)(2,1)S(1)}, u32[]{:S(2)}) copy-start(bf16[512,1024]{1,0:T(8,128)(2,1)S(1)} %get-tuple-element.31.unit_ref) | copy-start | bytes 3145732
  60.0 15.6 %all-to-all-start.2 = ((bf16[64,8,128]{2,1,0:T(8,128)(2,1)}), bf16[64,8,128]{2,1,0:T(8,128)(2,1)S(1)}, u32[]{:S(2)}, u32[]{:S(2)}) async-start(bf16[64,8,128]{2,1,0:T(8,128)(2,1)} %get-tuple-element.30), calls=%async_computation.2 | async-start | bytes 262144 | tf_op jit(solution)/shard_map/all_to_all | solution.py:43
  100.6 23.2 %all-to-all-start.4 = ((bf16[64,32,128]{2,1,0:T(8,128)(2,1)}), bf16[64,32,128]{2,1,0:T(8,128)(2,1)S(1)}, u32[]{:S(2)}, u32[]{:S(2)}) async-start(bf16[64,32,128]{2,1,0:T(8,128)(2,1)} %get-tuple-element.41), calls=%async_computation.4 | async-start | bytes 1048576 | tf_op jit(solution)/shard_map/all_to_all | solution.py:43
  106.6 17.1 %copy-start.1 = (bf16[128,8]{0,1:T(8,128)(2,1)S(1)}, bf16[128,8]{0,1:T(8,128)(2,1)}, u32[]{:S(2)}) copy-start(bf16[128,8]{0,1:T(8,128)(2,1)} %param.5) | copy-start | bytes 6148

commit v11 on v10

--- a/solution.py
+++ b/solution.py
@@ -184,8 +184,8 @@
 
 
 def student_kernel(
-    unit_ref, weight_far, near_ref, kernel_ref, logits_out, own_out, total_ref, kernel_out,
-    weight_ref, stage_ref, own_ref, sum_ref, sem_ref, own_sem, weight_sem, near_sem,
+    unit_ref, weight_far, near_ref, kernel_ref, own_out, total_ref, kernel_out,
+    weight_ref, stage_ref, own_ref, sum_ref, own_sem, weight_sem, near_sem,
 ):
     def copy_in(i):
         rows = pl.ds(pl.multiple_of(i * WIDE, WIDE), WIDE)
@@ -198,28 +198,23 @@
     sum_ref[...] = jnp.zeros_like(sum_ref)
     lanes = pl.ds(pl.multiple_of(lax.axis_index("smp") * 128, 128), 128)
 
-    def copies(i):
+    def copy_out(i):
         rows = pl.ds(pl.multiple_of(i * WIDE, WIDE), WIDE)
-        return (
-            pltpu.make_async_copy(stage_ref.at[rows], logits_out.at[rows], sem_ref.at[i]),
-            pltpu.make_async_copy(own_ref.at[rows], own_out.at[rows], own_sem.at[i]),
-        )
+        return pltpu.make_async_copy(own_ref.at[rows], own_out.at[rows], own_sem.at[i])
 
     @pl.loop(0, ROWS // WIDE)
     def _(i):
         copy_in(i).wait()
         rows = pl.ds(pl.multiple_of(i * WIDE, WIDE), WIDE)
         logits = jnp.dot(weight_ref[rows, :], unit_ref[...], preferred_element_type=f32) * (1.0 / STUDENT_TEMP)
-        stage_ref[rows, :] = logits
-        own_ref[rows, :] = stage_ref[rows, lanes]
-        for copy in copies(i):
-            copy.start()
+        stage_ref[...] = logits
+        own_ref[rows, :] = stage_ref[:, lanes]
+        copy_out(i).start()
         sum_ref[...] += folded(jnp.exp(logits))
 
     total_ref[...] = as_blocks(sum_ref[...])
     for i in range(ROWS // WIDE):
-        for copy in copies(i):
-            copy.wait()
+        copy_out(i).wait()
     near_copy.wait()
 
 
@@ -329,7 +324,7 @@
 
 
 def weight_kernel(
-    kernel_ref, logits_ref, total_ref, before_ref, unit_ref, out_ref, near_ref, far_ref, slice_ref, rows_ref
+    kernel_ref, weight_ref, total_ref, before_ref, unit_ref, out_ref, near_ref, far_ref, slice_ref, rows_ref
 ):
     @pl.when(pl.program_id(0) == 0)
     def _():
@@ -340,7 +335,8 @@
     kernel = kernel_ref[...]
     row_scale = 1.0 / (K * jnp.sum(kernel * rows_ref[0:1, :], axis=1, keepdims=True))
     targets = kernel * row_scale * rows_ref[1:2, :]
-    probs = jnp.exp(logits_ref[...]) * rows_ref[2:3, :]
+    logits = jnp.dot(weight_ref[...], unit_ref[...], preferred_element_type=f32) * (1.0 / STUDENT_TEMP)
+    probs = jnp.exp(logits) * rows_ref[2:3, :]
     grad = ((probs - targets) * SHARE).astype(bf16)
     shared = (targets * SHARE).astype(bf16)
 
@@ -403,7 +399,6 @@
     second, teacher_weight = lax.optimization_barrier((second, teacher_weight))
     other = lax.ppermute(second, "proto", [(i, i ^ 1) for i in range(64)])
 
-    stage = pltpu.VMEM((ROWS, B), f32)
     wide_sems, near_sems = pltpu.SemaphoreType.DMA((ROWS // WIDE,)), pltpu.SemaphoreType.DMA((ROWS // TILE,))
     row, rows8 = pltpu.VMEM((1, B), f32), pltpu.VMEM((8, B), f32)
     rows8_small = pltpu.VMEM((8, 128), f32)
@@ -423,14 +418,14 @@
         **matmul,
     )(second, other, weight_near)
     got_1 = sent_to_protos(sent_1)
-    logits, logits_own, local_total, kernel = call(
+    logits_own, local_total, kernel = call(
         student_kernel,
-        [pltpu.HBM((ROWS, B), f32), pltpu.HBM((ROWS, 128), f32), shape((8, 128)), pltpu.HBM((ROWS, B), f32)],
+        [pltpu.HBM((ROWS, 128), f32), shape((8, 128)), pltpu.HBM((ROWS, B), f32)],
         [VMEM, ANY, VMEM, ANY],
-        [ANY, ANY, VMEM, ANY],
-        [pltpu.VMEM((ROWS, D), bf16), stage, pltpu.VMEM((ROWS, 128), f32), rows8, wide_sems, wide_sems, wide_sems,
-         pltpu.SemaphoreType.DMA],
-        {3: 3},
+        [ANY, VMEM, ANY],
+        [pltpu.VMEM((ROWS, D), bf16), pltpu.VMEM((WIDE, B), f32), pltpu.VMEM((ROWS, 128), f32), rows8, wide_sems,
+         wide_sems, pltpu.SemaphoreType.DMA],
+        {3: 2},
         **matmul,
     )(student_unit, far(student_weight), kernel_end, far(kernel))
     kernel_near, sent_2, kept = call(
@@ -459,15 +454,15 @@
         weight_kernel,
         [shape((64, ROWS)), pltpu.VMEM((HALF * TILE, B), bf16), pltpu.HBM((ROWS - HALF * TILE, B), bf16),
          shape((64, B), bf16)],
-        [stripe(B), stripe(B), whole(8, 128), whole(8, 128), whole(D, B)],
+        [stripe(B), stripe(D), whole(8, 128), whole(8, 128), whole(D, B)],
         [pl.BlockSpec((64, TILE), lambda i: (0, i)),
          pl.BlockSpec((TILE, B), lambda i: (jnp.minimum(i, HALF - 1), 0)),
          pl.BlockSpec((TILE, B), lambda i: (jnp.maximum(i - HALF, 0), 0)), whole(64, B)],
         [rows8],
-        flops=2 * ROWS * B * 64,
-        moved=21 * 2**20,
+        flops=2 * ROWS * B * (64 + D),
+        moved=15 * 2**20,
         exps=ROWS * B,
-    )(far(kernel), far(logits), total, before, far(student_unit))
+    )(far(kernel), far(student_weight), total, before, far(student_unit))
     grad_features, loss, grad_weight = call(
         final_kernel,
         [shape((8, 128)), shape((1, 128)), shape((64, ROWS))],

time: 129 us -> 128 us (level)
  transfers between devices with their start and end apart: 3 -> 3, of which waited for: 3 -> 3; matrix products, arithmetic and copies ran while one was open for 0% -> 0% of each run, Pallas kernels for 15% -> 14%
where the time goes in v11:
time: 128 us; the launch traced here: 127 us
  blocking collectives  62.2 us (49%)
  Pallas kernels  34.2 us (27%)
  starting transfers between devices  18.1 us (14%)
  waiting for transfers between devices  11 us (9%)
    all_to_all x2, blocking collectives, gathered(): lax.all_to_all(copies, BOTH, 0, 0, tiled=True, axis_index_groups=group)  44.7 us
    all_to_all x1, blocking collectives, sent_to_protos(): return lax.all_to_all(x, 'proto', 0, 0, tiled=True)  17.4 us
    all_to_all x2, starting transfers between devices, sent_to_protos(): return lax.all_to_all(x, 'proto', 0, 0, tiled=True)  11.6 us
    pallas_call x1, Pallas kernels, on_device(): streamed(weight_kernel, [shape((64, ROWS)), pltpu.VMEM((HALF * TILE, B),...  11.6 us
    all_to_all x2, waiting for transfers between devices, sent_to_protos(): return lax.all_to_all(x, 'proto', 0, 0, tiled=True)  10.3 us
    ppermute x1, starting transfers between devices, on_device(): other = lax.ppermute(second, 'proto', [(i, i ^ 1) for i in range(64)])  6.53 us
    pallas_call x1, Pallas kernels, on_device(): call(student_kernel, [pltpu.HBM((ROWS, 128), f32), shape((8, 128)), pltpu...  5.24 us
    pallas_call x1, Pallas kernels, on_device(): call(first_kernel, [pltpu.HBM((ROWS, B), f32), pltpu.VMEM((ROWS - FAR, B)...  4.93 us
  transfers between devices with their start and end apart: 3, of which 3 were waited for; matrix products, arithmetic and copies ran while one was open for 0% of the time, Pallas kernels for 14%

profile of v11, /device:TPU:1, one launch (start us, length us, event | category | flops | bytes accessed | tf_op | source)
XLA Modules:
  0.0 127.2 jit_solution(2257052794819738352)
XLA Ops:
  0.6 0.7 pad_maximum_fusion
  1.4 29.5 %all_to_all.25 = bf16[64,16,128]{2,1,0:T(8,128)(2,1)S(1)} all-to-all(bf16[64,16,128]{2,1,0:T(8,128)(2,1)S(1)} %broadcast_in_dim.4), channel_id=1, replica_groups={{0,2,4,6,8,10,12,14,16,18,20,22,24,26,28,30,32,34,36,38,40,42,44,46,48,..., dimensions={0} | all-to-all | bytes 524288 | tf_op jit(solution)/shard_map/all_to_all | solution.py:39
  30.9 0.1 broadcast_in_dim.5
  31.0 15.2 %all_to_all.26.own_ref = bf16[4,64,16,128]{3,2,1,0:T(8,128)(2,1)S(1)} all-to-all(bf16[4,64,16,128]{3,2,1,0:T(8,128)(2,1)S(1)} %broadcast_in_dim.5), channel_id=1, replica_groups={{0,128,256,384},{1,129,257,385},{2,130,258,386},{3,131,259,387},{4,132,..., dimensions={0} | all-to-all | bytes 2097152 | tf_op jit(solution)/shard_map/all_to_all | solution.py:39
  46.2 6.5 %collective-permute-start = (bf16[4,64,16,128]{3,2,1,0:T(8,128)(2,1)S(1)}, bf16[4,64,16,128]{3,2,1,0:T(8,128)(2,1)S(1)}, u32[]{:S(2)}, u32[]{:S(2)}) collective-permute-start(bf16[4,64,16,128]{3,2,1,0:T(8,128)(2,1)S(1)} %all_to_all.26.own_ref), channel_id=1, source_target_pairs={{0,1},{1,0},{2,3},{3,2},{4,5},{5,4},{6,7},{7,6},{8,9},{9,8},{10,11... | collective-permute-start | bytes 3145736 | tf_op jit(solution)/shard_map/ppermute | solution.py:400
  52.8 1.6 %shard_map.67.weight_ref = bf16[2048,512]{1,0:T(8,128)(2,1)S(1)} custom-call(bf16[2048,512]{1,0:T(8,128)(2,1)} %far_ref), custom_call_target="tpu_custom_call" | custom-call | bytes 4194304 | tf_op jit(solution)/shard_map/pallas_call | solution.py:406
  54.3 0.7 collective-permute-done.other_ref
  55.0 4.9 %shard_map.68 = (f32[2048,1024]{1,0:T(8,128)}, f32[512,1024]{1,0:T(8,128)S(1)}, bf16[512,1024]{1,0:T(8,128)(2,1)S(1)}, bf16[64,8,128]{2,1,0:T(8,128)(2,1)}, f32[...) custom-call(bf16[4,64,16,128]{3,2,1,0:T(8,128)(2,1)S(1)} %all_to_all.26.own_ref, ...), custom_call_target="tpu_custom_call" | custom-call | flops 2147483648 | bytes 12582912 | tf_op jit(solution)/shard_map/pallas_call | solution.py:409
  60.0 0.0 copy-start
  60.0 5.6 %all-to-all-start.2 = ((bf16[64,8,128]{2,1,0:T(8,128)(2,1)}), bf16[64,8,128]{2,1,0:T(8,128)(2,1)S(1)}, u32[]{:S(2)}, u32[]{:S(2)}) async-start(bf16[64,8,128]{2,1,0:T(8,128)(2,1)} %get-tuple-element.29), calls=%async_computation.2 | async-start | bytes 262144 | tf_op jit(solution)/shard_map/all_to_all | solution.py:43
  65.6 5.2 %shard_map.69 = (f32[2048,128]{1,0:T(8,128)}, f32[8,128]{1,0:T(8,128)S(1)}, f32[2048,1024]{1,0:T(8,128)}) custom-call(bf16[512,1024]{1,0:T(8,128)(2,1)S(1)} %get-tuple-element.30.unit_ref, bf16[2048,512]{1,0:T(8,128)(2,1)} %weight_ref.1, f32[512,1024]{1,0:T(8,128)S(1)} %get-tuple-element.31.near_ref, ...), custom_call_target="tpu_custom_call", output_to_operand_aliasing={{2}: (3, {})} | custom-call | flops 2147483648 | bytes 12582912 | tf_op jit(solution)/shard_map/pallas_call | solution.py:421
  70.8 0.0 copy-done
  70.8 4.7 %all-to-all-done.2.got_ref = bf16[64,8,128]{2,1,0:T(8,128)(2,1)S(1)} async-done(((bf16[64,8,128]{2,1,0:T(8,128)(2,1)}), bf16[64,8,128]{2,1,0:T(8,128)(2,1)S(1)}, u32[]{:S(2)}, u32[]{:S(2)}) %all-to-all-start.2) | async-done | bytes 131104 | tf_op jit(solution)/shard_map/all_to_all | solution.py:43
  75.6 3.1 %shard_map.70 = (f32[2048,1024]{1,0:T(8,128)S(1)}, bf16[64,16,128]{2,1,0:T(8,128)(2,1)S(1)}, f32[8,128]{1,0:T(8,128)S(1)}) custom-call(bf16[64,8,128]{2,1,0:T(8,128)(2,1)S(1)} %all-to-all-done.2.got_ref, f32[2048,1024]{1,0:T(8,128)} %get-tuple-element.33.far_ref.kernel_ref, f32[512,1024]{1,0:T(8,128)S(1)} %get-tuple-element.31.near_ref, ...), custom_call_target="tpu_custom_call" | custom-call | flops 8388608 | bytes 8388608 | tf_op jit(solution)/shard_map/pallas_call | solution.py:431
  78.7 17.4 %all_to_all.27.got_ref = bf16[64,16,128]{2,1,0:T(8,128)(2,1)S(1)} all-to-all(bf16[64,16,128]{2,1,0:T(8,128)(2,1)S(1)} %get-tuple-element.35), channel_id=1, replica_groups=mesh['smp'=8,'proto'=64] {'proto'}, dimensions={0} | all-to-all | bytes 524288 | tf_op jit(solution)/shard_map/all_to_all | solution.py:43
  96.1 3.7 %shard_map.71 = (bf16[64,32,128]{2,1,0:T(8,128)(2,1)}, f32[8,128]{1,0:T(8,128)S(1)}, f32[8,128]{1,0:T(8,128)S(1)}) custom-call(bf16[64,16,128]{2,1,0:T(8,128)(2,1)S(1)} %all_to_all.27.got_ref, f32[2048,1024]{1,0:T(8,128)S(1)} %get-tuple-element.36.kernel_ref, f32[8,128]{1,0:T(8,128)S(1)} %get-tuple-element.37.kept_ref, ...), custom_call_target="tpu_custom_call" | custom-call | flops 536870912 | bytes 12582912 | tf_op jit(solution)/shard_map/pallas_call | solution.py:441
  99.8 6.0 %all-to-all-start.4 = ((bf16[64,32,128]{2,1,0:T(8,128)(2,1)}), bf16[64,32,128]{2,1,0:T(8,128)(2,1)S(1)}, u32[]{:S(2)}, u32[]{:S(2)}) async-start(bf16[64,32,128]{2,1,0:T(8,128)(2,1)} %get-tuple-element.40), calls=%async_computation.4 | async-start | bytes 1048576 | tf_op jit(solution)/shard_map/all_to_all | solution.py:43
  105.8 0.0 copy-start.1
  105.8 11.6 %shard_map.72 = (f32[64,2048]{1,0:T(8,128)S(1)}, bf16[1024,1024]{1,0:T(8,128)(2,1)S(1)}, bf16[1024,1024]{1,0:T(8,128)(2,1)}, bf16[64,1024]{1,0:T(8,128)(2,1)S(1)}) custom-call(f32[2048,1024]{1,0:T(8,128)} %get-tuple-element.33.far_ref.kernel_ref, bf16[2048,512]{1,0:T(8,128)(2,1)} %weight_ref.1, f32[8,128]{1,0:T(8,128)S(1)} %get-tuple-element.42.total_ref, ...), custom_call_target="tpu_custom_call" | custom-call | flops 2415919104 | bytes 15728640 | tf_op jit(solution)/shard_map/pallas_call | solution.py:453
  117.4 5.6 %all-to-all-done.4.got_ref = bf16[64,32,128]{2,1,0:T(8,128)(2,1)S(1)} async-done(((bf16[64,32,128]{2,1,0:T(8,128)(2,1)}), bf16[64,32,128]{2,1,0:T(8,128)(2,1)S(1)}, u32[]{:S(2)}, u32[]{:S(2)}) %all-to-all-start.4) | async-done | bytes 524320 | tf_op jit(solution)/shard_map/all_to_all | solution.py:43
  123.0 0.0 copy-done.1
  123.0 4.2 %shard_map.73 = (f32[8,128]{1,0:T(8,128)}, f32[1,128]{1,0:T(1,128)}, f32[64,2048]{1,0:T(8,128)}) custom-call(bf16[64,32,128]{2,1,0:T(8,128)(2,1)S(1)} %all-to-all-done.4.got_ref, bf16[8,128]{1,0:T(8,128)(2,1)S(1)} %bitcast.6, f32[8,128]{1,0:T(8,128)S(1)} %get-tuple-element.41.scale_ref, f32[8,128]{1,0:T(8,128)S(1)} %get-tuple-element.42.total_ref, ...), custom_call_target="tpu_custom_call" | custom-call | flops 268435456 | bytes 5242880 | tf_op jit(solution)/shard_map/pallas_call | solution.py:466
  (1 shorter events, 0.0 us)
Async XLA Ops:
  46.2 8.8 %collective-permute-start = (bf16[4,64,16,128]{3,2,1,0:T(8,128)(2,1)S(1)}, bf16[4,64,16,128]{3,2,1,0:T(8,128)(2,1)S(1)}, u32[]{:S(2)}, u32[]{:S(2)}) collective-permute-start(bf16[4,64,16,128]{3,2,1,0:T(8,128)(2,1)S(1)} %all_to_all.26.own_ref), channel_id=1, source_target_pairs={{0,1},{1,0},{2,3},{3,2},{4,5},{5,4},{6,7},{7,6},{8,9},{9,8},{10,11... | collective-permute-start | bytes 3145736 | tf_op jit(solution)/shard_map/ppermute | solution.py:400
  60.0 10.9 %copy-start = (bf16[512,1024]{1,0:T(8,128)(2,1)}, bf16[512,1024]{1,0:T(8,128)(2,1)S(1)}, u32[]{:S(2)}) copy-start(bf16[512,1024]{1,0:T(8,128)(2,1)S(1)} %get-tuple-element.30.unit_ref) | copy-start | bytes 3145732
  60.0 15.6 %all-to-all-start.2 = ((bf16[64,8,128]{2,1,0:T(8,128)(2,1)}), bf16[64,8,128]{2,1,0:T(8,128)(2,1)S(1)}, u32[]{:S(2)}, u32[]{:S(2)}) async-start(bf16[64,8,128]{2,1,0:T(8,128)(2,1)} %get-tuple-element.29), calls=%async_computation.2 | async-start | bytes 262144 | tf_op jit(solution)/shard_map/all_to_all | solution.py:43
  99.8 23.2 %all-to-all-start.4 = ((bf16[64,32,128]{2,1,0:T(8,128)(2,1)}), bf16[64,32,128]{2,1,0:T(8,128)(2,1)S(1)}, u32[]{:S(2)}, u32[]{:S(2)}) async-start(bf16[64,32,128]{2,1,0:T(8,128)(2,1)} %get-tuple-element.40), calls=%async_computation.4 | async-start | bytes 1048576 | tf_op jit(solution)/shard_map/all_to_all | solution.py:43
  105.8 17.1 %copy-start.1 = (bf16[128,8]{0,1:T(8,128)(2,1)S(1)}, bf16[128,8]{0,1:T(8,128)(2,1)}, u32[]{:S(2)}) copy-start(bf16[128,8]{0,1:T(8,128)(2,1)} %param.5) | copy-start | bytes 6148

commit v12 on v11

--- a/solution.py
+++ b/solution.py
@@ -191,10 +191,8 @@
         rows = pl.ds(pl.multiple_of(i * WIDE, WIDE), WIDE)
         return pltpu.make_async_copy(weight_far.at[rows], weight_ref.at[rows], weight_sem.at[i])
 
-    for i in range(ROWS // WIDE):
-        copy_in(i).start()
+    copy_in(0).start()
     near_copy = pltpu.make_async_copy(near_ref, kernel_out.at[pl.ds(FAR, ROWS - FAR)], near_sem)
-    near_copy.start()
     sum_ref[...] = jnp.zeros_like(sum_ref)
     lanes = pl.ds(pl.multiple_of(lax.axis_index("smp") * 128, 128), 128)
 
@@ -205,6 +203,16 @@
     @pl.loop(0, ROWS // WIDE)
     def _(i):
         copy_in(i).wait()
+
+        @pl.when(i == 0)
+        def _():
+            for later in range(1, ROWS // WIDE):
+                copy_in(later).start()
+
+        @pl.when(i == 1)
+        def _():
+            near_copy.start()
+
         rows = pl.ds(pl.multiple_of(i * WIDE, WIDE), WIDE)
         logits = jnp.dot(weight_ref[rows, :], unit_ref[...], preferred_element_type=f32) * (1.0 / STUDENT_TEMP)
         stage_ref[...] = logits

time: 128 us -> 128 us (level)
  no operation moved by 1% of the time
where the time goes in v12:
time: 128 us; the launch traced here: 127 us
  blocking collectives  62.1 us (49%)
  Pallas kernels  34.2 us (27%)
  starting transfers between devices  18.1 us (14%)
  waiting for transfers between devices  11 us (9%)
    all_to_all x2, blocking collectives, gathered(): lax.all_to_all(copies, BOTH, 0, 0, tiled=True, axis_index_groups=group)  44.7 us
    all_to_all x1, blocking collectives, sent_to_protos(): return lax.all_to_all(x, 'proto', 0, 0, tiled=True)  17.4 us
    all_to_all x2, starting transfers between devices, sent_to_protos(): return lax.all_to_all(x, 'proto', 0, 0, tiled=True)  11.6 us
    pallas_call x1, Pallas kernels, on_device(): streamed(weight_kernel, [shape((64, ROWS)), pltpu.VMEM((HALF * TILE, B),...  11.6 us
    all_to_all x2, waiting for transfers between devices, sent_to_protos(): return lax.all_to_all(x, 'proto', 0, 0, tiled=True)  10.3 us
    ppermute x1, starting transfers between devices, on_device(): other = lax.ppermute(second, 'proto', [(i, i ^ 1) for i in range(64)])  6.53 us
    pallas_call x1, Pallas kernels, on_device(): call(student_kernel, [pltpu.HBM((ROWS, 128), f32), shape((8, 128)), pltpu...  5.19 us
    pallas_call x1, Pallas kernels, on_device(): call(first_kernel, [pltpu.HBM((ROWS, B), f32), pltpu.VMEM((ROWS - FAR, B)...  4.93 us
  transfers between devices with their start and end apart: 3, of which 3 were waited for; matrix products, arithmetic and copies ran while one was open for 0% of the time, Pallas kernels for 14%

profile of v12, /device:TPU:1, one launch (start us, length us, event | category | flops | bytes accessed | tf_op | source)
XLA Modules:
  0.0 127.1 jit_solution(5636123724610001190)
XLA Ops:
  0.6 0.7 pad_maximum_fusion
  1.4 29.5 %all_to_all.25 = bf16[64,16,128]{2,1,0:T(8,128)(2,1)S(1)} all-to-all(bf16[64,16,128]{2,1,0:T(8,128)(2,1)S(1)} %broadcast_in_dim.4), channel_id=1, replica_groups={{0,2,4,6,8,10,12,14,16,18,20,22,24,26,28,30,32,34,36,38,40,42,44,46,48,..., dimensions={0} | all-to-all | bytes 524288 | tf_op jit(solution)/shard_map/all_to_all | solution.py:39
  30.9 0.1 broadcast_in_dim.5
  31.0 15.2 %all_to_all.26.own_ref = bf16[4,64,16,128]{3,2,1,0:T(8,128)(2,1)S(1)} all-to-all(bf16[4,64,16,128]{3,2,1,0:T(8,128)(2,1)S(1)} %broadcast_in_dim.5), channel_id=1, replica_groups={{0,128,256,384},{1,129,257,385},{2,130,258,386},{3,131,259,387},{4,132,..., dimensions={0} | all-to-all | bytes 2097152 | tf_op jit(solution)/shard_map/all_to_all | solution.py:39
  46.2 6.5 %collective-permute-start = (bf16[4,64,16,128]{3,2,1,0:T(8,128)(2,1)S(1)}, bf16[4,64,16,128]{3,2,1,0:T(8,128)(2,1)S(1)}, u32[]{:S(2)}, u32[]{:S(2)}) collective-permute-start(bf16[4,64,16,128]{3,2,1,0:T(8,128)(2,1)S(1)} %all_to_all.26.own_ref), channel_id=1, source_target_pairs={{0,1},{1,0},{2,3},{3,2},{4,5},{5,4},{6,7},{7,6},{8,9},{9,8},{10,11... | collective-permute-start | bytes 3145736 | tf_op jit(solution)/shard_map/ppermute | solution.py:408
  52.8 1.6 %shard_map.67.weight_ref = bf16[2048,512]{1,0:T(8,128)(2,1)S(1)} custom-call(bf16[2048,512]{1,0:T(8,128)(2,1)} %far_ref), custom_call_target="tpu_custom_call" | custom-call | bytes 4194304 | tf_op jit(solution)/shard_map/pallas_call | solution.py:414
  54.3 0.7 collective-permute-done.other_ref
  55.0 4.9 %shard_map.68 = (f32[2048,1024]{1,0:T(8,128)}, f32[512,1024]{1,0:T(8,128)S(1)}, bf16[512,1024]{1,0:T(8,128)(2,1)S(1)}, bf16[64,8,128]{2,1,0:T(8,128)(2,1)}, f32[...) custom-call(bf16[4,64,16,128]{3,2,1,0:T(8,128)(2,1)S(1)} %all_to_all.26.own_ref, ...), custom_call_target="tpu_custom_call" | custom-call | flops 2147483648 | bytes 12582912 | tf_op jit(solution)/shard_map/pallas_call | solution.py:417
  60.0 0.0 copy-start
  60.0 5.6 %all-to-all-start.2 = ((bf16[64,8,128]{2,1,0:T(8,128)(2,1)}), bf16[64,8,128]{2,1,0:T(8,128)(2,1)S(1)}, u32[]{:S(2)}, u32[]{:S(2)}) async-start(bf16[64,8,128]{2,1,0:T(8,128)(2,1)} %get-tuple-element.29), calls=%async_computation.2 | async-start | bytes 262144 | tf_op jit(solution)/shard_map/all_to_all | solution.py:43
  65.6 5.2 %shard_map.69 = (f32[2048,128]{1,0:T(8,128)}, f32[8,128]{1,0:T(8,128)S(1)}, f32[2048,1024]{1,0:T(8,128)}) custom-call(bf16[512,1024]{1,0:T(8,128)(2,1)S(1)} %get-tuple-element.30.unit_ref, bf16[2048,512]{1,0:T(8,128)(2,1)} %weight_ref.1, f32[512,1024]{1,0:T(8,128)S(1)} %get-tuple-element.31.near_ref, ...), custom_call_target="tpu_custom_call", output_to_operand_aliasing={{2}: (3, {})} | custom-call | flops 2147483648 | bytes 12582912 | tf_op jit(solution)/shard_map/pallas_call | solution.py:429
  70.8 0.0 copy-done
  70.8 4.8 %all-to-all-done.2.got_ref = bf16[64,8,128]{2,1,0:T(8,128)(2,1)S(1)} async-done(((bf16[64,8,128]{2,1,0:T(8,128)(2,1)}), bf16[64,8,128]{2,1,0:T(8,128)(2,1)S(1)}, u32[]{:S(2)}, u32[]{:S(2)}) %all-to-all-start.2) | async-done | bytes 131104 | tf_op jit(solution)/shard_map/all_to_all | solution.py:43
  75.6 3.1 %shard_map.70 = (f32[2048,1024]{1,0:T(8,128)S(1)}, bf16[64,16,128]{2,1,0:T(8,128)(2,1)S(1)}, f32[8,128]{1,0:T(8,128)S(1)}) custom-call(bf16[64,8,128]{2,1,0:T(8,128)(2,1)S(1)} %all-to-all-done.2.got_ref, f32[2048,1024]{1,0:T(8,128)} %get-tuple-element.33.far_ref.kernel_ref, f32[512,1024]{1,0:T(8,128)S(1)} %get-tuple-element.31.near_ref, ...), custom_call_target="tpu_custom_call" | custom-call | flops 8388608 | bytes 8388608 | tf_op jit(solution)/shard_map/pallas_call | solution.py:439
  78.7 17.4 %all_to_all.27.got_ref = bf16[64,16,128]{2,1,0:T(8,128)(2,1)S(1)} all-to-all(bf16[64,16,128]{2,1,0:T(8,128)(2,1)S(1)} %get-tuple-element.35), channel_id=1, replica_groups=mesh['smp'=8,'proto'=64] {'proto'}, dimensions={0} | all-to-all | bytes 524288 | tf_op jit(solution)/shard_map/all_to_all | solution.py:43
  96.0 3.7 %shard_map.71 = (bf16[64,32,128]{2,1,0:T(8,128)(2,1)}, f32[8,128]{1,0:T(8,128)S(1)}, f32[8,128]{1,0:T(8,128)S(1)}) custom-call(bf16[64,16,128]{2,1,0:T(8,128)(2,1)S(1)} %all_to_all.27.got_ref, f32[2048,1024]{1,0:T(8,128)S(1)} %get-tuple-element.36.kernel_ref, f32[8,128]{1,0:T(8,128)S(1)} %get-tuple-element.37.kept_ref, ...), custom_call_target="tpu_custom_call" | custom-call | flops 536870912 | bytes 12582912 | tf_op jit(solution)/shard_map/pallas_call | solution.py:449
  99.7 6.0 %all-to-all-start.4 = ((bf16[64,32,128]{2,1,0:T(8,128)(2,1)}), bf16[64,32,128]{2,1,0:T(8,128)(2,1)S(1)}, u32[]{:S(2)}, u32[]{:S(2)}) async-start(bf16[64,32,128]{2,1,0:T(8,128)(2,1)} %get-tuple-element.40), calls=%async_computation.4 | async-start | bytes 1048576 | tf_op jit(solution)/shard_map/all_to_all | solution.py:43
  105.8 0.0 copy-start.1
  105.8 11.6 %shard_map.72 = (f32[64,2048]{1,0:T(8,128)S(1)}, bf16[1024,1024]{1,0:T(8,128)(2,1)S(1)}, bf16[1024,1024]{1,0:T(8,128)(2,1)}, bf16[64,1024]{1,0:T(8,128)(2,1)S(1)}) custom-call(f32[2048,1024]{1,0:T(8,128)} %get-tuple-element.33.far_ref.kernel_ref, bf16[2048,512]{1,0:T(8,128)(2,1)} %weight_ref.1, f32[8,128]{1,0:T(8,128)S(1)} %get-tuple-element.42.total_ref, ...), custom_call_target="tpu_custom_call" | custom-call | flops 2415919104 | bytes 15728640 | tf_op jit(solution)/shard_map/pallas_call | solution.py:461
  117.4 5.6 %all-to-all-done.4.got_ref = bf16[64,32,128]{2,1,0:T(8,128)(2,1)S(1)} async-done(((bf16[64,32,128]{2,1,0:T(8,128)(2,1)}), bf16[64,32,128]{2,1,0:T(8,128)(2,1)S(1)}, u32[]{:S(2)}, u32[]{:S(2)}) %all-to-all-start.4) | async-done | bytes 524320 | tf_op jit(solution)/shard_map/all_to_all | solution.py:43
  122.9 0.0 copy-done.1
  122.9 4.2 %shard_map.73 = (f32[8,128]{1,0:T(8,128)}, f32[1,128]{1,0:T(1,128)}, f32[64,2048]{1,0:T(8,128)}) custom-call(bf16[64,32,128]{2,1,0:T(8,128)(2,1)S(1)} %all-to-all-done.4.got_ref, bf16[8,128]{1,0:T(8,128)(2,1)S(1)} %bitcast.6, f32[8,128]{1,0:T(8,128)S(1)} %get-tuple-element.41.scale_ref, f32[8,128]{1,0:T(8,128)S(1)} %get-tuple-element.42.total_ref, ...), custom_call_target="tpu_custom_call" | custom-call | flops 268435456 | bytes 5242880 | tf_op jit(solution)/shard_map/pallas_call | solution.py:474
  (1 shorter events, 0.0 us)
Async XLA Ops:
  46.2 8.8 %collective-permute-start = (bf16[4,64,16,128]{3,2,1,0:T(8,128)(2,1)S(1)}, bf16[4,64,16,128]{3,2,1,0:T(8,128)(2,1)S(1)}, u32[]{:S(2)}, u32[]{:S(2)}) collective-permute-start(bf16[4,64,16,128]{3,2,1,0:T(8,128)(2,1)S(1)} %all_to_all.26.own_ref), channel_id=1, source_target_pairs={{0,1},{1,0},{2,3},{3,2},{4,5},{5,4},{6,7},{7,6},{8,9},{9,8},{10,11... | collective-permute-start | bytes 3145736 | tf_op jit(solution)/shard_map/ppermute | solution.py:408
  60.0 10.8 %copy-start = (bf16[512,1024]{1,0:T(8,128)(2,1)}, bf16[512,1024]{1,0:T(8,128)(2,1)S(1)}, u32[]{:S(2)}) copy-start(bf16[512,1024]{1,0:T(8,128)(2,1)S(1)} %get-tuple-element.30.unit_ref) | copy-start | bytes 3145732
  60.0 15.6 %all-to-all-start.2 = ((bf16[64,8,128]{2,1,0:T(8,128)(2,1)}), bf16[64,8,128]{2,1,0:T(8,128)(2,1)S(1)}, u32[]{:S(2)}, u32[]{:S(2)}) async-start(bf16[64,8,128]{2,1,0:T(8,128)(2,1)} %get-tuple-element.29), calls=%async_computation.2 | async-start | bytes 262144 | tf_op jit(solution)/shard_map/all_to_all | solution.py:43
  99.7 23.2 %all-to-all-start.4 = ((bf16[64,32,128]{2,1,0:T(8,128)(2,1)}), bf16[64,32,128]{2,1,0:T(8,128)(2,1)S(1)}, u32[]{:S(2)}, u32[]{:S(2)}) async-start(bf16[64,32,128]{2,1,0:T(8,128)(2,1)} %get-tuple-element.40), calls=%async_computation.4 | async-start | bytes 1048576 | tf_op jit(solution)/shard_map/all_to_all | solution.py:43
  105.8 17.1 %copy-start.1 = (bf16[128,8]{0,1:T(8,128)(2,1)S(1)}, bf16[128,8]{0,1:T(8,128)(2,1)}, u32[]{:S(2)}) copy-start(bf16[128,8]{0,1:T(8,128)(2,1)} %param.5) | copy-start | bytes 6148
